TPU v7x, 32 devices: a whole 2x2x4 slice. The times are simulated.
32 devices in a mesh: row: 4 (over z), col: 8 (over y, x, core).
Axes of the slice: x: 2, y: 2, z: 4, core: 2. Of those that a mesh axis runs over, the one named last changes fastest.
Arguments:
- profiles: bfloat16 [50, 16384], P(None, ('col', 'row')), may hold values from -1.1953125 to 1.1953125
- cell_width: bfloat16 [16384], P(('col', 'row')), may hold values from 1 to 3
- basis: bfloat16 [64, 16384], P(None, ('col', 'row')), may hold values from -6 to 6
- block_lists: int32 [4, 8, 2, 128], P('row', 'col'), may hold values from 0 to 31, as said below
- block_counts: int32 [4, 8], P('row', 'col'), may hold values from 8 to 128, as said below
- landmarks: int32 [8], replicated, may hold values from 0 to 127, as said below
Outputs:
- row_scaling: float32 [16384], P('row')
- column_scaling: float32 [16384], P('col')
- ritz_basis: float32 [64, 16384], P(None, ('row', 'col'))
Inputs may be any that keep to these rules, and one draw needn't show every extreme that they name: `block_lists`: in each tile the first block_counts slots name distinct blocks, row block below 32 and column block below 16; every block of the tile whose global row block and global column block differ by at most one is among them; later slots also name blocks of the tile. `block_counts`: A tile whose column cells lie among its own row cells has exactly 128 live slots. `landmarks`: Distinct, increasing, one in each aligned group of 16 consecutive blocks.
All inputs are finite; a program needn't handle non-finite values.
Results may differ from a plain program's by a relative error of at most 0.0057.
Values may be sent and summed in bfloat16 or wider, within the bound.
No kernel may reach another device: no remote copies, remote signals or barrier semaphores. Data moves between devices by JAX's collectives and lax.ppermute only.
A program may use at most 64 MiB of HBM per device.

v0:
```python
import jax
import jax.numpy as jnp
from jax import lax
from jax.sharding import PartitionSpec as P

BLK = 128
PCS = 50
COLS = 64
SWEEPS = 3


affinity_scale = 0.001953125
highest = lax.Precision.HIGHEST


def block_kernel(row_slots, col_slots, live_mask, geometry):
    row_prof, row_norm, row_width, col_prof, col_norm, col_width = geometry
    left_prof = jnp.take(row_prof, row_slots, axis=1)
    right_prof = jnp.take(col_prof, col_slots, axis=1)
    inner_product = jnp.einsum(
        "pkb,pkd->kbd", left_prof, right_prof, preferred_element_type=jnp.float32
    )
    distance = (
        jnp.take(row_norm, row_slots, axis=0)[:, :, None]
        + jnp.take(col_norm, col_slots, axis=0)[:, None, :]
        - 2.0 * inner_product
    )
    width_pair = (
        jnp.take(row_width, row_slots, axis=0)[:, :, None]
        * jnp.take(col_width, col_slots, axis=0)[:, None, :]
    )
    return jnp.exp(-distance / width_pair) * (affinity_scale * live_mask)[:, None, None]


def affinity_sweep(update, initial, slot_lists, block_total, geometry):
    group_size = 8
    row_blocks = geometry[1].shape[0]
    col_blocks = geometry[4].shape[0]

    def advance(number, totals):
        first_slot = number * group_size
        row_slots = lax.dynamic_slice_in_dim(slot_lists[0], first_slot, group_size)
        col_slots = lax.dynamic_slice_in_dim(slot_lists[1], first_slot, group_size)
        live_mask = (first_slot + jnp.arange(group_size) < block_total).astype(jnp.float32)
        kernel = block_kernel(row_slots, col_slots, live_mask, geometry)
        row_onehot = (row_slots[:, None] == jnp.arange(row_blocks)[None, :]).astype(jnp.float32)
        col_onehot = (col_slots[:, None] == jnp.arange(col_blocks)[None, :]).astype(jnp.float32)
        return update(totals, kernel, row_slots, col_slots, row_onehot, col_onehot)

    trip_count = (block_total + group_size - 1) // group_size
    return lax.fori_loop(0, trip_count, advance, initial)


def with_rows(col_scaling):

    def update(totals, kernel, row_slots, col_slots, row_onehot, col_onehot):
        picked = jnp.take(col_scaling, col_slots, axis=0)
        partial_value = jnp.einsum("kbd,kd->kb", kernel, picked, precision=highest)
        return totals + jnp.einsum("kr,kb->rb", row_onehot, partial_value, precision=highest)

    return update


def with_cols(row_scaling):

    def update(totals, kernel, row_slots, col_slots, row_onehot, col_onehot):
        picked = jnp.take(row_scaling, row_slots, axis=0)
        partial_value = jnp.einsum("kbd,kb->kd", kernel, picked, precision=highest)
        return totals + jnp.einsum("kc,kd->cd", col_onehot, partial_value, precision=highest)

    return update


def with_subspace(scaled_basis):

    def update(totals, kernel, row_slots, col_slots, row_onehot, col_onehot):
        picked = jnp.take(scaled_basis, col_slots, axis=1)
        partial_value = jnp.einsum(
            "ckd,kbd->ckb", picked, kernel.astype(jnp.bfloat16), preferred_element_type=jnp.float32
        )
        return totals + jnp.einsum("kr,ckb->crb", row_onehot, partial_value, precision=highest)

    return update


def with_both(scaled_basis, col_scaling):
    row_update = with_rows(col_scaling)
    basis_update = with_subspace(scaled_basis)

    def update(totals, kernel, row_slots, col_slots, row_onehot, col_onehot):
        return (
            basis_update(totals[0], kernel, row_slots, col_slots, row_onehot, col_onehot),
            row_update(totals[1], kernel, row_slots, col_slots, row_onehot, col_onehot),
        )

    return update


def column_reciprocal(partial_value):
    return 1.0 / lax.psum(partial_value, "row")


def row_reciprocal(partial_value):
    return 1.0 / lax.psum(partial_value, "col")


def body(profiles, cell_width, basis, block_lists, block_counts, landmarks):
    col_prof, col_bw, col_basis = (
        lax.all_gather(profiles, "row", axis=1, tiled=True),
        lax.all_gather(cell_width, "row", axis=0, tiled=True),
        lax.all_gather(basis, "row", axis=1, tiled=True),
    )
    share_ratio = lax.axis_size("col") // lax.axis_size("row")
    cells_col = col_prof.shape[1]
    cells_row = cells_col * share_ratio
    every_prof, every_bw = (
        lax.all_gather(col_prof, "col", axis=1, tiled=True),
        lax.all_gather(col_bw, "col", axis=0, tiled=True),
    )
    first_cell = lax.axis_index("row") * cells_row
    row_prof = lax.dynamic_slice_in_dim(every_prof, first_cell, cells_row, 1)
    row_bw = lax.dynamic_slice_in_dim(every_bw, first_cell, cells_row, 0)
    row_blocks = cells_row // BLK
    col_blocks = cells_col // BLK
    geometry = (
        row_prof.reshape(PCS, row_blocks, BLK),
        jnp.sum(jnp.square(row_prof.astype(jnp.float32)), axis=0).reshape(row_blocks, BLK),
        row_bw.astype(jnp.float32).reshape(row_blocks, BLK),
        col_prof.reshape(PCS, col_blocks, BLK),
        jnp.sum(jnp.square(col_prof.astype(jnp.float32)), axis=0).reshape(col_blocks, BLK),
        col_bw.astype(jnp.float32).reshape(col_blocks, BLK),
    )
    slot_lists = block_lists[0, 0]
    block_total = block_counts[0, 0]
    row_scaling = jnp.ones((row_blocks, BLK), jnp.float32)
    col_scaling = jnp.ones((col_blocks, BLK), jnp.float32)
    for sweep_number in range(SWEEPS):
        col_part = affinity_sweep(
            with_cols(row_scaling),
            jnp.zeros((col_blocks, BLK), jnp.float32),
            slot_lists,
            block_total,
            geometry,
        )
        col_scaling = column_reciprocal(col_part.reshape(-1)).reshape(col_blocks, BLK)
        if sweep_number < SWEEPS - 1:
            row_part = affinity_sweep(
                with_rows(col_scaling),
                jnp.zeros((row_blocks, BLK), jnp.float32),
                slot_lists,
                block_total,
                geometry,
            )
            row_scaling = row_reciprocal(row_part.reshape(-1)).reshape(row_blocks, BLK)
    scaled_basis = (col_basis.astype(jnp.float32) * col_scaling.reshape(-1)[None, :]).astype(
        jnp.bfloat16
    )
    scaled_basis = scaled_basis.reshape(COLS, col_blocks, BLK)
    empty_sums = jnp.zeros((COLS, row_blocks, BLK), jnp.float32)
    mixed_sums, row_part = affinity_sweep(
        with_both(scaled_basis, col_scaling),
        (empty_sums, jnp.zeros((row_blocks, BLK), jnp.float32)),
        slot_lists,
        block_total,
        geometry,
    )
    share_cols, row_share = (
        lax.psum_scatter(
            mixed_sums.reshape(COLS, cells_row), "col", scatter_dimension=1, tiled=True
        ),
        lax.psum_scatter(row_part.reshape(-1), "col", scatter_dimension=0, tiled=True),
    )
    share_width = share_cols.shape[1]
    own_scaling = 1.0 / row_share
    row_flat = lax.all_gather(own_scaling, "col", axis=0, tiled=True)
    projected = share_cols * own_scaling[None, :]
    shard_number = lax.axis_index("row") * lax.axis_size("col") + lax.axis_index("col")
    cell_ids = shard_number * share_width + jnp.arange(share_width)
    block_ids = cell_ids // BLK
    cell_mask = jnp.any(block_ids[:, None] == landmarks[None, :], axis=1).astype(jnp.float32)
    masked = projected * cell_mask[None, :]
    gram_local = jnp.dot(masked, masked.T, precision=highest)
    gram_matrix = lax.psum(gram_local, ("row", "col")) / (landmarks.shape[0] * BLK)
    lower_factor = jnp.linalg.cholesky(gram_matrix)
    ritz_basis = jax.scipy.linalg.solve_triangular(lower_factor, projected, lower=True)
    return (row_flat, col_scaling.reshape(-1), ritz_basis)


def solution(mesh):
    placed = (
        P(None, ("col", "row")),
        P(("col", "row")),
        P(None, ("col", "row")),
        P("row", "col", None, None),
        P("row", "col"),
        P(),
    )
    return jax.shard_map(
        body,
        mesh=mesh,
        in_specs=placed,
        out_specs=(P("row"), P("col"), P(None, ("row", "col"))),
        check_vma=False,
    )
```

profile of v0, /device:TPU:0, one launch (start us, length us, event | category | flops | bytes accessed | tf_op | source)
XLA Modules:
  0.0 902.4 jit_solution(13601583082482498278)
XLA Ops:
  7.2 17.3 %all_gather.18 = bf16[50,2048]{1,0:T(8,128)(2,1)} all-gather(bf16[50,512]{1,0:T(8,128)(2,1)} %param.26), channel_id=1, replica_groups=mesh['row'=4,'col'=8] {'row'}, dimensions={1}, use_global_device_ids=true | all-gather | bytes 256000 | tf_op jit(solution)/shard_map/all_gather | solution.py:109
  26.0 11.9 %all-gather = bf16[4,1,512]{2,1,0:T(2,128)(2,1)S(1)} all-gather(bf16[1,1,512]{2,1,0:T(2,128)(2,1)S(1)} %reshape.653), channel_id=1, replica_groups=mesh['row'=4,'col'=8] {'row'}, dimensions={0}, use_global_device_ids=true | all-gather | bytes 5120 | tf_op jit(solution)/shard_map/all_gather | solution.py:110
  37.9 1.0 copy.78
  39.0 9.1 %all_gather.21 = bf16[16384]{0:T(1024)(128)(2,1)S(1)} all-gather(bf16[2048]{0:T(1024)(128)(2,1)S(1)} %bitcast.313), channel_id=1, replica_groups=mesh['row'=4,'col'=8] {'col'}, dimensions={0}, use_global_device_ids=true | all-gather | bytes 36864 | tf_op jit(solution)/shard_map/all_gather | solution.py:118
  48.1 14.0 %all_gather.22 = bf16[64,2048]{1,0:T(8,128)(2,1)S(1)} all-gather(bf16[64,512]{1,0:T(8,128)(2,1)S(1)} %copy-done.2), channel_id=1, replica_groups=mesh['row'=4,'col'=8] {'row'}, dimensions={1}, use_global_device_ids=true | all-gather | bytes 327680 | tf_op jit(solution)/shard_map/all_gather | solution.py:111
  62.2 1.2 multiply_reduce_fusion
  63.7 103.9 %while.62 = (s32[]{:T(128)}, f32[16,128]{1,0:T(8,128)S(1)}, s32[]{:T(128)}, s32[2,128]{1,0:T(2,128)S(1)}, f32[32,128]{1,0:T(8,128)S(1)}, /*index=5*/f32[16,128]{...) while((s32[]{:T(128)}, f32[16,128]{1,0:T(8,128)S(1)}, ...), condition=%wide.region_3.8_spmd, body=%wide.region_2.7_spmd.sunk | while | flops 15906070 | bytes 1817411 | solution.py:51
  167.6 8.5 psum.42
  176.2 110.1 %while.63 = (s32[]{:T(128)}, f32[32,128]{1,0:T(8,128)S(1)}, s32[]{:T(128)}, s32[2,128]{1,0:T(2,128)S(1)}, f32[32,128]{1,0:T(8,128)S(1)}, /*index=5*/f32[16,128]{...) while((s32[]{:T(128)}, f32[32,128]{1,0:T(8,128)S(1)}, ...), condition=%wide.region_6.11_spmd, body=%wide.region_5.0_spmd.sunk | while | flops 16104854 | bytes 1817407 | solution.py:51
  286.3 22.3 %psum.43 = f32[4096]{0:T(1024)S(1)} all-reduce(f32[4096]{0:T(1024)S(1)} %bitcast.311), channel_id=1, replica_groups=mesh['row'=4,'col'=8] {'col'}, use_global_device_ids=true, to_apply=%region_7.12 | all-reduce | flops 4096 | bytes 32768 | tf_op jit(solution)/shard_map/psum | solution.py:104
  308.7 103.8 %while.64 = (s32[]{:T(128)}, f32[16,128]{1,0:T(8,128)S(1)}, s32[]{:T(128)}, s32[2,128]{1,0:T(2,128)S(1)}, f32[32,128]{1,0:T(8,128)S(1)}, /*index=5*/f32[16,128]{...) while((s32[]{:T(128)}, f32[16,128]{1,0:T(8,128)S(1)}, ...), condition=%wide.region_9.14_spmd, body=%wide.region_8.13_spmd.sunk | while | flops 15906070 | bytes 1801023 | solution.py:51
  412.4 8.5 psum.44
  421.0 110.1 %while.65 = (s32[]{:T(128)}, f32[32,128]{1,0:T(8,128)S(1)}, s32[]{:T(128)}, s32[2,128]{1,0:T(2,128)S(1)}, f32[32,128]{1,0:T(8,128)S(1)}, /*index=5*/f32[16,128]{...) while((s32[]{:T(128)}, f32[32,128]{1,0:T(8,128)S(1)}, ...), condition=%wide.region_12.17_spmd, body=%wide.region_11.16_spmd.sunk | while | flops 16104854 | bytes 1817407 | solution.py:51
  531.1 22.3 %psum.45 = f32[4096]{0:T(1024)S(1)} all-reduce(f32[4096]{0:T(1024)S(1)} %bitcast.312), channel_id=1, replica_groups=mesh['row'=4,'col'=8] {'col'}, use_global_device_ids=true, to_apply=%region_13.18 | all-reduce | flops 4096 | bytes 32768 | tf_op jit(solution)/shard_map/psum | solution.py:104
  553.4 103.8 %while.66 = (s32[]{:T(128)}, f32[16,128]{1,0:T(8,128)S(1)}, s32[]{:T(128)}, s32[2,128]{1,0:T(2,128)S(1)}, f32[32,128]{1,0:T(8,128)S(1)}, /*index=5*/f32[16,128]{...) while((s32[]{:T(128)}, f32[16,128]{1,0:T(8,128)S(1)}, ...), condition=%wide.region_15.20_spmd, body=%wide.region_14.19_spmd.sunk | while | flops 15906070 | bytes 1801023 | solution.py:51
  657.2 8.5 psum.46
  666.3 140.1 %while.67 = (s32[]{:T(128)}, f32[64,32,128]{2,1,0:T(8,128)S(1)}, f32[32,128]{1,0:T(8,128)S(1)}, s32[]{:T(128)}, s32[2,128]{1,0:T(2,128)S(1)}, /*index=5*/f32[32,...) while((s32[]{:T(128)}, f32[64,32,128]{2,1,0:T(8,128)S(1)}, ...), condition=%wide.region_18.23_spmd, body=%wide.region_17.22_spmd.sunk | while | flops 58507948 | bytes 5360635 | solution.py:51
  672.7 0.9 fusion.250
  681.4 0.9 fusion.250
  690.2 0.9 fusion.250
  698.9 0.9 fusion.250
  707.7 0.9 fusion.250
  751.5 0.9 fusion.250
  786.5 0.9 fusion.250
  806.5 1.6 copy.85
  809.5 22.4 %all-reduce = f32[4096]{0:T(1024)S(1)} all-reduce(f32[4096]{0:T(1024)S(1)} %bitcast.310), channel_id=2, replica_groups=mesh['row'=4,'col'=8] {'col'}, use_global_device_ids=true, to_apply=%region_19.24.clone | all-reduce | flops 4096 | bytes 32768
  831.9 7.6 all-gather.1
  840.1 1.3 fusion.97
  841.4 39.5 %psum.47 = f32[64,64]{0,1:T(8,128)S(1)} all-reduce(f32[64,64]{0,1:T(8,128)S(1)} %fusion.97), channel_id=1, replica_groups=mesh['row'=4,'col'=8] {'row','col'}, use_global_device_ids=true, to_apply=%region_22.27 | all-reduce | flops 4096 | bytes 32768 | tf_op jit(solution)/shard_map/psum | solution.py:183
  881.0 5.8 cholesky.16
  888.2 4.9 custom-call.7
  893.1 1.9 fusion.99
  (1872 shorter events, 661.8 us)
Async XLA Ops:
  7.2 40.9 %copy-start.2 = (bf16[64,512]{1,0:T(8,128)(2,1)S(1)}, bf16[64,512]{1,0:T(8,128)(2,1)}, u32[]{:S(2)}) copy-start(bf16[64,512]{1,0:T(8,128)(2,1)} %param.28) | copy-start | bytes 196612
  7.2 55.1 %all-gather.4.cloned.1.call-start = ((), (), s32[]{:S(2)}) async-start(), calls=%async_computation.1 | async-start | bytes 2064384 | tf_op jit(solution)/shard_map/all_gather | solution.py:117
  24.5 37.6 %copy-start = (bf16[50,2048]{1,0:T(8,128)(2,1)S(1)}, bf16[50,2048]{1,0:T(8,128)(2,1)}, u32[]{:S(2)}) copy-start(bf16[50,2048]{1,0:T(8,128)(2,1)} %all_gather.18) | copy-start | bytes 614404
  24.6 815.6 %reduce-scatter.2.cloned.1.call-start = ((), (), s32[]{:S(2)}) async-start(), calls=%async_computation.2 | async-start | bytes 1179648 | tf_op jit(solution)/shard_map/reduce_scatter | solution.py:168
  62.2 1.5 copy-start.1
  665.7 0.6 copy-start.3
  806.4 1.7 copy-start.4
  806.5 1.8 copy-start.5
Sparse Core Ops, SparseCore 0:
  24.7 27.0 all-gather.3
  808.2 31.9 reduce-scatter.1
where the time goes:
time: 904 us; the launch traced here: 902 us
  local copies, waits for them, and re-layouts  391 us (43%)
  blocking collectives  192 us (21%)
  matrix products  192 us (21%)
  other arithmetic  102 us (11%)
  between operations  15.7 us (2%)
    dot_general x96, matrix products, block_kernel(): jnp.einsum('pkb,pkd->kbd', left_prof, right_prof, preferred_element_type=...  73.2 us
    mul x96, other arithmetic, block_kernel(): affinity_scale * live_mask  63.1 us
    gather x96, local copies, waits for them, and re-layouts, block_kernel(): right_prof = jnp.take(col_prof, col_slots, axis=1)  54.9 us
    gather x96, local copies, waits for them, and re-layouts, block_kernel(): left_prof = jnp.take(row_prof, row_slots, axis=1)  54.9 us
    gather x96, local copies, waits for them, and re-layouts, block_kernel(): jnp.take(row_width, row_slots, axis=0)[:, :, None]  53.4 us
    gather x96, local copies, waits for them, and re-layouts, block_kernel(): jnp.take(col_width, col_slots, axis=0)[:, None, :]  53.4 us
    gather x96, local copies, waits for them, and re-layouts, block_kernel(): jnp.take(col_norm, col_slots, axis=0)[:, None, :]  53.3 us
    gather x96, local copies, waits for them, and re-layouts, block_kernel(): jnp.take(row_norm, row_slots, axis=0)[:, :, None]  53.3 us
  transfers between devices with their start and end apart: 2, of which 1 were waited for; matrix products, arithmetic and copies ran while one was open for 0% of the time, Pallas kernels for 0%

commit v1 on v0

v1 whole, which is shorter than its diff:
```python
import functools

import jax
import jax.numpy as jnp
from jax import lax
from jax.experimental import pallas as pl
from jax.experimental.pallas import tpu as pltpu
from jax.sharding import PartitionSpec as P

BLK = 128
SWEEPS = 3
GROUP = 8
FEAT = 64
PIECES = 16
SCALE = 512.0
LOG2E = 1.4426950408889634
F32 = jnp.float32
BF16 = jnp.bfloat16
MIB = 1 << 20

VMEM_SPEC = pl.BlockSpec(memory_space=pltpu.VMEM)
SMEM_SPEC = pl.BlockSpec(memory_space=pltpu.SMEM)


def split3(x):
    high = x.astype(BF16).astype(F32)
    mid = (x - high).astype(BF16).astype(F32)
    low = (x - high - mid).astype(BF16).astype(F32)
    return high, mid, low


def tree_sum(values):
    values = list(values)
    while len(values) > 1:
        values = [a + b for a, b in zip(values[::2], values[1::2])]
    return values[0]


def call(kernel, outs, ins, scratch=(), limit=24, flops=1 << 24):
    args, specs = [], []
    for kind, array in ins:
        if kind == "smem":
            specs.append(SMEM_SPEC)
        else:
            specs.append(VMEM_SPEC)
            if kind == "keep":
                array = pltpu.with_memory_space_constraint(array, pltpu.VMEM)
        args.append(array)
    return pl.pallas_call(
        kernel,
        out_shape=tuple(outs),
        in_specs=specs,
        out_specs=tuple(VMEM_SPEC for _ in outs),
        scratch_shapes=list(scratch),
        compiler_params=pltpu.CompilerParams(vmem_limit_bytes=limit * MIB),
        cost_estimate=pl.CostEstimate(flops=flops, bytes_accessed=1 << 20, transcendentals=0),
    )(*args)


def pack_kernel(prof_ref, width_ref, out_ref, work):
    pcs = prof_ref.shape[0]
    prof = prof_ref[...].astype(F32)
    norm = jnp.sum(prof * prof, axis=0, keepdims=True)
    high, mid, low = split3(norm)
    work[...] = jnp.zeros_like(work)
    work[0:pcs, :] = prof
    work[pcs : pcs + 1, :] = high
    work[pcs + 1 : pcs + 2, :] = mid
    work[pcs + 2 : pcs + 3, :] = low
    work[pcs + 3 : pcs + 6, :] = jnp.ones((3, prof.shape[1]), F32)
    work[pcs + 6 : pcs + 7, :] = width_ref[...].astype(F32)
    out_ref[...] = work[...].astype(BF16)


def slot_loop(meta, step, count, group=GROUP):
    def advance(number, carry):
        for i in range(group):
            step(number * group + i)
        return carry

    lax.fori_loop(0, (count + group - 1) // group, advance, 0)


def build_kernel(pcs, n_row, n_col, *refs):
    meta = refs[0]
    col_in = refs[1 : 1 + n_row]
    row_in = refs[1 + n_row : 1 + n_row + n_col]
    tile, part, row_prof, row_inv, col_prof, col_inv, acc = refs[1 + n_row + n_col :]
    per = col_in[0].shape[1] // BLK
    col_blocks = n_row * per
    total, me_row, me_col = meta[2, 0], meta[2, 2], meta[2, 3]
    for k in range(n_col):
        piece = lax.bitwise_xor(me_col, k)
        for j in range(per):
            block = row_in[k][:, j * BLK : (j + 1) * BLK]
            row_prof[piece * per + j] = block
            width = block.astype(F32)[pcs + 6 : pcs + 7, :]
            row_inv[piece * per + j] = jnp.broadcast_to(1.0 / width, (8, BLK))
    rows = lax.broadcasted_iota(jnp.int32, (FEAT, BLK), 0)
    for k in range(n_row):
        piece = lax.bitwise_xor(me_row, k)
        for j in range(per):
            block = col_in[k][:, j * BLK : (j + 1) * BLK].astype(F32)
            left = jnp.where(rows < pcs, -2.0 * block, 0.0)
            left = jnp.where((rows >= pcs) & (rows < pcs + 3), 1.0, left)
            left = jnp.where(
                (rows >= pcs + 3) & (rows < pcs + 6), pltpu.roll(block, 3, 0), left
            )
            left = jnp.where(rows == pcs + 7, pltpu.roll(block, 1, 0), left)
            left = left.T
            col_prof[piece * per + j] = left.astype(BF16)
            col_inv[piece * per + j] = jnp.broadcast_to(
                -LOG2E / left[:, pcs + 7 : pcs + 8], (BLK, BLK)
            )
    acc[...] = jnp.zeros_like(acc)
    lead = (lax.broadcasted_iota(jnp.int32, (PIECES, BLK), 0) == 0).astype(F32).astype(BF16)

    def step(s):
        rb, cb = meta[0, s], meta[1, s]
        target = jnp.where(s < total, cb, col_blocks)
        distance = jnp.dot(col_prof[cb], row_prof[rb], preferred_element_type=F32)
        block = jnp.exp2(distance * col_inv[cb] * row_inv[rb][0:1, :]).astype(BF16)
        tile[s] = block
        sums = lax.dot_general(
            lead, block, (((1,), (1,)), ((), ())), preferred_element_type=F32
        )
        acc[target] += sums[0:8]

    slot_loop(meta, step, total)
    part[...] = jnp.sum(acc[0:col_blocks], axis=1)


def fill_pieces(target, first, scaling):
    high, mid, low = split3(scaling)
    rows = lax.broadcasted_iota(jnp.int32, (PIECES, BLK), 0)
    shape = (PIECES, BLK)
    for b in range(scaling.shape[0]):
        value = jnp.where(
            rows == 0,
            jnp.broadcast_to(high[b : b + 1], shape),
            jnp.where(
                rows == 1,
                jnp.broadcast_to(mid[b : b + 1], shape),
                jnp.where(rows == 2, jnp.broadcast_to(low[b : b + 1], shape), 0.0),
            ),
        )
        target[b, first : first + PIECES, :] = value.astype(BF16)


def pass_kernel(over_rows, n_parts, *refs):
    meta, tile = refs[0], refs[1]
    parts = refs[2 : 2 + n_parts]
    out, left, acc = refs[2 + n_parts :]
    total = meta[2, 0]
    blocks = out.shape[0]
    scaling = SCALE / tree_sum([p[...] for p in parts])
    fill_pieces(left, 0, scaling)
    acc[...] = jnp.zeros_like(acc)
    dims = (((1,), (0,)), ((), ())) if over_rows else (((1,), (1,)), ((), ()))

    def step(s):
        rb, cb = meta[0, s], meta[1, s]
        source, target = (cb, rb) if over_rows else (rb, cb)
        target = jnp.where(s < total, target, blocks)
        sums = lax.dot_general(left[source], tile[s], dims, preferred_element_type=F32)
        acc[target] += sums[0:8]

    slot_loop(meta, step, total)
    out[...] = jnp.sum(acc[0:blocks], axis=1)


def last_row_kernel(n_row, n_land, *refs):
    meta, tile = refs[0], refs[1]
    parts = refs[2 : 2 + n_row]
    bases = refs[2 + n_row : 2 + 2 * n_row]
    out, land, scaling_out, scaled, left, acc, land_acc = refs[2 + 2 * n_row :]
    total, n_slots, me_row = meta[2, 0], meta[2, 1], meta[2, 2]
    blocks = out.shape[0]
    per = bases[0].shape[1] // BLK
    scaling_out[...] = SCALE / tree_sum([p[...] for p in parts])
    scaling = scaling_out[...]
    fill_pieces(left, 0, scaling)
    for k in range(n_row):
        piece = lax.bitwise_xor(me_row, k)
        for j in range(per):
            block = bases[k][:, j * BLK : (j + 1) * BLK].astype(F32)
            scaled[piece * per + j] = (
                block * scaling_out[pl.ds(piece * per + j, 1), :]
            ).astype(BF16)
    acc[...] = jnp.zeros_like(acc)
    land_acc[...] = jnp.zeros_like(land_acc)

    def land_step(s):
        rb, cb = meta[0, s], meta[1, s]
        which = 0
        for i in range(1, n_land):
            which = jnp.where(rb == meta[2, 4 + i], i, which)
        which = jnp.where(s < n_slots, which, n_land)
        land_acc[which] += jnp.dot(scaled[cb], tile[s], preferred_element_type=F32)

    slot_loop(meta, land_step, n_slots, 4)
    land[...] = land_acc[0:n_land].astype(land.dtype)

    def step(s):
        rb, cb = meta[0, s], meta[1, s]
        target = jnp.where(s < total, rb, blocks)
        sums = jnp.dot(left[cb], tile[s], preferred_element_type=F32)
        acc[target] += sums[0:8]

    slot_loop(meta, step, total)
    out[...] = jnp.sum(acc[0:blocks], axis=1)


def mixed_kernel(n_col, *refs):
    meta, tile, scaled = refs[:3]
    outs = refs[3 : 3 + n_col]
    acc = refs[3 + n_col]
    per = outs[0].shape[0]
    blocks = n_col * per
    total, me_col = meta[2, 0], meta[2, 3]
    acc[...] = jnp.zeros_like(acc)

    def step(s):
        rb, cb = meta[0, s], meta[1, s]
        target = jnp.where(s < total, rb, blocks)
        acc[target] += jnp.dot(scaled[cb], tile[s], preferred_element_type=F32)

    slot_loop(meta, step, total)
    for k in range(n_col):
        piece = lax.bitwise_xor(me_col, k)
        outs[k][...] = acc[pl.ds(piece * per, per)].astype(outs[k].dtype)


def gram_kernel(n_col, n_land, *refs):
    meta = refs[0]
    parts = refs[1 : 1 + n_col]
    lands = refs[1 + n_col : 1 + 2 * n_col]
    gram, scaling_out, inverse = refs[1 + 2 * n_col :]
    inverse[...] = 1.0 / tree_sum([p[...] for p in parts])
    scaling_out[...] = SCALE * inverse[...]
    total = None
    for i in range(n_land):
        summed = tree_sum([m[i].astype(F32) for m in lands])
        projected = summed * inverse[pl.ds(meta[2, 4 + i], 1), :]
        product = lax.dot_general(
            projected,
            projected,
            (((1,), (1,)), ((), ())),
            precision=lax.Precision.HIGHEST,
            preferred_element_type=F32,
        )
        total = product if total is None else total + product
    gram[...] = total


def ritz_kernel(n_row, n_col, cells, *refs):
    meta = refs[0]
    grams = refs[1 : 1 + n_row]
    shares = refs[1 + n_row : 1 + n_row + n_col]
    scaling, out = refs[1 + n_row + n_col :]
    per, cols = shares[0].shape[0], shares[0].shape[1]
    me_col = meta[2, 3]
    gram = tree_sum([g[...] for g in grams]) * (1.0 / cells)
    rows = lax.broadcasted_iota(jnp.int32, (cols, 2 * cols), 0)
    lanes = lax.broadcasted_iota(jnp.int32, (cols, 2 * cols), 1)
    unit = (lax.broadcasted_iota(jnp.int32, (cols, cols), 0)
            == lax.broadcasted_iota(jnp.int32, (cols, cols), 1)).astype(F32)
    work = jnp.concatenate([gram, unit], axis=1)
    for j in range(cols):
        root = lax.rsqrt(work[j : j + 1, j : j + 1])
        upper = work[j : j + 1, :] * root
        lower = work[:, j : j + 1] * root
        work = jnp.where(
            rows > j, work - lower * upper, jnp.where(rows == j, upper, work)
        )
    inverse = work[:, cols:]
    for j in range(per):
        summed = tree_sum([m[j].astype(F32) for m in shares])
        projected = summed * (scaling[pl.ds(me_col * per + j, 1), :] * (1.0 / SCALE))
        out[:, j * BLK : (j + 1) * BLK] = jnp.dot(
            inverse, projected, precision=lax.Precision.HIGHEST, preferred_element_type=F32
        )


def exchange(x, axis):
    n = lax.axis_size(axis)
    return [x] + [
        lax.ppermute(x, axis, [(i, i ^ k) for i in range(n)]) for k in range(1, n)
    ]


def vec(*arrays):
    return [("vmem", a) for a in arrays]


def slot_table(block_lists, block_counts, landmarks, row_blocks, n_land):
    slots = block_lists.shape[-1]
    total = block_counts[0, 0]
    me_row, me_col = lax.axis_index("row"), lax.axis_index("col")
    own = lax.dynamic_slice_in_dim(landmarks, me_row * n_land, n_land) - me_row * row_blocks
    rows, cols = block_lists[0, 0, 0], block_lists[0, 0, 1]
    index = jnp.arange(slots, dtype=jnp.int32)
    live = index < total
    marked = live & jnp.any(rows[:, None] == own[None, :], axis=1)
    key = jnp.where(marked, 0, jnp.where(live, 1, 2)) * slots + index
    place = jnp.sum((key[None, :] < key[:, None]).astype(jnp.int32), axis=1)
    chosen = (place[:, None] == index[None, :]).astype(jnp.int32)
    lists = jnp.sum(chosen[None] * jnp.stack([rows, cols])[:, :, None], axis=1)
    scalars = jnp.concatenate(
        [
            jnp.stack([total, jnp.sum(marked.astype(jnp.int32)), me_row, me_col]),
            own,
            jnp.zeros((slots - 4 - n_land,), jnp.int32),
        ]
    )
    return jnp.concatenate([lists, scalars[None]], axis=0)


def body(profiles, cell_width, basis, block_lists, block_counts, landmarks):
    n_row, n_col = lax.axis_size("row"), lax.axis_size("col")
    pcs, share = profiles.shape
    cols = basis.shape[0]
    per = share // BLK
    row_blocks, col_blocks = n_col * per, n_row * per
    slots = block_lists.shape[-1]
    n_land = landmarks.shape[0] // n_row

    def shape(*dims, dtype=F32):
        return jax.ShapeDtypeStruct(dims, dtype)

    (packed,) = call(
        pack_kernel,
        [shape(FEAT, share, dtype=BF16)],
        vec(profiles, cell_width.reshape(1, share)),
        [pltpu.VMEM((FEAT, share), F32)],
    )
    spread = lax.ppermute(
        packed,
        ("row", "col"),
        [((q % n_row) * n_col + q // n_row, q) for q in range(n_row * n_col)],
    )
    col_packs = exchange(packed, "row")
    row_packs = exchange(spread, "col")
    bases = exchange(basis, "row")
    meta = slot_table(block_lists, block_counts, landmarks, row_blocks, n_land)
    tile, part = call(
        functools.partial(build_kernel, pcs, n_row, n_col),
        [pltpu.VMEM((slots, BLK, BLK), BF16), shape(col_blocks, BLK)],
        [("smem", meta)] + vec(*col_packs, *row_packs),
        [
            pltpu.VMEM((row_blocks, FEAT, BLK), BF16),
            pltpu.VMEM((row_blocks, 8, BLK), F32),
            pltpu.VMEM((col_blocks, BLK, FEAT), BF16),
            pltpu.VMEM((col_blocks, BLK, BLK), F32),
            pltpu.VMEM((col_blocks + 1, 8, BLK), F32),
        ],
    )
    for _ in range(SWEEPS - 1):
        parts = exchange(part, "row")
        (part,) = call(
            functools.partial(pass_kernel, True, n_row),
            [shape(row_blocks, BLK)],
            [("smem", meta), ("keep", tile)] + vec(*parts),
            [
                pltpu.VMEM((col_blocks, PIECES, BLK), BF16),
                pltpu.VMEM((row_blocks + 1, 8, BLK), F32),
            ],
        )
        parts = exchange(part, "col")
        (part,) = call(
            functools.partial(pass_kernel, False, n_col),
            [shape(col_blocks, BLK)],
            [("smem", meta), ("keep", tile)] + vec(*parts),
            [
                pltpu.VMEM((row_blocks, PIECES, BLK), BF16),
                pltpu.VMEM((col_blocks + 1, 8, BLK), F32),
            ],
        )
    parts = exchange(part, "row")
    row_part, land, col_scaling, scaled = call(
        functools.partial(last_row_kernel, n_row, n_land),
        [
            shape(row_blocks, BLK),
            shape(n_land, cols, BLK, dtype=BF16),
            shape(col_blocks, BLK),
            shape(col_blocks, cols, BLK, dtype=BF16),
        ],
        [("smem", meta), ("keep", tile)] + vec(*parts, *bases),
        [
            pltpu.VMEM((col_blocks, PIECES, BLK), BF16),
            pltpu.VMEM((row_blocks + 1, 8, BLK), F32),
            pltpu.VMEM((n_land + 1, cols, BLK), F32),
        ],
    )
    row_parts = exchange(row_part, "col")
    lands = exchange(land, "col")
    mixed = call(
        functools.partial(mixed_kernel, n_col),
        [shape(per, cols, BLK, dtype=BF16)] * n_col,
        [("smem", meta), ("keep", tile)] + vec(scaled),
        [pltpu.VMEM((row_blocks + 1, cols, BLK), F32)],
    )
    shares = [mixed[0]] + [
        lax.ppermute(mixed[k], "col", [(i, i ^ k) for i in range(n_col)])
        for k in range(1, n_col)
    ]
    gram, row_scaling = call(
        functools.partial(gram_kernel, n_col, n_land),
        [shape(cols, cols), shape(row_blocks, BLK)],
        [("smem", meta)] + vec(*row_parts, *lands),
        [pltpu.VMEM((row_blocks, BLK), F32)],
    )
    grams = exchange(gram, "row")
    (ritz,) = call(
        functools.partial(ritz_kernel, n_row, n_col, landmarks.shape[0] * BLK),
        [shape(cols, share)],
        [("smem", meta)] + vec(*grams, *shares, row_scaling),
    )
    return row_scaling.reshape(-1), col_scaling.reshape(-1), ritz


def solution(mesh):
    placed = (
        P(None, ("col", "row")),
        P(("col", "row")),
        P(None, ("col", "row")),
        P("row", "col", None, None),
        P("row", "col"),
        P(),
    )
    return jax.shard_map(
        body,
        mesh=mesh,
        in_specs=placed,
        out_specs=(P("row"), P("col"), P(None, ("row", "col"))),
        check_vma=False,
    )
```

time: 904 us -> 153 us (0.17)
  local copies, waits for them, and re-layouts: 391 us -> 3.71 us
  matrix products: 192 us -> 0 us
  blocking collectives: 192 us -> 0 us
  other arithmetic: 102 us -> 1.85 us
  starting transfers between devices: 0.08 us -> 64.8 us
  Pallas kernels: 0 us -> 48.2 us
  waiting for transfers between devices: 0.66 us -> 32.7 us
  between operations: 15.7 us -> 1.57 us
    gather x688 -> x0, local copies, waits for them, and re-layouts: 386 us -> none  [the longest x96 54.9 us: block_kernel(): right_prof = jnp.take(col_prof, col_slots, axis=1)]
    dot_general x321 -> x0, matrix products: 190 us -> none  [the longest x96 73.2 us: block_kernel(): jnp.einsum('pkb,pkd->kbd', left_prof, right_prof, preferred_element_type=...]
    psum x6 -> x0, blocking collectives: 110 us -> none  [the longest x2 44.6 us: row_reciprocal(): return 1.0 / lax.psum(partial_value, 'col')]
    ppermute x0 -> x61, starting transfers between devices: none -> 64.8 us  [the longest x53 59.4 us: exchange(): lax.ppermute(x, axis, [(i, i ^ k) for i in range(n)])]
    mul x96 -> x0, other arithmetic: 63.1 us -> none  [block_kernel(): affinity_scale * live_mask]
    all_gather x5 -> x0, blocking collectives: 59.9 us -> none  [the longest x1 17.3 us: body(): lax.all_gather(profiles, 'row', axis=1, tiled=True)]
    pallas_call x0 -> x10, Pallas kernels: none -> 48.2 us  [call(): pl.pallas_call(kernel, out_shape=tuple(outs), in_specs=specs, out_specs=t...]
    ppermute x0 -> x61, waiting for transfers between devices: none -> 32.7 us  [the longest x53 29.3 us: exchange(): lax.ppermute(x, axis, [(i, i ^ k) for i in range(n)])]
  transfers between devices with their start and end apart: 2 -> 61, of which waited for: 1 -> 24; matrix products, arithmetic and copies ran while one was open for 0% -> 2% of each run, Pallas kernels for 0% -> 7%
where the time goes in v1:
time: 153 us
  starting transfers between devices  64.8 us (42%)
  Pallas kernels  48.2 us (32%)
  waiting for transfers between devices  32.7 us (21%)
  local copies, waits for them, and re-layouts  3.71 us (2%)
  other arithmetic  1.85 us (1%)
  between operations  1.57 us (1%)
    ppermute x53, starting transfers between devices, exchange(): lax.ppermute(x, axis, [(i, i ^ k) for i in range(n)])  59.4 us
    pallas_call x10, Pallas kernels, call(): pl.pallas_call(kernel, out_shape=tuple(outs), in_specs=specs, out_specs=t...  48.2 us
    ppermute x53, waiting for transfers between devices, exchange(): lax.ppermute(x, axis, [(i, i ^ k) for i in range(n)])  29.3 us
    ppermute x7, starting transfers between devices, body(): lax.ppermute(mixed[k], 'col', [(i, i ^ k) for i in range(n_col)])  4.74 us
    ppermute x7, waiting for transfers between devices, body(): lax.ppermute(mixed[k], 'col', [(i, i ^ k) for i in range(n_col)])  3.4 us
  transfers between devices with their start and end apart: 61, of which 24 were waited for; matrix products, arithmetic and copies ran while one was open for 2% of the time, Pallas kernels for 7%

profile of v1, /device:TPU:0, one launch (start us, length us, event | category | flops | bytes accessed | tf_op | source)
XLA Modules:
  0.0 152.8 jit_solution(2265888453819354464)
XLA Ops:
  2.8 4.3 %collective-permute-start = (bf16[64,512]{1,0:T(8,128)(2,1)S(1)}, bf16[64,512]{1,0:T(8,128)(2,1)S(1)}, u32[]{:S(2)}, u32[]{:S(2)}) collective-permute-start(bf16[64,512]{1,0:T(8,128)(2,1)S(1)} %shard_map.85.refs_1_), channel_id=1, source_target_pairs={{0,8},{8,0},{16,24},{24,16},{1,9},{9,1},{17,25},{25,17},{2,10},{10... | collective-permute-start | bytes 196616 | tf_op jit(solution)/shard_map/ppermute | solution.py:288
  7.2 3.2 %collective-permute-start.1 = (bf16[64,512]{1,0:T(8,128)(2,1)S(1)}, bf16[64,512]{1,0:T(8,128)(2,1)S(1)}, u32[]{:S(2)}, u32[]{:S(2)}) collective-permute-start(bf16[64,512]{1,0:T(8,128)(2,1)S(1)} %shard_map.85.refs_1_), channel_id=1, source_target_pairs={{0,16},{8,24},{16,0},{24,8},{1,17},{9,25},{17,1},{25,9},{2,18},{10... | collective-permute-start | bytes 196616 | tf_op jit(solution)/shard_map/ppermute | solution.py:288
  14.8 4.0 %collective-permute-start.10 = (bf16[64,512]{1,0:T(8,128)(2,1)S(1)}, bf16[64,512]{1,0:T(8,128)(2,1)S(1)}, u32[]{:S(2)}, u32[]{:S(2)}) collective-permute-start(bf16[64,512]{1,0:T(8,128)(2,1)S(1)} %collective-permute-done.3.refs_5_), channel_id=1, source_target_pairs={{0,7},{1,6},{2,5},{3,4},{4,3},{5,2},{6,1},{7,0},{8,15},{9,14},{10,... | collective-permute-start | bytes 196616 | tf_op jit(solution)/shard_map/ppermute | solution.py:288
  21.6 2.1 %collective-permute-start.8 = (bf16[64,512]{1,0:T(8,128)(2,1)S(1)}, bf16[64,512]{1,0:T(8,128)(2,1)S(1)}, u32[]{:S(2)}, u32[]{:S(2)}) collective-permute-start(bf16[64,512]{1,0:T(8,128)(2,1)S(1)} %collective-permute-done.3.refs_5_), channel_id=1, source_target_pairs={{0,5},{1,4},{2,7},{3,6},{4,1},{5,0},{6,3},{7,2},{8,13},{9,12},{10,... | collective-permute-start | bytes 196616 | tf_op jit(solution)/shard_map/ppermute | solution.py:288
  26.6 2.4 %collective-permute-done.8.refs_10_ = bf16[64,512]{1,0:T(8,128)(2,1)S(1)} collective-permute-done((bf16[64,512]{1,0:T(8,128)(2,1)S(1)}, bf16[64,512]{1,0:T(8,128)(2,1)S(1)}, u32[]{:S(2)}, u32[]{:S(2)}) %collective-permute-start.8) | collective-permute-done | bytes 65568 | tf_op jit(solution)/shard_map/ppermute | solution.py:288
  29.0 14.4 %shard_map.86 = (bf16[128,128,128]{2,1,0:T(8,128)(2,1)S(1)}, f32[16,128]{1,0:T(8,128)S(1)}) custom-call(s32[3,128]{1,0:T(4,128)S(1)} %pad_add_fusion.refs_0_, bf16[64,512]{1,0:T(8,128)(2,1)S(1)} %shard_map.85.refs_1_, bf16[64,512]{1,0:T(8,128)(2,1)S(1)} %collective-permute-done.refs_2_, bf16[64,512]{1,0:T(8,128)(2,1)S(1)} %collective-permute-done.1.refs_3_, ...), custom_call_target="tpu_custom_call" | custom-call | flops 16777216 | bytes 1048576 | tf_op jit(solution)/shard_map/pallas_call | solution.py:49
  43.5 4.3 %collective-permute-start.13 = (f32[16,128]{1,0:T(8,128)S(1)}, f32[16,128]{1,0:T(8,128)S(1)}, u32[]{:S(2)}, u32[]{:S(2)}) collective-permute-start(f32[16,128]{1,0:T(8,128)S(1)} %get-tuple-element.20.refs_2_), channel_id=1, source_target_pairs={{0,24},{8,16},{16,8},{24,0},{1,25},{9,17},{17,9},{25,1},{2,26},{10... | collective-permute-start | bytes 24584 | tf_op jit(solution)/shard_map/ppermute | solution.py:288
  49.5 3.6 %shard_map.87.refs_2_ = f32[32,128]{1,0:T(8,128)S(1)} custom-call(s32[3,128]{1,0:T(4,128)S(1)} %pad_add_fusion.refs_0_, bf16[128,128,128]{2,1,0:T(8,128)(2,1)S(1)} %get-tuple-element.19.refs_1_, f32[16,128]{1,0:T(8,128)S(1)} %get-tuple-element.20.refs_2_, f32[16,128]{1,0:T(8,128)S(1)} %collective-permute-done.11.refs_3_, ...), custom_call_target="tpu_custom_call" | custom-call | flops 16777216 | bytes 1048576 | tf_op jit(solution)/shard_map/pallas_call | solution.py:49
  53.3 1.8 %collective-permute-start.16 = (f32[32,128]{1,0:T(8,128)S(1)}, f32[32,128]{1,0:T(8,128)S(1)}, u32[]{:S(2)}, u32[]{:S(2)}) collective-permute-start(f32[32,128]{1,0:T(8,128)S(1)} %shard_map.87.refs_2_), channel_id=1, source_target_pairs={{0,3},{1,2},{2,1},{3,0},{4,7},{5,6},{6,5},{7,4},{8,11},{9,10},{10,... | collective-permute-start | bytes 49160 | tf_op jit(solution)/shard_map/ppermute | solution.py:288
  57.4 2.2 %collective-permute-start.20 = (f32[32,128]{1,0:T(8,128)S(1)}, f32[32,128]{1,0:T(8,128)S(1)}, u32[]{:S(2)}, u32[]{:S(2)}) collective-permute-start(f32[32,128]{1,0:T(8,128)S(1)} %shard_map.87.refs_2_), channel_id=1, source_target_pairs={{0,7},{1,6},{2,5},{3,4},{4,3},{5,2},{6,1},{7,0},{8,15},{9,14},{10,... | collective-permute-start | bytes 49160 | tf_op jit(solution)/shard_map/ppermute | solution.py:288
  59.6 2.1 %collective-permute-done.19.refs_8_ = f32[32,128]{1,0:T(8,128)S(1)} collective-permute-done((f32[32,128]{1,0:T(8,128)S(1)}, f32[32,128]{1,0:T(8,128)S(1)}, u32[]{:S(2)}, u32[]{:S(2)}) %collective-permute-start.19) | collective-permute-done | bytes 16416 | tf_op jit(solution)/shard_map/ppermute | solution.py:288
  61.6 4.7 %shard_map.88.refs_2_ = f32[16,128]{1,0:T(8,128)S(1)} custom-call(s32[3,128]{1,0:T(4,128)S(1)} %pad_add_fusion.refs_0_, bf16[128,128,128]{2,1,0:T(8,128)(2,1)S(1)} %get-tuple-element.19.refs_1_, f32[32,128]{1,0:T(8,128)S(1)} %shard_map.87.refs_2_, f32[32,128]{1,0:T(8,128)S(1)} %collective-permute-done.14.refs_3_, ...), custom_call_target="tpu_custom_call" | custom-call | flops 16777216 | bytes 1048576 | tf_op jit(solution)/shard_map/pallas_call | solution.py:49
  66.5 4.3 %collective-permute-start.23 = (f32[16,128]{1,0:T(8,128)S(1)}, f32[16,128]{1,0:T(8,128)S(1)}, u32[]{:S(2)}, u32[]{:S(2)}) collective-permute-start(f32[16,128]{1,0:T(8,128)S(1)} %shard_map.88.refs_2_), channel_id=1, source_target_pairs={{0,24},{8,16},{16,8},{24,0},{1,25},{9,17},{17,9},{25,1},{2,26},{10... | collective-permute-start | bytes 24584 | tf_op jit(solution)/shard_map/ppermute | solution.py:288
  72.5 3.6 %shard_map.89.refs_2_ = f32[32,128]{1,0:T(8,128)S(1)} custom-call(s32[3,128]{1,0:T(4,128)S(1)} %pad_add_fusion.refs_0_, bf16[128,128,128]{2,1,0:T(8,128)(2,1)S(1)} %get-tuple-element.19.refs_1_, f32[16,128]{1,0:T(8,128)S(1)} %shard_map.88.refs_2_, f32[16,128]{1,0:T(8,128)S(1)} %collective-permute-done.21.refs_3_, ...), custom_call_target="tpu_custom_call" | custom-call | flops 16777216 | bytes 1048576 | tf_op jit(solution)/shard_map/pallas_call | solution.py:49
  76.3 2.0 %collective-permute-start.35 = (bf16[64,512]{1,0:T(8,128)(2,1)S(1)}, bf16[64,512]{1,0:T(8,128)(2,1)S(1)}, u32[]{:S(2)}, u32[]{:S(2)}) collective-permute-start(bf16[64,512]{1,0:T(8,128)(2,1)S(1)} %copy-done), channel_id=1, source_target_pairs={{0,16},{8,24},{16,0},{24,8},{1,17},{9,25},{17,1},{25,9},{2,18},{10... | collective-permute-start | bytes 196616 | tf_op jit(solution)/shard_map/ppermute | solution.py:288
  78.4 2.3 %collective-permute-start.36 = (bf16[64,512]{1,0:T(8,128)(2,1)S(1)}, bf16[64,512]{1,0:T(8,128)(2,1)S(1)}, u32[]{:S(2)}, u32[]{:S(2)}) collective-permute-start(bf16[64,512]{1,0:T(8,128)(2,1)S(1)} %copy-done), channel_id=1, source_target_pairs={{0,24},{8,16},{16,8},{24,0},{1,25},{9,17},{17,9},{25,1},{2,26},{10... | collective-permute-start | bytes 196616 | tf_op jit(solution)/shard_map/ppermute | solution.py:288
  81.7 2.8 %collective-permute-done.25.refs_4_ = f32[32,128]{1,0:T(8,128)S(1)} collective-permute-done((f32[32,128]{1,0:T(8,128)S(1)}, f32[32,128]{1,0:T(8,128)S(1)}, u32[]{:S(2)}, u32[]{:S(2)}) %collective-permute-start.25) | collective-permute-done | bytes 16416 | tf_op jit(solution)/shard_map/ppermute | solution.py:288
  84.7 3.5 %collective-permute-done.27.refs_6_ = f32[32,128]{1,0:T(8,128)S(1)} collective-permute-done((f32[32,128]{1,0:T(8,128)S(1)}, f32[32,128]{1,0:T(8,128)S(1)}, u32[]{:S(2)}, u32[]{:S(2)}) %collective-permute-start.27) | collective-permute-done | bytes 16416 | tf_op jit(solution)/shard_map/ppermute | solution.py:288
  89.5 3.3 %collective-permute-done.29.refs_8_ = f32[32,128]{1,0:T(8,128)S(1)} collective-permute-done((f32[32,128]{1,0:T(8,128)S(1)}, f32[32,128]{1,0:T(8,128)S(1)}, u32[]{:S(2)}, u32[]{:S(2)}) %collective-permute-start.29) | collective-permute-done | bytes 16416 | tf_op jit(solution)/shard_map/ppermute | solution.py:288
  93.6 4.7 %shard_map.90.refs_2_ = f32[16,128]{1,0:T(8,128)S(1)} custom-call(s32[3,128]{1,0:T(4,128)S(1)} %pad_add_fusion.refs_0_, bf16[128,128,128]{2,1,0:T(8,128)(2,1)S(1)} %get-tuple-element.19.refs_1_, f32[32,128]{1,0:T(8,128)S(1)} %shard_map.89.refs_2_, f32[32,128]{1,0:T(8,128)S(1)} %collective-permute-done.24.refs_3_, ...), custom_call_target="tpu_custom_call" | custom-call | flops 16777216 | bytes 1048576 | tf_op jit(solution)/shard_map/pallas_call | solution.py:49
  98.5 4.3 %collective-permute-start.33 = (f32[16,128]{1,0:T(8,128)S(1)}, f32[16,128]{1,0:T(8,128)S(1)}, u32[]{:S(2)}, u32[]{:S(2)}) collective-permute-start(f32[16,128]{1,0:T(8,128)S(1)} %shard_map.90.refs_2_), channel_id=1, source_target_pairs={{0,24},{8,16},{16,8},{24,0},{1,25},{9,17},{17,9},{25,1},{2,26},{10... | collective-permute-start | bytes 24584 | tf_op jit(solution)/shard_map/ppermute | solution.py:288
  104.5 4.8 %shard_map.91 = (f32[32,128]{1,0:T(8,128)S(1)}, bf16[2,64,128]{2,1,0:T(8,128)(2,1)S(1)}, f32[16,128]{1,0:T(8,128)}, bf16[16,64,128]{2,1,0:T(8,128)(2,1)S(1)}) custom-call(s32[3,128]{1,0:T(4,128)S(1)} %pad_add_fusion.refs_0_, bf16[128,128,128]{2,1,0:T(8,128)(2,1)S(1)} %get-tuple-element.19.refs_1_, f32[16,128]{1,0:T(8,128)S(1)} %shard_map.90.refs_2_, ...), custom_call_target="tpu_custom_call" | custom-call | flops 16777216 | bytes 1048576 | tf_op jit(solution)/shard_map/pallas_call | solution.py:49
  109.3 1.9 %collective-permute-start.39 = (f32[32,128]{1,0:T(8,128)S(1)}, f32[32,128]{1,0:T(8,128)S(1)}, u32[]{:S(2)}, u32[]{:S(2)}) collective-permute-start(f32[32,128]{1,0:T(8,128)S(1)} %get-tuple-element.21.refs_1_), channel_id=1, source_target_pairs={{0,3},{1,2},{2,1},{3,0},{4,7},{5,6},{6,5},{7,4},{8,11},{9,10},{10,... | collective-permute-start | bytes 49160 | tf_op jit(solution)/shard_map/ppermute | solution.py:288
  117.8 4.1 %shard_map.93 = (bf16[4,64,128]{2,1,0:T(8,128)(2,1)S(1)}, bf16[4,64,128]{2,1,0:T(8,128)(2,1)S(1)}, bf16[4,64,128]{2,1,0:T(8,128)(2,1)S(1)}, bf16[4,64,128]{2,1,0...) custom-call(s32[3,128]{1,0:T(4,128)S(1)} %pad_add_fusion.refs_0_, ...), custom_call_target="tpu_custom_call" | custom-call | flops 16777216 | bytes 1048576 | tf_op jit(solution)/shard_map/pallas_call | solution.py:49
  122.5 2.8 %collective-permute-start.49 = (bf16[2,64,128]{2,1,0:T(8,128)(2,1)S(1)}, bf16[2,64,128]{2,1,0:T(8,128)(2,1)S(1)}, u32[]{:S(2)}, u32[]{:S(2)}) collective-permute-start(bf16[2,64,128]{2,1,0:T(8,128)(2,1)S(1)} %get-tuple-element.22.refs_9_), channel_id=1, source_target_pairs={{0,6},{1,7},{2,4},{3,5},{4,2},{5,3},{6,0},{7,1},{8,14},{9,15},{10,... | collective-permute-start | bytes 98312 | tf_op jit(solution)/shard_map/ppermute | solution.py:288
  127.4 2.1 %collective-permute-done.50.refs_16_ = bf16[2,64,128]{2,1,0:T(8,128)(2,1)S(1)} collective-permute-done((bf16[2,64,128]{2,1,0:T(8,128)(2,1)S(1)}, bf16[2,64,128]{2,1,0:T(8,128)(2,1)S(1)}, u32[]{:S(2)}, u32[]{:S(2)}) %collective-permute-start.50) | collective-permute-done | bytes 32800 | tf_op jit(solution)/shard_map/ppermute | solution.py:288
  130.9 2.1 %collective-permute-start.52 = (f32[64,64]{1,0:T(8,128)S(1)}, f32[64,64]{1,0:T(8,128)S(1)}, u32[]{:S(2)}, u32[]{:S(2)}) collective-permute-start(f32[64,64]{1,0:T(8,128)S(1)} %get-tuple-element.25.refs_1_), channel_id=1, source_target_pairs={{0,16},{8,24},{16,0},{24,8},{1,17},{9,25},{17,1},{25,9},{2,18},{10... | collective-permute-start | bytes 49160 | tf_op jit(solution)/shard_map/ppermute | solution.py:288
  132.9 2.3 %collective-permute-start.53 = (f32[64,64]{1,0:T(8,128)S(1)}, f32[64,64]{1,0:T(8,128)S(1)}, u32[]{:S(2)}, u32[]{:S(2)}) collective-permute-start(f32[64,64]{1,0:T(8,128)S(1)} %get-tuple-element.25.refs_1_), channel_id=1, source_target_pairs={{0,24},{8,16},{16,8},{24,0},{1,25},{9,17},{17,9},{25,1},{2,26},{10... | collective-permute-start | bytes 49160 | tf_op jit(solution)/shard_map/ppermute | solution.py:288
  136.7 1.9 %collective-permute-done.53.refs_4_ = f32[64,64]{1,0:T(8,128)S(1)} collective-permute-done((f32[64,64]{1,0:T(8,128)S(1)}, f32[64,64]{1,0:T(8,128)S(1)}, u32[]{:S(2)}, u32[]{:S(2)}) %collective-permute-start.53) | collective-permute-done | bytes 16416 | tf_op jit(solution)/shard_map/ppermute | solution.py:288
  138.7 1.8 %collective-permute-start.59 = (bf16[4,64,128]{2,1,0:T(8,128)(2,1)S(1)}, bf16[4,64,128]{2,1,0:T(8,128)(2,1)S(1)}, u32[]{:S(2)}, u32[]{:S(2)}) collective-permute-start(bf16[4,64,128]{2,1,0:T(8,128)(2,1)S(1)} %get-tuple-element.33), channel_id=1, source_target_pairs={{0,6},{1,7},{2,4},{3,5},{4,2},{5,3},{6,0},{7,1},{8,14},{9,15},{10,... | collective-permute-start | bytes 196616 | tf_op jit(solution)/shard_map/ppermute | solution.py:404
  142.4 2.1 %collective-permute-done.59.refs_11_ = bf16[4,64,128]{2,1,0:T(8,128)(2,1)S(1)} collective-permute-done((bf16[4,64,128]{2,1,0:T(8,128)(2,1)S(1)}, bf16[4,64,128]{2,1,0:T(8,128)(2,1)S(1)}, u32[]{:S(2)}, u32[]{:S(2)}) %collective-permute-start.59) | collective-permute-done | bytes 65568 | tf_op jit(solution)/shard_map/ppermute | solution.py:404
  145.9 6.9 %shard_map.94 = f32[64,512]{1,0:T(8,128)} custom-call(s32[3,128]{1,0:T(4,128)S(1)} %pad_add_fusion.refs_0_, f32[64,64]{1,0:T(8,128)S(1)} %get-tuple-element.25.refs_1_, f32[64,64]{1,0:T(8,128)S(1)} %collective-permute-done.51.refs_2_, f32[64,64]{1,0:T(8,128)S(1)} %collective-permute-done.52.refs_3_, f32[64,64]{1,0:T(8,128)S(1)} %collective-permute-done.53.refs_4_, ...), custom_call_target="tpu_custom_call" | custom-call | flops 16777216 | bytes 1048576 | tf_op jit(solution)/shard_map/pallas_call | solution.py:49
  (118 shorter events, 38.5 us)
Async XLA Ops:
  2.2 12.6 %collective-permute-start.3 = (bf16[64,512]{1,0:T(8,128)(2,1)S(1)}, bf16[64,512]{1,0:T(8,128)(2,1)S(1)}, u32[]{:S(2)}, u32[]{:S(2)}) collective-permute-start(bf16[64,512]{1,0:T(8,128)(2,1)S(1)} %shard_map.85.refs_1_), channel_id=1, source_target_pairs={{0,0},{8,1},{16,2},{24,3},{1,4},{9,5},{17,6},{25,7},{2,8},{10,9},{... | collective-permute-start | bytes 196616 | tf_op jit(solution)/shard_map/ppermute | solution.py:337
  2.8 17.3 %collective-permute-start = (bf16[64,512]{1,0:T(8,128)(2,1)S(1)}, bf16[64,512]{1,0:T(8,128)(2,1)S(1)}, u32[]{:S(2)}, u32[]{:S(2)}) collective-permute-start(bf16[64,512]{1,0:T(8,128)(2,1)S(1)} %shard_map.85.refs_1_), channel_id=1, source_target_pairs={{0,8},{8,0},{16,24},{24,16},{1,9},{9,1},{17,25},{25,17},{2,10},{10... | collective-permute-start | bytes 196616 | tf_op jit(solution)/shard_map/ppermute | solution.py:288
  7.2 13.0 %collective-permute-start.1 = (bf16[64,512]{1,0:T(8,128)(2,1)S(1)}, bf16[64,512]{1,0:T(8,128)(2,1)S(1)}, u32[]{:S(2)}, u32[]{:S(2)}) collective-permute-start(bf16[64,512]{1,0:T(8,128)(2,1)S(1)} %shard_map.85.refs_1_), channel_id=1, source_target_pairs={{0,16},{8,24},{16,0},{24,8},{1,17},{9,25},{17,1},{25,9},{2,18},{10... | collective-permute-start | bytes 196616 | tf_op jit(solution)/shard_map/ppermute | solution.py:288
  10.4 11.2 %collective-permute-start.2 = (bf16[64,512]{1,0:T(8,128)(2,1)S(1)}, bf16[64,512]{1,0:T(8,128)(2,1)S(1)}, u32[]{:S(2)}, u32[]{:S(2)}) collective-permute-start(bf16[64,512]{1,0:T(8,128)(2,1)S(1)} %shard_map.85.refs_1_), channel_id=1, source_target_pairs={{0,24},{8,16},{16,8},{24,0},{1,25},{9,17},{17,9},{25,1},{2,26},{10... | collective-permute-start | bytes 196616 | tf_op jit(solution)/shard_map/ppermute | solution.py:288
  14.8 6.8 %collective-permute-start.10 = (bf16[64,512]{1,0:T(8,128)(2,1)S(1)}, bf16[64,512]{1,0:T(8,128)(2,1)S(1)}, u32[]{:S(2)}, u32[]{:S(2)}) collective-permute-start(bf16[64,512]{1,0:T(8,128)(2,1)S(1)} %collective-permute-done.3.refs_5_), channel_id=1, source_target_pairs={{0,7},{1,6},{2,5},{3,4},{4,3},{5,2},{6,1},{7,0},{8,15},{9,14},{10,... | collective-permute-start | bytes 196616 | tf_op jit(solution)/shard_map/ppermute | solution.py:288
  18.9 4.9 %collective-permute-start.4 = (bf16[64,512]{1,0:T(8,128)(2,1)S(1)}, bf16[64,512]{1,0:T(8,128)(2,1)S(1)}, u32[]{:S(2)}, u32[]{:S(2)}) collective-permute-start(bf16[64,512]{1,0:T(8,128)(2,1)S(1)} %collective-permute-done.3.refs_5_), channel_id=1, source_target_pairs={{0,1},{1,0},{2,3},{3,2},{4,5},{5,4},{6,7},{7,6},{8,9},{9,8},{10,11... | collective-permute-start | bytes 196616 | tf_op jit(solution)/shard_map/ppermute | solution.py:288
  20.2 4.8 %collective-permute-start.5 = (bf16[64,512]{1,0:T(8,128)(2,1)S(1)}, bf16[64,512]{1,0:T(8,128)(2,1)S(1)}, u32[]{:S(2)}, u32[]{:S(2)}) collective-permute-start(bf16[64,512]{1,0:T(8,128)(2,1)S(1)} %collective-permute-done.3.refs_5_), channel_id=1, source_target_pairs={{0,2},{1,3},{2,0},{3,1},{4,6},{5,7},{6,4},{7,5},{8,10},{9,11},{10,... | collective-permute-start | bytes 196616 | tf_op jit(solution)/shard_map/ppermute | solution.py:288
  21.6 5.0 %collective-permute-start.7 = (bf16[64,512]{1,0:T(8,128)(2,1)S(1)}, bf16[64,512]{1,0:T(8,128)(2,1)S(1)}, u32[]{:S(2)}, u32[]{:S(2)}) collective-permute-start(bf16[64,512]{1,0:T(8,128)(2,1)S(1)} %collective-permute-done.3.refs_5_), channel_id=1, source_target_pairs={{0,4},{1,5},{2,6},{3,7},{4,0},{5,1},{6,2},{7,3},{8,12},{9,13},{10,... | collective-permute-start | bytes 196616 | tf_op jit(solution)/shard_map/ppermute | solution.py:288
  21.6 7.4 %collective-permute-start.8 = (bf16[64,512]{1,0:T(8,128)(2,1)S(1)}, bf16[64,512]{1,0:T(8,128)(2,1)S(1)}, u32[]{:S(2)}, u32[]{:S(2)}) collective-permute-start(bf16[64,512]{1,0:T(8,128)(2,1)S(1)} %collective-permute-done.3.refs_5_), channel_id=1, source_target_pairs={{0,5},{1,4},{2,7},{3,6},{4,1},{5,0},{6,3},{7,2},{8,13},{9,12},{10,... | collective-permute-start | bytes 196616 | tf_op jit(solution)/shard_map/ppermute | solution.py:288
  23.7 5.3 %collective-permute-start.9 = (bf16[64,512]{1,0:T(8,128)(2,1)S(1)}, bf16[64,512]{1,0:T(8,128)(2,1)S(1)}, u32[]{:S(2)}, u32[]{:S(2)}) collective-permute-start(bf16[64,512]{1,0:T(8,128)(2,1)S(1)} %collective-permute-done.3.refs_5_), channel_id=1, source_target_pairs={{0,6},{1,7},{2,4},{3,5},{4,2},{5,3},{6,0},{7,1},{8,14},{9,15},{10,... | collective-permute-start | bytes 196616 | tf_op jit(solution)/shard_map/ppermute | solution.py:288
  43.5 6.0 %collective-permute-start.13 = (f32[16,128]{1,0:T(8,128)S(1)}, f32[16,128]{1,0:T(8,128)S(1)}, u32[]{:S(2)}, u32[]{:S(2)}) collective-permute-start(f32[16,128]{1,0:T(8,128)S(1)} %get-tuple-element.20.refs_2_), channel_id=1, source_target_pairs={{0,24},{8,16},{16,8},{24,0},{1,25},{9,17},{17,9},{25,1},{2,26},{10... | collective-permute-start | bytes 24584 | tf_op jit(solution)/shard_map/ppermute | solution.py:288
  53.3 6.2 %collective-permute-start.16 = (f32[32,128]{1,0:T(8,128)S(1)}, f32[32,128]{1,0:T(8,128)S(1)}, u32[]{:S(2)}, u32[]{:S(2)}) collective-permute-start(f32[32,128]{1,0:T(8,128)S(1)} %shard_map.87.refs_2_), channel_id=1, source_target_pairs={{0,3},{1,2},{2,1},{3,0},{4,7},{5,6},{6,5},{7,4},{8,11},{9,10},{10,... | collective-permute-start | bytes 49160 | tf_op jit(solution)/shard_map/ppermute | solution.py:288
  56.8 4.8 %collective-permute-start.19 = (f32[32,128]{1,0:T(8,128)S(1)}, f32[32,128]{1,0:T(8,128)S(1)}, u32[]{:S(2)}, u32[]{:S(2)}) collective-permute-start(f32[32,128]{1,0:T(8,128)S(1)} %shard_map.87.refs_2_), channel_id=1, source_target_pairs={{0,6},{1,7},{2,4},{3,5},{4,2},{5,3},{6,0},{7,1},{8,14},{9,15},{10,... | collective-permute-start | bytes 49160 | tf_op jit(solution)/shard_map/ppermute | solution.py:288
  66.5 6.0 %collective-permute-start.23 = (f32[16,128]{1,0:T(8,128)S(1)}, f32[16,128]{1,0:T(8,128)S(1)}, u32[]{:S(2)}, u32[]{:S(2)}) collective-permute-start(f32[16,128]{1,0:T(8,128)S(1)} %shard_map.88.refs_2_), channel_id=1, source_target_pairs={{0,24},{8,16},{16,8},{24,0},{1,25},{9,17},{17,9},{25,1},{2,26},{10... | collective-permute-start | bytes 24584 | tf_op jit(solution)/shard_map/ppermute | solution.py:288
  76.2 22.2 %collective-permute-start.34 = (bf16[64,512]{1,0:T(8,128)(2,1)S(1)}, bf16[64,512]{1,0:T(8,128)(2,1)S(1)}, u32[]{:S(2)}, u32[]{:S(2)}) collective-permute-start(bf16[64,512]{1,0:T(8,128)(2,1)S(1)} %copy-done), channel_id=1, source_target_pairs={{0,8},{8,0},{16,24},{24,16},{1,9},{9,1},{17,25},{25,17},{2,10},{10... | collective-permute-start | bytes 196616 | tf_op jit(solution)/shard_map/ppermute | solution.py:288
  76.3 26.5 %collective-permute-start.35 = (bf16[64,512]{1,0:T(8,128)(2,1)S(1)}, bf16[64,512]{1,0:T(8,128)(2,1)S(1)}, u32[]{:S(2)}, u32[]{:S(2)}) collective-permute-start(bf16[64,512]{1,0:T(8,128)(2,1)S(1)} %copy-done), channel_id=1, source_target_pairs={{0,16},{8,24},{16,0},{24,8},{1,17},{9,25},{17,1},{25,9},{2,18},{10... | collective-permute-start | bytes 196616 | tf_op jit(solution)/shard_map/ppermute | solution.py:288
  78.4 24.4 %collective-permute-start.36 = (bf16[64,512]{1,0:T(8,128)(2,1)S(1)}, bf16[64,512]{1,0:T(8,128)(2,1)S(1)}, u32[]{:S(2)}, u32[]{:S(2)}) collective-permute-start(bf16[64,512]{1,0:T(8,128)(2,1)S(1)} %copy-done), channel_id=1, source_target_pairs={{0,24},{8,16},{16,8},{24,0},{1,25},{9,17},{17,9},{25,1},{2,26},{10... | collective-permute-start | bytes 196616 | tf_op jit(solution)/shard_map/ppermute | solution.py:288
  84.4 5.1 %collective-permute-start.28 = (f32[32,128]{1,0:T(8,128)S(1)}, f32[32,128]{1,0:T(8,128)S(1)}, u32[]{:S(2)}, u32[]{:S(2)}) collective-permute-start(f32[32,128]{1,0:T(8,128)S(1)} %shard_map.89.refs_2_), channel_id=1, source_target_pairs={{0,5},{1,4},{2,7},{3,6},{4,1},{5,0},{6,3},{7,2},{8,13},{9,12},{10,... | collective-permute-start | bytes 49160 | tf_op jit(solution)/shard_map/ppermute | solution.py:288
  98.5 6.0 %collective-permute-start.33 = (f32[16,128]{1,0:T(8,128)S(1)}, f32[16,128]{1,0:T(8,128)S(1)}, u32[]{:S(2)}, u32[]{:S(2)}) collective-permute-start(f32[16,128]{1,0:T(8,128)S(1)} %shard_map.90.refs_2_), channel_id=1, source_target_pairs={{0,24},{8,16},{16,8},{24,0},{1,25},{9,17},{17,9},{25,1},{2,26},{10... | collective-permute-start | bytes 24584 | tf_op jit(solution)/shard_map/ppermute | solution.py:288
  112.8 4.8 %collective-permute-start.42 = (f32[32,128]{1,0:T(8,128)S(1)}, f32[32,128]{1,0:T(8,128)S(1)}, u32[]{:S(2)}, u32[]{:S(2)}) collective-permute-start(f32[32,128]{1,0:T(8,128)S(1)} %get-tuple-element.21.refs_1_), channel_id=1, source_target_pairs={{0,6},{1,7},{2,4},{3,5},{4,2},{5,3},{6,0},{7,1},{8,14},{9,15},{10,... | collective-permute-start | bytes 49160 | tf_op jit(solution)/shard_map/ppermute | solution.py:288
  113.3 8.9 %collective-permute-start.44 = (bf16[2,64,128]{2,1,0:T(8,128)(2,1)S(1)}, bf16[2,64,128]{2,1,0:T(8,128)(2,1)S(1)}, u32[]{:S(2)}, u32[]{:S(2)}) collective-permute-start(bf16[2,64,128]{2,1,0:T(8,128)(2,1)S(1)} %get-tuple-element.22.refs_9_), channel_id=1, source_target_pairs={{0,1},{1,0},{2,3},{3,2},{4,5},{5,4},{6,7},{7,6},{8,9},{9,8},{10,11... | collective-permute-start | bytes 98312 | tf_op jit(solution)/shard_map/ppermute | solution.py:288
  113.6 8.9 %collective-permute-start.45 = (bf16[2,64,128]{2,1,0:T(8,128)(2,1)S(1)}, bf16[2,64,128]{2,1,0:T(8,128)(2,1)S(1)}, u32[]{:S(2)}, u32[]{:S(2)}) collective-permute-start(bf16[2,64,128]{2,1,0:T(8,128)(2,1)S(1)} %get-tuple-element.22.refs_9_), channel_id=1, source_target_pairs={{0,2},{1,3},{2,0},{3,1},{4,6},{5,7},{6,4},{7,5},{8,10},{9,11},{10,... | collective-permute-start | bytes 98312 | tf_op jit(solution)/shard_map/ppermute | solution.py:288
  114.9 7.6 %collective-permute-start.46 = (bf16[2,64,128]{2,1,0:T(8,128)(2,1)S(1)}, bf16[2,64,128]{2,1,0:T(8,128)(2,1)S(1)}, u32[]{:S(2)}, u32[]{:S(2)}) collective-permute-start(bf16[2,64,128]{2,1,0:T(8,128)(2,1)S(1)} %get-tuple-element.22.refs_9_), channel_id=1, source_target_pairs={{0,3},{1,2},{2,1},{3,0},{4,7},{5,6},{6,5},{7,4},{8,11},{9,10},{10,... | collective-permute-start | bytes 98312 | tf_op jit(solution)/shard_map/ppermute | solution.py:288
  115.2 10.1 %collective-permute-start.47 = (bf16[2,64,128]{2,1,0:T(8,128)(2,1)S(1)}, bf16[2,64,128]{2,1,0:T(8,128)(2,1)S(1)}, u32[]{:S(2)}, u32[]{:S(2)}) collective-permute-start(bf16[2,64,128]{2,1,0:T(8,128)(2,1)S(1)} %get-tuple-element.22.refs_9_), channel_id=1, source_target_pairs={{0,4},{1,5},{2,6},{3,7},{4,0},{5,1},{6,2},{7,3},{8,12},{9,13},{10,... | collective-permute-start | bytes 98312 | tf_op jit(solution)/shard_map/ppermute | solution.py:288
  121.9 16.8 %collective-permute-start.54 = (bf16[4,64,128]{2,1,0:T(8,128)(2,1)S(1)}, bf16[4,64,128]{2,1,0:T(8,128)(2,1)S(1)}, u32[]{:S(2)}, u32[]{:S(2)}) collective-permute-start(bf16[4,64,128]{2,1,0:T(8,128)(2,1)S(1)} %get-tuple-element.28), channel_id=1, source_target_pairs={{0,1},{1,0},{2,3},{3,2},{4,5},{5,4},{6,7},{7,6},{8,9},{9,8},{10,11... | collective-permute-start | bytes 196616 | tf_op jit(solution)/shard_map/ppermute | solution.py:404
  122.2 18.3 %collective-permute-start.55 = (bf16[4,64,128]{2,1,0:T(8,128)(2,1)S(1)}, bf16[4,64,128]{2,1,0:T(8,128)(2,1)S(1)}, u32[]{:S(2)}, u32[]{:S(2)}) collective-permute-start(bf16[4,64,128]{2,1,0:T(8,128)(2,1)S(1)} %get-tuple-element.29), channel_id=1, source_target_pairs={{0,2},{1,3},{2,0},{3,1},{4,6},{5,7},{6,4},{7,5},{8,10},{9,11},{10,... | collective-permute-start | bytes 196616 | tf_op jit(solution)/shard_map/ppermute | solution.py:404
  122.5 4.9 %collective-permute-start.49 = (bf16[2,64,128]{2,1,0:T(8,128)(2,1)S(1)}, bf16[2,64,128]{2,1,0:T(8,128)(2,1)S(1)}, u32[]{:S(2)}, u32[]{:S(2)}) collective-permute-start(bf16[2,64,128]{2,1,0:T(8,128)(2,1)S(1)} %get-tuple-element.22.refs_9_), channel_id=1, source_target_pairs={{0,6},{1,7},{2,4},{3,5},{4,2},{5,3},{6,0},{7,1},{8,14},{9,15},{10,... | collective-permute-start | bytes 98312 | tf_op jit(solution)/shard_map/ppermute | solution.py:288
  130.9 4.8 %collective-permute-start.52 = (f32[64,64]{1,0:T(8,128)S(1)}, f32[64,64]{1,0:T(8,128)S(1)}, u32[]{:S(2)}, u32[]{:S(2)}) collective-permute-start(f32[64,64]{1,0:T(8,128)S(1)} %get-tuple-element.25.refs_1_), channel_id=1, source_target_pairs={{0,16},{8,24},{16,0},{24,8},{1,17},{9,25},{17,1},{25,9},{2,18},{10... | collective-permute-start | bytes 49160 | tf_op jit(solution)/shard_map/ppermute | solution.py:288
  132.9 5.7 %collective-permute-start.53 = (f32[64,64]{1,0:T(8,128)S(1)}, f32[64,64]{1,0:T(8,128)S(1)}, u32[]{:S(2)}, u32[]{:S(2)}) collective-permute-start(f32[64,64]{1,0:T(8,128)S(1)} %get-tuple-element.25.refs_1_), channel_id=1, source_target_pairs={{0,24},{8,16},{16,8},{24,0},{1,25},{9,17},{17,9},{25,1},{2,26},{10... | collective-permute-start | bytes 49160 | tf_op jit(solution)/shard_map/ppermute | solution.py:288
  135.2 6.6 %collective-permute-start.56 = (bf16[4,64,128]{2,1,0:T(8,128)(2,1)S(1)}, bf16[4,64,128]{2,1,0:T(8,128)(2,1)S(1)}, u32[]{:S(2)}, u32[]{:S(2)}) collective-permute-start(bf16[4,64,128]{2,1,0:T(8,128)(2,1)S(1)} %get-tuple-element.30), channel_id=1, source_target_pairs={{0,3},{1,2},{2,1},{3,0},{4,7},{5,6},{6,5},{7,4},{8,11},{9,10},{10,... | collective-permute-start | bytes 196616 | tf_op jit(solution)/shard_map/ppermute | solution.py:404
  135.7 6.1 %collective-permute-start.57 = (bf16[4,64,128]{2,1,0:T(8,128)(2,1)S(1)}, bf16[4,64,128]{2,1,0:T(8,128)(2,1)S(1)}, u32[]{:S(2)}, u32[]{:S(2)}) collective-permute-start(bf16[4,64,128]{2,1,0:T(8,128)(2,1)S(1)} %get-tuple-element.31), channel_id=1, source_target_pairs={{0,4},{1,5},{2,6},{3,7},{4,0},{5,1},{6,2},{7,3},{8,12},{9,13},{10,... | collective-permute-start | bytes 196616 | tf_op jit(solution)/shard_map/ppermute | solution.py:404
  138.7 5.8 %collective-permute-start.59 = (bf16[4,64,128]{2,1,0:T(8,128)(2,1)S(1)}, bf16[4,64,128]{2,1,0:T(8,128)(2,1)S(1)}, u32[]{:S(2)}, u32[]{:S(2)}) collective-permute-start(bf16[4,64,128]{2,1,0:T(8,128)(2,1)S(1)} %get-tuple-element.33), channel_id=1, source_target_pairs={{0,6},{1,7},{2,4},{3,5},{4,2},{5,3},{6,0},{7,1},{8,14},{9,15},{10,... | collective-permute-start | bytes 196616 | tf_op jit(solution)/shard_map/ppermute | solution.py:404
  (32 other events, 146.2 us)

commit v2 on v1

v2 whole, which is shorter than its diff:
```python
import functools

import jax
import jax.numpy as jnp
from jax import lax
from jax.experimental import pallas as pl
from jax.experimental.pallas import tpu as pltpu
from jax.sharding import PartitionSpec as P

BLK = 128
SWEEPS = 3
GROUP = 16
FEAT = 64
PIECES = 16
SCALE = 512.0
LOG2E = 1.4426950408889634
F32 = jnp.float32
BF16 = jnp.bfloat16
MIB = 1 << 20

VMEM_SPEC = pl.BlockSpec(memory_space=pltpu.VMEM)
SMEM_SPEC = pl.BlockSpec(memory_space=pltpu.SMEM)


def split3(x):
    high = x.astype(BF16).astype(F32)
    mid = (x - high).astype(BF16).astype(F32)
    low = (x - high - mid).astype(BF16).astype(F32)
    return high, mid, low


def tree_sum(values):
    values = list(values)
    while len(values) > 1:
        values = [a + b for a, b in zip(values[::2], values[1::2])]
    return values[0]


def call(kernel, outs, ins, scratch=(), limit=24, flops=1 << 24):
    args, specs = [], []
    for kind, array in ins:
        if kind == "smem":
            specs.append(SMEM_SPEC)
        elif kind == "any":
            specs.append(pl.BlockSpec(memory_space=pl.ANY))
        else:
            specs.append(VMEM_SPEC)
            if kind == "keep":
                array = pltpu.with_memory_space_constraint(array, pltpu.VMEM)
        args.append(array)
    return pl.pallas_call(
        kernel,
        out_shape=tuple(outs),
        in_specs=specs,
        out_specs=tuple(VMEM_SPEC for _ in outs),
        scratch_shapes=list(scratch),
        compiler_params=pltpu.CompilerParams(vmem_limit_bytes=limit * MIB),
        cost_estimate=pl.CostEstimate(flops=flops, bytes_accessed=1 << 20, transcendentals=0),
    )(*args)


def pack_kernel(prof_ref, width_ref, out_ref, work):
    pcs = prof_ref.shape[0]
    prof = prof_ref[...].astype(F32)
    norm = jnp.sum(prof * prof, axis=0, keepdims=True)
    high, mid, low = split3(norm)
    work[...] = jnp.zeros_like(work)
    work[0:pcs, :] = prof
    work[pcs : pcs + 1, :] = high
    work[pcs + 1 : pcs + 2, :] = mid
    work[pcs + 2 : pcs + 3, :] = low
    work[pcs + 3 : pcs + 6, :] = jnp.ones((3, prof.shape[1]), F32)
    work[pcs + 6 : pcs + 7, :] = width_ref[...].astype(F32)
    out_ref[...] = work[...].astype(BF16)


def slot_loop(step, count, size, group):
    def advance(number, carry):
        for i in range(0, group, size):
            step(*[number * group + i + j for j in range(size)])
        return carry

    lax.fori_loop(0, (count + group - 1) // group, advance, 0)


def shifted(me, k, n):
    return lax.rem(me + (n - k), n)


def ordered_sum(stage, refs, me):
    n = len(refs)
    for k, ref in enumerate(refs):
        stage[shifted(me, k, n)] = ref[...]
    return tree_sum([stage[i] for i in range(n)])


def square(tile, slots):
    a, b, c, d = [tile[s] for s in slots]
    return jnp.concatenate(
        [jnp.concatenate([a, b], axis=1), jnp.concatenate([c, d], axis=1)], axis=0
    )


def add_rows(acc, meta, target, slots, sums, total, spare, firsts):
    for i, (s, (row, lane)) in enumerate(zip(slots, firsts)):
        place = jnp.where(s < total, meta[target, s], spare)
        acc[place] += sums[row : row + 8, lane : lane + BLK]


def row_sums(meta, tile, left, acc, total, spare):
    def step(*slots):
        low = [left[0, meta[1, s]] for s in slots[:2]]
        high = [left[1, meta[1, s]] for s in slots[2:]]
        sums = jnp.dot(
            jnp.concatenate(low + high, axis=0),
            square(tile, slots),
            preferred_element_type=F32,
        )
        firsts = [(0, 0), (PIECES, BLK), (2 * PIECES, 0), (3 * PIECES, BLK)]
        add_rows(acc, meta, 0, slots, sums, total, spare, firsts)

    slot_loop(step, total, 4, GROUP)


def col_sums(meta, tile, left, acc, total, spare):
    def step(*slots):
        pieces = [left[i % 2, meta[0, s]] for i, s in enumerate(slots)]
        sums = lax.dot_general(
            jnp.concatenate(pieces, axis=0),
            square(tile, slots),
            (((1,), (1,)), ((), ())),
            preferred_element_type=F32,
        )
        firsts = [(0, 0), (PIECES, 0), (2 * PIECES, BLK), (3 * PIECES, BLK)]
        add_rows(acc, meta, 1, slots, sums, total, spare, firsts)

    slot_loop(step, total, 4, GROUP)


def fill_pieces(left, scaling):
    high, mid, low = split3(scaling)
    shape = (PIECES, BLK)
    rows = lax.broadcasted_iota(jnp.int32, shape, 0)
    empty = jnp.zeros(shape, F32).astype(BF16)
    for b in range(scaling.shape[0]):
        value = jnp.where(
            rows == 0,
            jnp.broadcast_to(high[b : b + 1], shape),
            jnp.where(
                rows == 1,
                jnp.broadcast_to(mid[b : b + 1], shape),
                jnp.where(rows == 2, jnp.broadcast_to(low[b : b + 1], shape), 0.0),
            ),
        ).astype(BF16)
        left[0, b] = jnp.concatenate([value, empty], axis=1)
        left[1, b] = jnp.concatenate([empty, value], axis=1)


def build_kernel(pcs, n_row, n_col, *refs):
    meta = refs[0]
    col_in = refs[1 : 1 + n_row]
    row_in = refs[1 + n_row : 1 + n_row + n_col]
    tile, part, row_prof, row_inv, col_prof, col_inv, acc, left = refs[1 + n_row + n_col :]
    per = col_in[0].shape[1] // BLK
    col_blocks, row_blocks = n_row * per, n_col * per
    total, me_row, me_col = meta[2, 0], meta[2, 2], meta[2, 3]
    chip, core = me_col // 2, lax.rem(me_col, 2)
    for k, ref in enumerate(row_in):
        piece = shifted(chip, k // 2, n_col // 2) * 2
        piece = piece + (core if k % 2 == 0 else 1 - core)
        for j in range(per):
            block = ref[:, j * BLK : (j + 1) * BLK]
            row_prof[piece * per + j] = block
            width = block.astype(F32)[pcs + 6 : pcs + 7, :]
            row_inv[piece * per + j] = jnp.broadcast_to(1.0 / width, (8, BLK))
    rows = lax.broadcasted_iota(jnp.int32, (FEAT, BLK), 0)
    for k, ref in enumerate(col_in):
        piece = shifted(me_row, k, n_row)
        for j in range(per):
            block = ref[:, j * BLK : (j + 1) * BLK].astype(F32)
            turned = jnp.where(rows < pcs, -2.0 * block, 0.0)
            turned = jnp.where((rows >= pcs) & (rows < pcs + 3), 1.0, turned)
            turned = jnp.where(
                (rows >= pcs + 3) & (rows < pcs + 6), pltpu.roll(block, 3, 0), turned
            )
            turned = jnp.where(rows == pcs + 7, pltpu.roll(block, 1, 0), turned)
            turned = turned.T
            col_prof[piece * per + j] = turned.astype(BF16)
            col_inv[piece * per + j] = jnp.broadcast_to(
                -LOG2E / turned[:, pcs + 7 : pcs + 8], (BLK, BLK)
            )

    def step(s):
        rb, cb = meta[0, s], meta[1, s]
        distance = jnp.dot(col_prof[cb], row_prof[rb], preferred_element_type=F32)
        block = jnp.exp2(distance * col_inv[cb] * row_inv[rb][0:1, :])
        tile[s] = block.astype(BF16)

    slot_loop(step, total, 1, GROUP)
    ones = (lax.broadcasted_iota(jnp.int32, (PIECES, BLK), 0) == 0).astype(F32).astype(BF16)
    empty = jnp.zeros_like(ones)
    for b in range(row_blocks):
        left[0, b] = jnp.concatenate([ones, empty], axis=1)
        left[1, b] = jnp.concatenate([empty, ones], axis=1)
    acc[...] = jnp.zeros_like(acc)
    col_sums(meta, tile, left, acc, total, col_blocks)
    part[...] = jnp.sum(acc[0:col_blocks], axis=1)


def pass_kernel(over_rows, n_parts, *refs):
    meta, tile = refs[:2]
    parts = refs[2 : 2 + n_parts]
    out, stage, left, acc = refs[-4:]
    total = meta[2, 0]
    blocks = out.shape[0]
    me = meta[2, 2] if over_rows else meta[2, 3]
    fill_pieces(left, SCALE / ordered_sum(stage, parts, me))
    acc[...] = jnp.zeros_like(acc)
    (row_sums if over_rows else col_sums)(meta, tile, left, acc, total, blocks)
    out[...] = jnp.sum(acc[0:blocks], axis=1)


def pieces_of(value):
    return [v.astype(BF16) for v in split3(value)]


def last_kernel(n_row, n_col, n_land, *refs):
    meta, tile = refs[:2]
    parts = refs[2 : 2 + n_row]
    bases = refs[2 + n_row : 2 + 2 * n_row]
    keep, away, both, scaling_out, stage, scaled, pieces, acc = refs[2 + 2 * n_row :]
    cols = bases[0].shape[0]
    per = bases[0].shape[1] // BLK
    blocks = n_col * per
    total, me_row, me_col = meta[2, 0], meta[2, 2], meta[2, 3]
    scaling = SCALE / ordered_sum(stage, parts, me_row)
    scaling_out[...] = scaling
    for k in range(n_row):
        piece = shifted(me_row, k, n_row)
        for j in range(per):
            block = bases[k][:, j * BLK : (j + 1) * BLK].astype(F32)
            b = piece * per + j
            scaled[b, 0:cols] = (block * scaling_out[pl.ds(b, 1), :]).astype(BF16)
    high, mid, low = split3(scaling)
    shape = (PIECES, BLK)
    rows = lax.broadcasted_iota(jnp.int32, shape, 0)
    for b in range(scaling.shape[0]):
        value = jnp.where(
            rows == 0,
            jnp.broadcast_to(high[b : b + 1], shape),
            jnp.where(
                rows == 1,
                jnp.broadcast_to(mid[b : b + 1], shape),
                jnp.where(rows == 2, jnp.broadcast_to(low[b : b + 1], shape), 0.0),
            ),
        )
        scaled[b, cols : cols + PIECES] = value.astype(BF16)
    acc[...] = jnp.zeros_like(acc)

    def step(s):
        target = jnp.where(s < total, meta[0, s], blocks)
        sums = jnp.dot(scaled[meta[1, s]], tile[s], preferred_element_type=F32)
        acc[target] += sums[0 : cols + 8]

    slot_loop(step, total, 1, 8)
    core = lax.rem(me_col, 2)
    for q in range(n_col // 2):
        own = (2 * q + core) * per
        other = (2 * q + 1 - core) * per
        for j in range(per):
            keep[q, j] = acc[own + j, 0:cols]
            away[q, j] = acc[other + j, 0:cols].astype(BF16)
    row_part = jnp.sum(acc[0:blocks, cols : cols + 8], axis=1)
    for i, value in enumerate(pieces_of(row_part)):
        both[i * blocks : (i + 1) * blocks] = value
    for i in range(n_land):
        first = 3 * blocks + i * cols
        both[first : first + cols] = acc[meta[2, 4 + i], 0:cols].astype(BF16)


def three(ref, blocks):
    value = ref[0 : 3 * blocks].astype(F32)
    return (value[2 * blocks :] + value[blocks : 2 * blocks]) + value[0:blocks]


def pair_kernel(n_land, *refs):
    meta, keep, away, both, both_in = refs[:5]
    outs = refs[5:]
    n_chip, per, cols = keep.shape[:3]
    blocks = 2 * n_chip * per
    chip = meta[2, 3] // 2
    share = per * cols
    summed = three(both, blocks) + three(both_in, blocks)
    parts = pieces_of(summed)
    first = 3 * blocks
    lands = both[first:].astype(F32) + both_in[first:].astype(F32)
    lands = lands.astype(BF16)
    for k, out in enumerate(outs):
        to = lax.rem(chip + k, n_chip)
        for j in range(per):
            value = keep[to, j] + away[to, j].astype(F32)
            out[j * cols : (j + 1) * cols] = value.astype(BF16)
        for i, value in enumerate(parts):
            out[share + i * blocks : share + (i + 1) * blocks] = value
        out[share + first :] = lands


def gram_kernel(n_land, cols, per, *refs):
    meta = refs[0]
    gram, scaling_out, inverse, stage, land_stage = refs[-5:]
    parts = refs[1:-5]
    n = len(parts)
    chip = meta[2, 3] // 2
    blocks = scaling_out.shape[0]
    share = per * cols
    for k, part in enumerate(parts):
        stage[shifted(chip, k, n)] = three(part.at[share : share + 3 * blocks], blocks)
    inverse[...] = 1.0 / tree_sum([stage[i] for i in range(n)])
    scaling_out[...] = SCALE * inverse[...]
    for k, part in enumerate(parts):
        land_stage[shifted(chip, k, n)] = part[share + 3 * blocks :]
    total = None
    for i in range(n_land):
        summed = tree_sum(
            [land_stage[k, i * cols : (i + 1) * cols].astype(F32) for k in range(n)]
        )
        projected = summed * inverse[pl.ds(meta[2, 4 + i], 1), :]
        product = lax.dot_general(
            projected,
            projected,
            (((1,), (1,)), ((), ())),
            precision=lax.Precision.HIGHEST,
            preferred_element_type=F32,
        )
        total = product if total is None else total + product
    gram[...] = total


def ritz_kernel(n_row, cells, *refs):
    meta = refs[0]
    grams = refs[1 : 1 + n_row]
    parts = refs[1 + n_row : -3]
    scaling, out, stage = refs[-3:]
    cols = grams[0].shape[0]
    per = out.shape[1] // BLK
    me_col = meta[2, 3]
    gram = ordered_sum(stage, grams, meta[2, 2]) * (1.0 / cells)
    rows = lax.broadcasted_iota(jnp.int32, (cols, 2 * cols), 0)
    lanes = lax.broadcasted_iota(jnp.int32, (cols, 2 * cols), 1)
    unit = (lax.broadcasted_iota(jnp.int32, (cols, cols), 0)
            == lax.broadcasted_iota(jnp.int32, (cols, cols), 1)).astype(F32)
    work = jnp.concatenate([gram, unit], axis=1)
    for j in range(cols):
        root = lax.rsqrt(work[j : j + 1, j : j + 1])
        upper = work[j : j + 1, :] * root
        lower = work[:, j : j + 1] * root
        work = jnp.where(
            rows > j, work - lower * upper, jnp.where(rows == j, upper, work)
        )
    inverse = work[:, cols:]
    for j in range(per):
        summed = tree_sum([m[j * cols : (j + 1) * cols].astype(F32) for m in parts])
        projected = summed * (scaling[pl.ds(me_col * per + j, 1), :] * (1.0 / SCALE))
        out[:, j * BLK : (j + 1) * BLK] = jnp.dot(
            inverse, projected, precision=lax.Precision.HIGHEST, preferred_element_type=F32
        )


def shift(x, axis, k):
    n = lax.axis_size(axis)
    return lax.ppermute(x, axis, [(i, (i + k) % n) for i in range(n)])


def exchange(x, axis):
    return [x] + [shift(x, axis, k) for k in range(1, lax.axis_size(axis))]


def chip_shift(x, k):
    n = lax.axis_size("col") // 2
    return lax.ppermute(
        x,
        "col",
        [(2 * q + p, 2 * ((q + k) % n) + p) for q in range(n) for p in range(2)],
    )


def sibling(x):
    return lax.ppermute(x, "col", [(i, i ^ 1) for i in range(lax.axis_size("col"))])


def vec(*arrays):
    return [("vmem", a) for a in arrays]


def slot_table(block_lists, block_counts, landmarks, row_blocks, n_land):
    slots = block_lists.shape[-1]
    total = block_counts[0, 0]
    me_row, me_col = lax.axis_index("row"), lax.axis_index("col")
    own = lax.dynamic_slice_in_dim(landmarks, me_row * n_land, n_land) - me_row * row_blocks
    rows, cols = block_lists[0, 0, 0], block_lists[0, 0, 1]
    index = jnp.arange(slots, dtype=jnp.int32)
    live = index < total
    marked = live & jnp.any(rows[:, None] == own[None, :], axis=1)
    key = jnp.where(marked, 0, jnp.where(live, 1, 2)) * slots + index
    place = jnp.sum((key[None, :] < key[:, None]).astype(jnp.int32), axis=1)
    chosen = (place[:, None] == index[None, :]).astype(jnp.int32)
    lists = jnp.sum(chosen[None] * jnp.stack([rows, cols])[:, :, None], axis=1)
    scalars = jnp.concatenate(
        [
            jnp.stack([total, jnp.sum(marked.astype(jnp.int32)), me_row, me_col]),
            own,
            jnp.zeros((slots - 4 - n_land,), jnp.int32),
        ]
    )
    return jnp.concatenate([lists, scalars[None]], axis=0)


def body(profiles, cell_width, basis, block_lists, block_counts, landmarks):
    n_row, n_col = lax.axis_size("row"), lax.axis_size("col")
    n_chip = n_col // 2
    pcs, share = profiles.shape
    cols = basis.shape[0]
    per = share // BLK
    row_blocks, col_blocks = n_col * per, n_row * per
    slots = block_lists.shape[-1]
    n_land = landmarks.shape[0] // n_row

    def shape(*dims, dtype=F32):
        return jax.ShapeDtypeStruct(dims, dtype)

    (packed,) = call(
        pack_kernel,
        [shape(FEAT, share, dtype=BF16)],
        vec(profiles, cell_width.reshape(1, share)),
        [pltpu.VMEM((FEAT, share), F32)],
    )
    spread = lax.ppermute(
        packed,
        ("row", "col"),
        [((q % n_row) * n_col + q // n_row, q) for q in range(n_row * n_col)],
    )
    col_packs = exchange(packed, "row")
    row_packs = []
    for k in range(n_chip):
        pack = chip_shift(spread, k) if k else spread
        row_packs += [pack, sibling(pack)]
    bases = exchange(basis, "row")
    meta = slot_table(block_lists, block_counts, landmarks, row_blocks, n_land)
    tile, part = call(
        functools.partial(build_kernel, pcs, n_row, n_col),
        [pltpu.VMEM((slots, BLK, BLK), BF16), shape(col_blocks, BLK)],
        [("smem", meta)] + vec(*col_packs, *row_packs),
        [
            pltpu.VMEM((row_blocks, FEAT, BLK), BF16),
            pltpu.VMEM((row_blocks, 8, BLK), F32),
            pltpu.VMEM((col_blocks, BLK, FEAT), BF16),
            pltpu.VMEM((col_blocks, BLK, BLK), F32),
            pltpu.VMEM((col_blocks + 1, 8, BLK), F32),
            pltpu.VMEM((2, row_blocks, PIECES, 2 * BLK), BF16),
        ],
        flops=1 << 33,
    )
    for number in range(SWEEPS - 1):
        early = [("any", b) for b in bases[1:]] if number == 0 else []
        (part,) = call(
            functools.partial(pass_kernel, True, n_row),
            [shape(row_blocks, BLK)],
            [("smem", meta), ("keep", tile)] + vec(*exchange(part, "row")) + early,
            [
                pltpu.VMEM((n_row, col_blocks, BLK), F32),
                pltpu.VMEM((2, col_blocks, PIECES, 2 * BLK), BF16),
                pltpu.VMEM((row_blocks + 1, 8, BLK), F32),
            ],
        )
        (part,) = call(
            functools.partial(pass_kernel, False, n_col),
            [shape(col_blocks, BLK)],
            [("smem", meta), ("keep", tile)] + vec(*exchange(part, "col")),
            [
                pltpu.VMEM((n_col, row_blocks, BLK), F32),
                pltpu.VMEM((2, row_blocks, PIECES, 2 * BLK), BF16),
                pltpu.VMEM((col_blocks + 1, 8, BLK), F32),
            ],
        )
    both_rows = 3 * row_blocks + n_land * cols
    keep, away, both, col_scaling = call(
        functools.partial(last_kernel, n_row, n_col, n_land),
        [
            shape(n_chip, per, cols, BLK),
            shape(n_chip, per, cols, BLK, dtype=BF16),
            shape(both_rows, BLK, dtype=BF16),
            shape(col_blocks, BLK),
        ],
        [("smem", meta), ("keep", tile)] + vec(*exchange(part, "row"), *bases),
        [
            pltpu.VMEM((n_row, col_blocks, BLK), F32),
            pltpu.VMEM((col_blocks, cols + PIECES, BLK), BF16),
            pltpu.VMEM((8, BLK), F32),
            pltpu.VMEM((row_blocks + 1, cols + 8, BLK), F32),
        ],
    )
    sums = call(
        functools.partial(pair_kernel, n_land),
        [shape(per * cols + both_rows, BLK, dtype=BF16)] * n_chip,
        [("smem", meta)] + vec(keep, sibling(away), both, sibling(both)),
    )
    parts = [sums[0]] + [chip_shift(sums[k], k) for k in range(1, n_chip)]
    gram, row_scaling = call(
        functools.partial(gram_kernel, n_land, cols, per),
        [shape(cols, cols), shape(row_blocks, BLK)],
        [("smem", meta)] + vec(*parts),
        [
            pltpu.VMEM((row_blocks, BLK), F32),
            pltpu.VMEM((n_chip, row_blocks, BLK), F32),
            pltpu.VMEM((n_chip, n_land * cols, BLK), BF16),
        ],
    )
    (ritz,) = call(
        functools.partial(ritz_kernel, n_row, landmarks.shape[0] * BLK),
        [shape(cols, share)],
        [("smem", meta)] + vec(*exchange(gram, "row"), *parts, row_scaling),
        [pltpu.VMEM((n_row, cols, cols), F32)],
    )
    return row_scaling.reshape(-1), col_scaling.reshape(-1), ritz


def solution(mesh):
    placed = (
        P(None, ("col", "row")),
        P(("col", "row")),
        P(None, ("col", "row")),
        P("row", "col", None, None),
        P("row", "col"),
        P(),
    )
    return jax.shard_map(
        body,
        mesh=mesh,
        in_specs=placed,
        out_specs=(P("row"), P("col"), P(None, ("row", "col"))),
        check_vma=False,
    )
```

time: 153 us -> 114 us (0.75)
  starting transfers between devices: 64.8 us -> 39.5 us
  Pallas kernels: 48.2 us -> 31.4 us
  waiting for transfers between devices: 32.7 us -> 35.5 us
    ppermute x60 -> x44, starting transfers between devices: 64.1 us -> 38.9 us  [the longest x32 30.9 us: shift(): return lax.ppermute(x, axis, [(i, (i + k) % n) for i in range(n)])]
    pallas_call x10, Pallas kernels: 48.2 us -> 31.4 us  [call(): pl.pallas_call(kernel, out_shape=tuple(outs), in_specs=specs, out_specs=t...]
    ppermute x60 -> x44, waiting for transfers between devices: 32.7 us -> 35.5 us  [the longest x32 26.9 us: shift(): return lax.ppermute(x, axis, [(i, (i + k) % n) for i in range(n)])]
  transfers between devices with their start and end apart: 61 -> 45, of which waited for: 24 -> 23; matrix products, arithmetic and copies ran while one was open for 2% -> 3% of each run, Pallas kernels for 7% -> 5%
where the time goes in v2:
time: 114 us
  starting transfers between devices  39.5 us (35%)
  waiting for transfers between devices  35.5 us (31%)
  Pallas kernels  31.4 us (28%)
  local copies, waits for them, and re-layouts  3.72 us (3%)
  other arithmetic  1.84 us (2%)
  between operations  1.54 us (1%)
    pallas_call x10, Pallas kernels, call(): pl.pallas_call(kernel, out_shape=tuple(outs), in_specs=specs, out_specs=t...  31.4 us
    ppermute x32, starting transfers between devices, shift(): return lax.ppermute(x, axis, [(i, (i + k) % n) for i in range(n)])  30.9 us
    ppermute x32, waiting for transfers between devices, shift(): return lax.ppermute(x, axis, [(i, (i + k) % n) for i in range(n)])  26.9 us
    ppermute x6, waiting for transfers between devices, chip_shift(): lax.ppermute(x, 'col', [(2 * q + p, 2 * ((q + k) % n) + p) for q in range...  7.46 us
    ppermute x6, starting transfers between devices, chip_shift(): lax.ppermute(x, 'col', [(2 * q + p, 2 * ((q + k) % n) + p) for q in range...  6.89 us
  transfers between devices with their start and end apart: 45, of which 23 were waited for; matrix products, arithmetic and copies ran while one was open for 3% of the time, Pallas kernels for 5%

profile of v2, /device:TPU:0, one launch (start us, length us, event | category | flops | bytes accessed | tf_op | source)
XLA Modules:
  0.0 113.5 jit_solution(2999332623606735145)
XLA Ops:
  2.8 6.9 %collective-permute-start.2 = (bf16[64,512]{1,0:T(8,128)(2,1)S(1)}, bf16[64,512]{1,0:T(8,128)(2,1)S(1)}, u32[]{:S(2)}, u32[]{:S(2)}) collective-permute-start(bf16[64,512]{1,0:T(8,128)(2,1)S(1)} %shard_map.85.refs_1_), channel_id=1, source_target_pairs={{0,24},{8,0},{16,8},{24,16},{1,25},{9,1},{17,9},{25,17},{2,26},{10... | collective-permute-start | bytes 196616 | tf_op jit(solution)/shard_map/ppermute | solution.py:371
  13.7 3.3 %collective-permute-start.9 = (bf16[64,512]{1,0:T(8,128)(2,1)S(1)}, bf16[64,512]{1,0:T(8,128)(2,1)S(1)}, u32[]{:S(2)}, u32[]{:S(2)}) collective-permute-start(bf16[64,512]{1,0:T(8,128)(2,1)S(1)} %collective-permute-done.3.refs_5_), channel_id=1, source_target_pairs={{0,6},{1,7},{2,0},{3,1},{4,2},{5,3},{6,4},{7,5},{8,14},{9,15},{10,... | collective-permute-start | bytes 196616 | tf_op jit(solution)/shard_map/ppermute | solution.py:380
  17.7 1.6 %collective-permute-start = (bf16[64,512]{1,0:T(8,128)(2,1)S(1)}, bf16[64,512]{1,0:T(8,128)(2,1)S(1)}, u32[]{:S(2)}, u32[]{:S(2)}) collective-permute-start(bf16[64,512]{1,0:T(8,128)(2,1)S(1)} %shard_map.85.refs_1_), channel_id=1, source_target_pairs={{0,8},{8,16},{16,24},{24,0},{1,9},{9,17},{17,25},{25,1},{2,10},{10... | collective-permute-start | bytes 196616 | tf_op jit(solution)/shard_map/ppermute | solution.py:371
  22.2 2.0 %collective-permute-done.refs_2_ = bf16[64,512]{1,0:T(8,128)(2,1)S(1)} collective-permute-done((bf16[64,512]{1,0:T(8,128)(2,1)S(1)}, bf16[64,512]{1,0:T(8,128)(2,1)S(1)}, u32[]{:S(2)}, u32[]{:S(2)}) %collective-permute-start) | collective-permute-done | bytes 65568 | tf_op jit(solution)/shard_map/ppermute | solution.py:371
  24.8 2.7 %collective-permute-start.14 = (bf16[64,512]{1,0:T(8,128)(2,1)}, bf16[64,512]{1,0:T(8,128)(2,1)S(1)}, u32[]{:S(2)}, u32[]{:S(2)}) collective-permute-start(bf16[64,512]{1,0:T(8,128)(2,1)} %refs_6_.1), channel_id=1, source_target_pairs={{0,8},{8,16},{16,24},{24,0},{1,9},{9,17},{17,25},{25,1},{2,10},{10... | collective-permute-start | bytes 196616 | tf_op jit(solution)/shard_map/ppermute | solution.py:371
  28.7 6.0 %shard_map.86 = (bf16[128,128,128]{2,1,0:T(8,128)(2,1)S(1)}, f32[16,128]{1,0:T(8,128)S(1)}) custom-call(s32[3,128]{1,0:T(4,128)S(1)} %pad_add_fusion.refs_0_, bf16[64,512]{1,0:T(8,128)(2,1)S(1)} %shard_map.85.refs_1_, bf16[64,512]{1,0:T(8,128)(2,1)S(1)} %collective-permute-done.refs_2_, bf16[64,512]{1,0:T(8,128)(2,1)S(1)} %collective-permute-done.1.refs_3_, ...), custom_call_target="tpu_custom_call" | custom-call | flops 8589934592 | bytes 1048576 | tf_op jit(solution)/shard_map/pallas_call | solution.py:51
  34.8 1.9 %collective-permute-start.11 = (f32[16,128]{1,0:T(8,128)S(1)}, f32[16,128]{1,0:T(8,128)S(1)}, u32[]{:S(2)}, u32[]{:S(2)}) collective-permute-start(f32[16,128]{1,0:T(8,128)S(1)} %get-tuple-element.16.refs_2_), channel_id=1, source_target_pairs={{0,8},{8,16},{16,24},{24,0},{1,9},{9,17},{17,25},{25,1},{2,10},{10... | collective-permute-start | bytes 24584 | tf_op jit(solution)/shard_map/ppermute | solution.py:371
  36.7 1.6 %collective-permute-done.13.refs_5_ = f32[16,128]{1,0:T(8,128)S(1)} collective-permute-done((f32[16,128]{1,0:T(8,128)S(1)}, f32[16,128]{1,0:T(8,128)S(1)}, u32[]{:S(2)}, u32[]{:S(2)}) %collective-permute-start.13) | collective-permute-done | bytes 8224 | tf_op jit(solution)/shard_map/ppermute | solution.py:371
  39.3 1.5 %collective-permute-done.11.refs_3_ = f32[16,128]{1,0:T(8,128)S(1)} collective-permute-done((f32[16,128]{1,0:T(8,128)S(1)}, f32[16,128]{1,0:T(8,128)S(1)}, u32[]{:S(2)}, u32[]{:S(2)}) %collective-permute-start.11) | collective-permute-done | bytes 8224 | tf_op jit(solution)/shard_map/ppermute | solution.py:371
  40.8 2.5 %shard_map.87.refs_2_ = f32[32,128]{1,0:T(8,128)S(1)} custom-call(s32[3,128]{1,0:T(4,128)S(1)} %pad_add_fusion.refs_0_, bf16[128,128,128]{2,1,0:T(8,128)(2,1)S(1)} %get-tuple-element.15.refs_1_, f32[16,128]{1,0:T(8,128)S(1)} %get-tuple-element.16.refs_2_, f32[16,128]{1,0:T(8,128)S(1)} %collective-permute-done.11.refs_3_, ...), custom_call_target="tpu_custom_call" | custom-call | flops 16777216 | bytes 1048576 | tf_op jit(solution)/shard_map/pallas_call | solution.py:51
  44.3 1.6 %collective-permute-start.21 = (f32[32,128]{1,0:T(8,128)S(1)}, f32[32,128]{1,0:T(8,128)S(1)}, u32[]{:S(2)}, u32[]{:S(2)}) collective-permute-start(f32[32,128]{1,0:T(8,128)S(1)} %shard_map.87.refs_2_), channel_id=1, source_target_pairs={{0,5},{1,6},{2,7},{3,0},{4,1},{5,2},{6,3},{7,4},{8,13},{9,14},{10,... | collective-permute-start | bytes 49160 | tf_op jit(solution)/shard_map/ppermute | solution.py:371
  48.1 1.5 %collective-permute-done.20.refs_6_ = f32[32,128]{1,0:T(8,128)S(1)} collective-permute-done((f32[32,128]{1,0:T(8,128)S(1)}, f32[32,128]{1,0:T(8,128)S(1)}, u32[]{:S(2)}, u32[]{:S(2)}) %collective-permute-start.20) | collective-permute-done | bytes 16416 | tf_op jit(solution)/shard_map/ppermute | solution.py:371
  49.7 2.7 %collective-permute-done.18.refs_4_ = f32[32,128]{1,0:T(8,128)S(1)} collective-permute-done((f32[32,128]{1,0:T(8,128)S(1)}, f32[32,128]{1,0:T(8,128)S(1)}, u32[]{:S(2)}, u32[]{:S(2)}) %collective-permute-start.18) | collective-permute-done | bytes 16416 | tf_op jit(solution)/shard_map/ppermute | solution.py:371
  52.4 3.1 %shard_map.88.refs_2_ = f32[16,128]{1,0:T(8,128)S(1)} custom-call(s32[3,128]{1,0:T(4,128)S(1)} %pad_add_fusion.refs_0_, bf16[128,128,128]{2,1,0:T(8,128)(2,1)S(1)} %get-tuple-element.15.refs_1_, f32[32,128]{1,0:T(8,128)S(1)} %shard_map.87.refs_2_, f32[32,128]{1,0:T(8,128)S(1)} %collective-permute-done.17.refs_3_, ...), custom_call_target="tpu_custom_call" | custom-call | flops 16777216 | bytes 1048576 | tf_op jit(solution)/shard_map/pallas_call | solution.py:51
  55.6 1.9 %collective-permute-start.24 = (f32[16,128]{1,0:T(8,128)S(1)}, f32[16,128]{1,0:T(8,128)S(1)}, u32[]{:S(2)}, u32[]{:S(2)}) collective-permute-start(f32[16,128]{1,0:T(8,128)S(1)} %shard_map.88.refs_2_), channel_id=1, source_target_pairs={{0,8},{8,16},{16,24},{24,0},{1,9},{9,17},{17,25},{25,1},{2,10},{10... | collective-permute-start | bytes 24584 | tf_op jit(solution)/shard_map/ppermute | solution.py:371
  57.5 1.6 %collective-permute-done.26.refs_5_ = f32[16,128]{1,0:T(8,128)S(1)} collective-permute-done((f32[16,128]{1,0:T(8,128)S(1)}, f32[16,128]{1,0:T(8,128)S(1)}, u32[]{:S(2)}, u32[]{:S(2)}) %collective-permute-start.26) | collective-permute-done | bytes 8224 | tf_op jit(solution)/shard_map/ppermute | solution.py:371
  60.1 1.5 %collective-permute-done.24.refs_3_ = f32[16,128]{1,0:T(8,128)S(1)} collective-permute-done((f32[16,128]{1,0:T(8,128)S(1)}, f32[16,128]{1,0:T(8,128)S(1)}, u32[]{:S(2)}, u32[]{:S(2)}) %collective-permute-start.24) | collective-permute-done | bytes 8224 | tf_op jit(solution)/shard_map/ppermute | solution.py:371
  61.6 2.5 %shard_map.89.refs_2_ = f32[32,128]{1,0:T(8,128)S(1)} custom-call(s32[3,128]{1,0:T(4,128)S(1)} %pad_add_fusion.refs_0_, bf16[128,128,128]{2,1,0:T(8,128)(2,1)S(1)} %get-tuple-element.15.refs_1_, f32[16,128]{1,0:T(8,128)S(1)} %shard_map.88.refs_2_, f32[16,128]{1,0:T(8,128)S(1)} %collective-permute-done.24.refs_3_, ...), custom_call_target="tpu_custom_call" | custom-call | flops 16777216 | bytes 1048576 | tf_op jit(solution)/shard_map/pallas_call | solution.py:51
  64.8 1.6 %collective-permute-start.30 = (f32[32,128]{1,0:T(8,128)S(1)}, f32[32,128]{1,0:T(8,128)S(1)}, u32[]{:S(2)}, u32[]{:S(2)}) collective-permute-start(f32[32,128]{1,0:T(8,128)S(1)} %shard_map.89.refs_2_), channel_id=1, source_target_pairs={{0,4},{1,5},{2,6},{3,7},{4,0},{5,1},{6,2},{7,3},{8,12},{9,13},{10,... | collective-permute-start | bytes 49160 | tf_op jit(solution)/shard_map/ppermute | solution.py:371
  66.5 2.4 %collective-permute-start.28 = (f32[32,128]{1,0:T(8,128)S(1)}, f32[32,128]{1,0:T(8,128)S(1)}, u32[]{:S(2)}, u32[]{:S(2)}) collective-permute-start(f32[32,128]{1,0:T(8,128)S(1)} %shard_map.89.refs_2_), channel_id=1, source_target_pairs={{0,2},{1,3},{2,4},{3,5},{4,6},{5,7},{6,0},{7,1},{8,10},{9,11},{10,... | collective-permute-start | bytes 49160 | tf_op jit(solution)/shard_map/ppermute | solution.py:371
  69.5 2.5 %collective-permute-done.28.refs_4_ = f32[32,128]{1,0:T(8,128)S(1)} collective-permute-done((f32[32,128]{1,0:T(8,128)S(1)}, f32[32,128]{1,0:T(8,128)S(1)}, u32[]{:S(2)}, u32[]{:S(2)}) %collective-permute-start.28) | collective-permute-done | bytes 16416 | tf_op jit(solution)/shard_map/ppermute | solution.py:371
  73.0 3.1 %shard_map.90.refs_2_ = f32[16,128]{1,0:T(8,128)S(1)} custom-call(s32[3,128]{1,0:T(4,128)S(1)} %pad_add_fusion.refs_0_, bf16[128,128,128]{2,1,0:T(8,128)(2,1)S(1)} %get-tuple-element.15.refs_1_, f32[32,128]{1,0:T(8,128)S(1)} %shard_map.89.refs_2_, f32[32,128]{1,0:T(8,128)S(1)} %collective-permute-done.27.refs_3_, ...), custom_call_target="tpu_custom_call" | custom-call | flops 16777216 | bytes 1048576 | tf_op jit(solution)/shard_map/pallas_call | solution.py:51
  76.2 1.9 %collective-permute-start.34 = (f32[16,128]{1,0:T(8,128)S(1)}, f32[16,128]{1,0:T(8,128)S(1)}, u32[]{:S(2)}, u32[]{:S(2)}) collective-permute-start(f32[16,128]{1,0:T(8,128)S(1)} %shard_map.90.refs_2_), channel_id=1, source_target_pairs={{0,8},{8,16},{16,24},{24,0},{1,9},{9,17},{17,25},{25,1},{2,10},{10... | collective-permute-start | bytes 24584 | tf_op jit(solution)/shard_map/ppermute | solution.py:371
  78.2 1.6 %collective-permute-done.36.refs_5_ = f32[16,128]{1,0:T(8,128)S(1)} collective-permute-done((f32[16,128]{1,0:T(8,128)S(1)}, f32[16,128]{1,0:T(8,128)S(1)}, u32[]{:S(2)}, u32[]{:S(2)}) %collective-permute-start.36) | collective-permute-done | bytes 8224 | tf_op jit(solution)/shard_map/ppermute | solution.py:371
  80.8 1.5 %collective-permute-done.34.refs_3_ = f32[16,128]{1,0:T(8,128)S(1)} collective-permute-done((f32[16,128]{1,0:T(8,128)S(1)}, f32[16,128]{1,0:T(8,128)S(1)}, u32[]{:S(2)}, u32[]{:S(2)}) %collective-permute-start.34) | collective-permute-done | bytes 8224 | tf_op jit(solution)/shard_map/ppermute | solution.py:371
  82.2 5.3 %shard_map.91 = (f32[4,4,64,128]{3,2,1,0:T(8,128)S(1)}, bf16[4,4,64,128]{3,2,1,0:T(8,128)(2,1)S(1)}, bf16[224,128]{1,0:T(8,128)(2,1)S(1)}, f32[16,128]{1,0:T(8,128)}) custom-call(s32[3,128]{1,0:T(4,128)S(1)} %pad_add_fusion.refs_0_, bf16[128,128,128]{2,1,0:T(8,128)(2,1)S(1)} %get-tuple-element.15.refs_1_, f32[16,128]{1,0:T(8,128)S(1)} %shard_map.90.refs_2_, ...), custom_call_target="tpu_custom_call" | custom-call | flops 16777216 | bytes 1048576 | tf_op jit(solution)/shard_map/pallas_call | solution.py:51
  90.0 2.8 %collective-permute-start.41 = (bf16[480,128]{1,0:T(8,128)(2,1)S(1)}, bf16[480,128]{1,0:T(8,128)(2,1)S(1)}, u32[]{:S(2)}, u32[]{:S(2)}) collective-permute-start(bf16[480,128]{1,0:T(8,128)(2,1)S(1)} %get-tuple-element.23), channel_id=1, source_target_pairs={{0,6},{1,7},{2,0},{3,1},{4,2},{5,3},{6,4},{7,5},{8,14},{9,15},{10,... | collective-permute-start | bytes 368648 | tf_op jit(solution)/shard_map/ppermute | solution.py:380
  92.8 4.2 %collective-permute-done.39.refs_2_.refs_6_ = bf16[480,128]{1,0:T(8,128)(2,1)S(1)} collective-permute-done((bf16[480,128]{1,0:T(8,128)(2,1)S(1)}, bf16[480,128]{1,0:T(8,128)(2,1)S(1)}, u32[]{:S(2)}, u32[]{:S(2)}) %collective-permute-start.39) | collective-permute-done | bytes 122912 | tf_op jit(solution)/shard_map/ppermute | solution.py:380
  99.5 2.0 %collective-permute-start.42 = (f32[64,64]{1,0:T(8,128)S(1)}, f32[64,64]{1,0:T(8,128)S(1)}, u32[]{:S(2)}, u32[]{:S(2)}) collective-permute-start(f32[64,64]{1,0:T(8,128)S(1)} %get-tuple-element.26.refs_1_), channel_id=1, source_target_pairs={{0,8},{8,16},{16,24},{24,0},{1,9},{9,17},{17,25},{25,1},{2,10},{10... | collective-permute-start | bytes 49160 | tf_op jit(solution)/shard_map/ppermute | solution.py:371
  101.5 1.7 %collective-permute-done.44.refs_4_ = f32[64,64]{1,0:T(8,128)S(1)} collective-permute-done((f32[64,64]{1,0:T(8,128)S(1)}, f32[64,64]{1,0:T(8,128)S(1)}, u32[]{:S(2)}, u32[]{:S(2)}) %collective-permute-start.44) | collective-permute-done | bytes 16416 | tf_op jit(solution)/shard_map/ppermute | solution.py:371
  104.3 1.6 %collective-permute-done.42.refs_2_ = f32[64,64]{1,0:T(8,128)S(1)} collective-permute-done((f32[64,64]{1,0:T(8,128)S(1)}, f32[64,64]{1,0:T(8,128)S(1)}, u32[]{:S(2)}, u32[]{:S(2)}) %collective-permute-start.42) | collective-permute-done | bytes 16416 | tf_op jit(solution)/shard_map/ppermute | solution.py:371
  106.6 6.9 %shard_map.94 = f32[64,512]{1,0:T(8,128)} custom-call(s32[3,128]{1,0:T(4,128)S(1)} %pad_add_fusion.refs_0_, f32[64,64]{1,0:T(8,128)S(1)} %get-tuple-element.26.refs_1_, f32[64,64]{1,0:T(8,128)S(1)} %collective-permute-done.42.refs_2_, f32[64,64]{1,0:T(8,128)S(1)} %collective-permute-done.43.refs_3_, f32[64,64]{1,0:T(8,128)S(1)} %collective-permute-done.44.refs_4_, ...), custom_call_target="tpu_custom_call" | custom-call | flops 16777216 | bytes 1048576 | tf_op jit(solution)/shard_map/pallas_call | solution.py:51
  (86 shorter events, 26.3 us)
Async XLA Ops:
  2.2 11.5 %collective-permute-start.3 = (bf16[64,512]{1,0:T(8,128)(2,1)S(1)}, bf16[64,512]{1,0:T(8,128)(2,1)S(1)}, u32[]{:S(2)}, u32[]{:S(2)}) collective-permute-start(bf16[64,512]{1,0:T(8,128)(2,1)S(1)} %shard_map.85.refs_1_), channel_id=1, source_target_pairs={{0,0},{8,1},{16,2},{24,3},{1,4},{9,5},{17,6},{25,7},{2,8},{10,9},{... | collective-permute-start | bytes 196616 | tf_op jit(solution)/shard_map/ppermute | solution.py:437
  2.8 14.9 %collective-permute-start.2 = (bf16[64,512]{1,0:T(8,128)(2,1)S(1)}, bf16[64,512]{1,0:T(8,128)(2,1)S(1)}, u32[]{:S(2)}, u32[]{:S(2)}) collective-permute-start(bf16[64,512]{1,0:T(8,128)(2,1)S(1)} %shard_map.85.refs_1_), channel_id=1, source_target_pairs={{0,24},{8,0},{16,8},{24,16},{1,25},{9,1},{17,9},{25,17},{2,26},{10... | collective-permute-start | bytes 196616 | tf_op jit(solution)/shard_map/ppermute | solution.py:371
  9.8 9.5 %collective-permute-start.1 = (bf16[64,512]{1,0:T(8,128)(2,1)S(1)}, bf16[64,512]{1,0:T(8,128)(2,1)S(1)}, u32[]{:S(2)}, u32[]{:S(2)}) collective-permute-start(bf16[64,512]{1,0:T(8,128)(2,1)S(1)} %shard_map.85.refs_1_), channel_id=1, source_target_pairs={{0,16},{8,24},{16,0},{24,8},{1,17},{9,25},{17,1},{25,9},{2,18},{10... | collective-permute-start | bytes 196616 | tf_op jit(solution)/shard_map/ppermute | solution.py:371
  13.7 5.6 %collective-permute-start.9 = (bf16[64,512]{1,0:T(8,128)(2,1)S(1)}, bf16[64,512]{1,0:T(8,128)(2,1)S(1)}, u32[]{:S(2)}, u32[]{:S(2)}) collective-permute-start(bf16[64,512]{1,0:T(8,128)(2,1)S(1)} %collective-permute-done.3.refs_5_), channel_id=1, source_target_pairs={{0,6},{1,7},{2,0},{3,1},{4,2},{5,3},{6,4},{7,5},{8,14},{9,15},{10,... | collective-permute-start | bytes 196616 | tf_op jit(solution)/shard_map/ppermute | solution.py:380
  17.0 4.3 %collective-permute-start.7 = (bf16[64,512]{1,0:T(8,128)(2,1)S(1)}, bf16[64,512]{1,0:T(8,128)(2,1)S(1)}, u32[]{:S(2)}, u32[]{:S(2)}) collective-permute-start(bf16[64,512]{1,0:T(8,128)(2,1)S(1)} %collective-permute-done.3.refs_5_), channel_id=1, source_target_pairs={{0,4},{1,5},{2,6},{3,7},{4,0},{5,1},{6,2},{7,3},{8,12},{9,13},{10,... | collective-permute-start | bytes 196616 | tf_op jit(solution)/shard_map/ppermute | solution.py:380
  17.0 5.2 %collective-permute-start.5 = (bf16[64,512]{1,0:T(8,128)(2,1)S(1)}, bf16[64,512]{1,0:T(8,128)(2,1)S(1)}, u32[]{:S(2)}, u32[]{:S(2)}) collective-permute-start(bf16[64,512]{1,0:T(8,128)(2,1)S(1)} %collective-permute-done.3.refs_5_), channel_id=1, source_target_pairs={{0,2},{1,3},{2,4},{3,5},{4,6},{5,7},{6,0},{7,1},{8,10},{9,11},{10,... | collective-permute-start | bytes 196616 | tf_op jit(solution)/shard_map/ppermute | solution.py:380
  17.7 6.4 %collective-permute-start = (bf16[64,512]{1,0:T(8,128)(2,1)S(1)}, bf16[64,512]{1,0:T(8,128)(2,1)S(1)}, u32[]{:S(2)}, u32[]{:S(2)}) collective-permute-start(bf16[64,512]{1,0:T(8,128)(2,1)S(1)} %shard_map.85.refs_1_), channel_id=1, source_target_pairs={{0,8},{8,16},{16,24},{24,0},{1,9},{9,17},{17,25},{25,1},{2,10},{10... | collective-permute-start | bytes 196616 | tf_op jit(solution)/shard_map/ppermute | solution.py:371
  19.3 5.5 %collective-permute-start.4 = (bf16[64,512]{1,0:T(8,128)(2,1)S(1)}, bf16[64,512]{1,0:T(8,128)(2,1)S(1)}, u32[]{:S(2)}, u32[]{:S(2)}) collective-permute-start(bf16[64,512]{1,0:T(8,128)(2,1)S(1)} %collective-permute-done.3.refs_5_), channel_id=1, source_target_pairs={{0,1},{1,0},{2,3},{3,2},{4,5},{5,4},{6,7},{7,6},{8,9},{9,8},{10,11... | collective-permute-start | bytes 196616 | tf_op jit(solution)/shard_map/ppermute | solution.py:388
  19.3 8.2 %collective-permute-start.10 = (bf16[64,512]{1,0:T(8,128)(2,1)S(1)}, bf16[64,512]{1,0:T(8,128)(2,1)S(1)}, u32[]{:S(2)}, u32[]{:S(2)}) collective-permute-start(bf16[64,512]{1,0:T(8,128)(2,1)S(1)} %collective-permute-done.9.refs_11_), channel_id=1, source_target_pairs={{0,1},{1,0},{2,3},{3,2},{4,5},{5,4},{6,7},{7,6},{8,9},{9,8},{10,11... | collective-permute-start | bytes 196616 | tf_op jit(solution)/shard_map/ppermute | solution.py:388
  21.2 7.4 %collective-permute-start.8 = (bf16[64,512]{1,0:T(8,128)(2,1)S(1)}, bf16[64,512]{1,0:T(8,128)(2,1)S(1)}, u32[]{:S(2)}, u32[]{:S(2)}) collective-permute-start(bf16[64,512]{1,0:T(8,128)(2,1)S(1)} %collective-permute-done.7.refs_9_), channel_id=1, source_target_pairs={{0,1},{1,0},{2,3},{3,2},{4,5},{5,4},{6,7},{7,6},{8,9},{9,8},{10,11... | collective-permute-start | bytes 196616 | tf_op jit(solution)/shard_map/ppermute | solution.py:388
  22.1 6.5 %collective-permute-start.6 = (bf16[64,512]{1,0:T(8,128)(2,1)S(1)}, bf16[64,512]{1,0:T(8,128)(2,1)S(1)}, u32[]{:S(2)}, u32[]{:S(2)}) collective-permute-start(bf16[64,512]{1,0:T(8,128)(2,1)S(1)} %collective-permute-done.5.refs_7_), channel_id=1, source_target_pairs={{0,1},{1,0},{2,3},{3,2},{4,5},{5,4},{6,7},{7,6},{8,9},{9,8},{10,11... | collective-permute-start | bytes 196616 | tf_op jit(solution)/shard_map/ppermute | solution.py:388
  24.2 10.7 %collective-permute-start.15 = (bf16[64,512]{1,0:T(8,128)(2,1)}, bf16[64,512]{1,0:T(8,128)(2,1)S(1)}, u32[]{:S(2)}, u32[]{:S(2)}) collective-permute-start(bf16[64,512]{1,0:T(8,128)(2,1)} %refs_6_.1), channel_id=1, source_target_pairs={{0,16},{8,24},{16,0},{24,8},{1,17},{9,25},{17,1},{25,9},{2,18},{10... | collective-permute-start | bytes 196616 | tf_op jit(solution)/shard_map/ppermute | solution.py:371
  24.8 11.9 %collective-permute-start.14 = (bf16[64,512]{1,0:T(8,128)(2,1)}, bf16[64,512]{1,0:T(8,128)(2,1)S(1)}, u32[]{:S(2)}, u32[]{:S(2)}) collective-permute-start(bf16[64,512]{1,0:T(8,128)(2,1)} %refs_6_.1), channel_id=1, source_target_pairs={{0,8},{8,16},{16,24},{24,0},{1,9},{9,17},{17,25},{25,1},{2,10},{10... | collective-permute-start | bytes 196616 | tf_op jit(solution)/shard_map/ppermute | solution.py:371
  27.6 9.2 %collective-permute-start.16 = (bf16[64,512]{1,0:T(8,128)(2,1)}, bf16[64,512]{1,0:T(8,128)(2,1)S(1)}, u32[]{:S(2)}, u32[]{:S(2)}) collective-permute-start(bf16[64,512]{1,0:T(8,128)(2,1)} %refs_6_.1), channel_id=1, source_target_pairs={{0,24},{8,0},{16,8},{24,16},{1,25},{9,1},{17,9},{25,17},{2,26},{10... | collective-permute-start | bytes 196616 | tf_op jit(solution)/shard_map/ppermute | solution.py:371
  34.7 4.6 %collective-permute-start.12 = (f32[16,128]{1,0:T(8,128)S(1)}, f32[16,128]{1,0:T(8,128)S(1)}, u32[]{:S(2)}, u32[]{:S(2)}) collective-permute-start(f32[16,128]{1,0:T(8,128)S(1)} %get-tuple-element.16.refs_2_), channel_id=1, source_target_pairs={{0,16},{8,24},{16,0},{24,8},{1,17},{9,25},{17,1},{25,9},{2,18},{10... | collective-permute-start | bytes 24584 | tf_op jit(solution)/shard_map/ppermute | solution.py:371
  34.8 6.0 %collective-permute-start.11 = (f32[16,128]{1,0:T(8,128)S(1)}, f32[16,128]{1,0:T(8,128)S(1)}, u32[]{:S(2)}, u32[]{:S(2)}) collective-permute-start(f32[16,128]{1,0:T(8,128)S(1)} %get-tuple-element.16.refs_2_), channel_id=1, source_target_pairs={{0,8},{8,16},{16,24},{24,0},{1,9},{9,17},{17,25},{25,1},{2,10},{10... | collective-permute-start | bytes 24584 | tf_op jit(solution)/shard_map/ppermute | solution.py:371
  43.3 4.3 %collective-permute-start.23 = (f32[32,128]{1,0:T(8,128)S(1)}, f32[32,128]{1,0:T(8,128)S(1)}, u32[]{:S(2)}, u32[]{:S(2)}) collective-permute-start(f32[32,128]{1,0:T(8,128)S(1)} %shard_map.87.refs_2_), channel_id=1, source_target_pairs={{0,7},{1,0},{2,1},{3,2},{4,3},{5,4},{6,5},{7,6},{8,15},{9,8},{10,9... | collective-permute-start | bytes 49160 | tf_op jit(solution)/shard_map/ppermute | solution.py:371
  43.4 4.7 %collective-permute-start.22 = (f32[32,128]{1,0:T(8,128)S(1)}, f32[32,128]{1,0:T(8,128)S(1)}, u32[]{:S(2)}, u32[]{:S(2)}) collective-permute-start(f32[32,128]{1,0:T(8,128)S(1)} %shard_map.87.refs_2_), channel_id=1, source_target_pairs={{0,6},{1,7},{2,0},{3,1},{4,2},{5,3},{6,4},{7,5},{8,14},{9,15},{10,... | collective-permute-start | bytes 49160 | tf_op jit(solution)/shard_map/ppermute | solution.py:371
  47.6 4.8 %collective-permute-start.18 = (f32[32,128]{1,0:T(8,128)S(1)}, f32[32,128]{1,0:T(8,128)S(1)}, u32[]{:S(2)}, u32[]{:S(2)}) collective-permute-start(f32[32,128]{1,0:T(8,128)S(1)} %shard_map.87.refs_2_), channel_id=1, source_target_pairs={{0,2},{1,3},{2,4},{3,5},{4,6},{5,7},{6,0},{7,1},{8,10},{9,11},{10,... | collective-permute-start | bytes 49160 | tf_op jit(solution)/shard_map/ppermute | solution.py:371
  48.1 4.2 %collective-permute-start.17 = (f32[32,128]{1,0:T(8,128)S(1)}, f32[32,128]{1,0:T(8,128)S(1)}, u32[]{:S(2)}, u32[]{:S(2)}) collective-permute-start(f32[32,128]{1,0:T(8,128)S(1)} %shard_map.87.refs_2_), channel_id=1, source_target_pairs={{0,1},{1,2},{2,3},{3,4},{4,5},{5,6},{6,7},{7,0},{8,9},{9,10},{10,1... | collective-permute-start | bytes 49160 | tf_op jit(solution)/shard_map/ppermute | solution.py:371
  55.5 4.6 %collective-permute-start.25 = (f32[16,128]{1,0:T(8,128)S(1)}, f32[16,128]{1,0:T(8,128)S(1)}, u32[]{:S(2)}, u32[]{:S(2)}) collective-permute-start(f32[16,128]{1,0:T(8,128)S(1)} %shard_map.88.refs_2_), channel_id=1, source_target_pairs={{0,16},{8,24},{16,0},{24,8},{1,17},{9,25},{17,1},{25,9},{2,18},{10... | collective-permute-start | bytes 24584 | tf_op jit(solution)/shard_map/ppermute | solution.py:371
  55.6 6.0 %collective-permute-start.24 = (f32[16,128]{1,0:T(8,128)S(1)}, f32[16,128]{1,0:T(8,128)S(1)}, u32[]{:S(2)}, u32[]{:S(2)}) collective-permute-start(f32[16,128]{1,0:T(8,128)S(1)} %shard_map.88.refs_2_), channel_id=1, source_target_pairs={{0,8},{8,16},{16,24},{24,0},{1,9},{9,17},{17,25},{25,1},{2,10},{10... | collective-permute-start | bytes 24584 | tf_op jit(solution)/shard_map/ppermute | solution.py:371
  64.2 4.7 %collective-permute-start.32 = (f32[32,128]{1,0:T(8,128)S(1)}, f32[32,128]{1,0:T(8,128)S(1)}, u32[]{:S(2)}, u32[]{:S(2)}) collective-permute-start(f32[32,128]{1,0:T(8,128)S(1)} %shard_map.89.refs_2_), channel_id=1, source_target_pairs={{0,6},{1,7},{2,0},{3,1},{4,2},{5,3},{6,4},{7,5},{8,14},{9,15},{10,... | collective-permute-start | bytes 49160 | tf_op jit(solution)/shard_map/ppermute | solution.py:371
  64.3 4.7 %collective-permute-start.31 = (f32[32,128]{1,0:T(8,128)S(1)}, f32[32,128]{1,0:T(8,128)S(1)}, u32[]{:S(2)}, u32[]{:S(2)}) collective-permute-start(f32[32,128]{1,0:T(8,128)S(1)} %shard_map.89.refs_2_), channel_id=1, source_target_pairs={{0,5},{1,6},{2,7},{3,0},{4,1},{5,2},{6,3},{7,4},{8,13},{9,14},{10,... | collective-permute-start | bytes 49160 | tf_op jit(solution)/shard_map/ppermute | solution.py:371
  66.5 5.5 %collective-permute-start.28 = (f32[32,128]{1,0:T(8,128)S(1)}, f32[32,128]{1,0:T(8,128)S(1)}, u32[]{:S(2)}, u32[]{:S(2)}) collective-permute-start(f32[32,128]{1,0:T(8,128)S(1)} %shard_map.89.refs_2_), channel_id=1, source_target_pairs={{0,2},{1,3},{2,4},{3,5},{4,6},{5,7},{6,0},{7,1},{8,10},{9,11},{10,... | collective-permute-start | bytes 49160 | tf_op jit(solution)/shard_map/ppermute | solution.py:371
  76.2 4.6 %collective-permute-start.35 = (f32[16,128]{1,0:T(8,128)S(1)}, f32[16,128]{1,0:T(8,128)S(1)}, u32[]{:S(2)}, u32[]{:S(2)}) collective-permute-start(f32[16,128]{1,0:T(8,128)S(1)} %shard_map.90.refs_2_), channel_id=1, source_target_pairs={{0,16},{8,24},{16,0},{24,8},{1,17},{9,25},{17,1},{25,9},{2,18},{10... | collective-permute-start | bytes 24584 | tf_op jit(solution)/shard_map/ppermute | solution.py:371
  76.2 6.0 %collective-permute-start.34 = (f32[16,128]{1,0:T(8,128)S(1)}, f32[16,128]{1,0:T(8,128)S(1)}, u32[]{:S(2)}, u32[]{:S(2)}) collective-permute-start(f32[16,128]{1,0:T(8,128)S(1)} %shard_map.90.refs_2_), channel_id=1, source_target_pairs={{0,8},{8,16},{16,24},{24,0},{1,9},{9,17},{17,25},{25,1},{2,10},{10... | collective-permute-start | bytes 24584 | tf_op jit(solution)/shard_map/ppermute | solution.py:371
  89.8 7.2 %collective-permute-start.39 = (bf16[480,128]{1,0:T(8,128)(2,1)S(1)}, bf16[480,128]{1,0:T(8,128)(2,1)S(1)}, u32[]{:S(2)}, u32[]{:S(2)}) collective-permute-start(bf16[480,128]{1,0:T(8,128)(2,1)S(1)} %get-tuple-element.21), channel_id=1, source_target_pairs={{0,2},{1,3},{2,4},{3,5},{4,6},{5,7},{6,0},{7,1},{8,10},{9,11},{10,... | collective-permute-start | bytes 368648 | tf_op jit(solution)/shard_map/ppermute | solution.py:380
  89.9 8.1 %collective-permute-start.40 = (bf16[480,128]{1,0:T(8,128)(2,1)S(1)}, bf16[480,128]{1,0:T(8,128)(2,1)S(1)}, u32[]{:S(2)}, u32[]{:S(2)}) collective-permute-start(bf16[480,128]{1,0:T(8,128)(2,1)S(1)} %get-tuple-element.22), channel_id=1, source_target_pairs={{0,4},{1,5},{2,6},{3,7},{4,0},{5,1},{6,2},{7,3},{8,12},{9,13},{10,... | collective-permute-start | bytes 368648 | tf_op jit(solution)/shard_map/ppermute | solution.py:380
  90.0 8.0 %collective-permute-start.41 = (bf16[480,128]{1,0:T(8,128)(2,1)S(1)}, bf16[480,128]{1,0:T(8,128)(2,1)S(1)}, u32[]{:S(2)}, u32[]{:S(2)}) collective-permute-start(bf16[480,128]{1,0:T(8,128)(2,1)S(1)} %get-tuple-element.23), channel_id=1, source_target_pairs={{0,6},{1,7},{2,0},{3,1},{4,2},{5,3},{6,4},{7,5},{8,14},{9,15},{10,... | collective-permute-start | bytes 368648 | tf_op jit(solution)/shard_map/ppermute | solution.py:380
  99.3 5.0 %collective-permute-start.43 = (f32[64,64]{1,0:T(8,128)S(1)}, f32[64,64]{1,0:T(8,128)S(1)}, u32[]{:S(2)}, u32[]{:S(2)}) collective-permute-start(f32[64,64]{1,0:T(8,128)S(1)} %get-tuple-element.26.refs_1_), channel_id=1, source_target_pairs={{0,16},{8,24},{16,0},{24,8},{1,17},{9,25},{17,1},{25,9},{2,18},{10... | collective-permute-start | bytes 49160 | tf_op jit(solution)/shard_map/ppermute | solution.py:371
  99.5 6.5 %collective-permute-start.42 = (f32[64,64]{1,0:T(8,128)S(1)}, f32[64,64]{1,0:T(8,128)S(1)}, u32[]{:S(2)}, u32[]{:S(2)}) collective-permute-start(f32[64,64]{1,0:T(8,128)S(1)} %get-tuple-element.26.refs_1_), channel_id=1, source_target_pairs={{0,8},{8,16},{16,24},{24,0},{1,9},{9,17},{17,25},{25,1},{2,10},{10... | collective-permute-start | bytes 49160 | tf_op jit(solution)/shard_map/ppermute | solution.py:371
  (16 other events, 71.4 us)

commit v3 on v2

v3 whole, which is shorter than its diff:
```python
import functools

import jax
import jax.numpy as jnp
from jax import lax
from jax.experimental import pallas as pl
from jax.experimental.pallas import tpu as pltpu
from jax.sharding import PartitionSpec as P

BLK = 128
SWEEPS = 3
GROUP = 16
FEAT = 64
PIECES = 16
SCALE = 512.0
LOG2E = 1.4426950408889634
F32 = jnp.float32
BF16 = jnp.bfloat16
MIB = 1 << 20

VMEM_SPEC = pl.BlockSpec(memory_space=pltpu.VMEM)
SMEM_SPEC = pl.BlockSpec(memory_space=pltpu.SMEM)


def split3(x):
    high = x.astype(BF16).astype(F32)
    mid = (x - high).astype(BF16).astype(F32)
    low = (x - high - mid).astype(BF16).astype(F32)
    return high, mid, low


def tree_sum(values):
    values = list(values)
    while len(values) > 1:
        values = [a + b for a, b in zip(values[::2], values[1::2])]
    return values[0]


def call(kernel, outs, ins, scratch=(), limit=24, flops=1 << 24):
    args, specs = [], []
    for kind, array in ins:
        if kind == "smem":
            specs.append(SMEM_SPEC)
        elif kind == "any":
            specs.append(pl.BlockSpec(memory_space=pl.ANY))
        else:
            specs.append(VMEM_SPEC)
            if kind == "keep":
                array = pltpu.with_memory_space_constraint(array, pltpu.VMEM)
        args.append(array)
    return pl.pallas_call(
        kernel,
        out_shape=tuple(outs),
        in_specs=specs,
        out_specs=tuple(VMEM_SPEC for _ in outs),
        scratch_shapes=list(scratch),
        compiler_params=pltpu.CompilerParams(vmem_limit_bytes=limit * MIB),
        cost_estimate=pl.CostEstimate(flops=flops, bytes_accessed=1 << 20, transcendentals=0),
    )(*args)


def pack_kernel(prof_ref, width_ref, basis_ref, out_ref, all_ref, work):
    pcs = prof_ref.shape[0]
    prof = prof_ref[...].astype(F32)
    norm = jnp.sum(prof * prof, axis=0, keepdims=True)
    high, mid, low = split3(norm)
    work[...] = jnp.zeros_like(work)
    work[0:pcs, :] = prof
    work[pcs : pcs + 1, :] = high
    work[pcs + 1 : pcs + 2, :] = mid
    work[pcs + 2 : pcs + 3, :] = low
    work[pcs + 3 : pcs + 6, :] = jnp.ones((3, prof.shape[1]), F32)
    work[pcs + 6 : pcs + 7, :] = width_ref[...].astype(F32)
    packed = work[...].astype(BF16)
    out_ref[...] = packed
    all_ref[0:FEAT] = packed
    all_ref[FEAT:] = basis_ref[...]


def places():
    return lax.axis_index("row"), lax.axis_index("col")


def slot_loop(step, count, size, group):
    def advance(number, carry):
        for i in range(0, group, size):
            step(*[number * group + i + j for j in range(size)])
        return carry

    lax.fori_loop(0, (count + group - 1) // group, advance, 0)


def shifted(me, k, n):
    return lax.rem(me + (n - k), n)


def ordered_sum(stage, refs, where, n):
    for place, ref in zip(where, refs):
        stage[place] = ref[...]
    return tree_sum([stage[i] for i in range(n)])


def square(tile, slots):
    a, b, c, d = [tile[s] for s in slots]
    return jnp.concatenate(
        [jnp.concatenate([a, b], axis=1), jnp.concatenate([c, d], axis=1)], axis=0
    )


def add_rows(acc, lists, target, slots, sums, total, spare, firsts):
    for i, (s, (row, lane)) in enumerate(zip(slots, firsts)):
        place = jnp.where(s < total, lists[0, 0, target, s], spare)
        acc[place] += sums[row : row + 8, lane : lane + BLK]


def row_sums(lists, tile, left, acc, total, spare):
    def step(*slots):
        low = [left[0, lists[0, 0, 1, s]] for s in slots[:2]]
        high = [left[1, lists[0, 0, 1, s]] for s in slots[2:]]
        sums = jnp.dot(
            jnp.concatenate(low + high, axis=0),
            square(tile, slots),
            preferred_element_type=F32,
        )
        firsts = [(0, 0), (PIECES, BLK), (2 * PIECES, 0), (3 * PIECES, BLK)]
        add_rows(acc, lists, 0, slots, sums, total, spare, firsts)

    slot_loop(step, total, 4, GROUP)


def col_sums(lists, tile, left, acc, total, spare):
    def step(*slots):
        pieces = [left[i % 2, lists[0, 0, 0, s]] for i, s in enumerate(slots)]
        sums = lax.dot_general(
            jnp.concatenate(pieces, axis=0),
            square(tile, slots),
            (((1,), (1,)), ((), ())),
            preferred_element_type=F32,
        )
        firsts = [(0, 0), (PIECES, 0), (2 * PIECES, BLK), (3 * PIECES, BLK)]
        add_rows(acc, lists, 1, slots, sums, total, spare, firsts)

    slot_loop(step, total, 4, GROUP)


def fill_pieces(left, scaling):
    high, mid, low = split3(scaling)
    shape = (PIECES, BLK)
    rows = lax.broadcasted_iota(jnp.int32, shape, 0)
    empty = jnp.zeros(shape, F32).astype(BF16)
    for b in range(scaling.shape[0]):
        value = jnp.where(
            rows == 0,
            jnp.broadcast_to(high[b : b + 1], shape),
            jnp.where(
                rows == 1,
                jnp.broadcast_to(mid[b : b + 1], shape),
                jnp.where(rows == 2, jnp.broadcast_to(low[b : b + 1], shape), 0.0),
            ),
        ).astype(BF16)
        left[0, b] = jnp.concatenate([value, empty], axis=1)
        left[1, b] = jnp.concatenate([empty, value], axis=1)


def build_kernel(pcs, n_row, n_col, *refs):
    lists, counts = refs[:2]
    col_in = refs[2 : 2 + n_row]
    row_in = refs[2 + n_row : 2 + n_row + n_col]
    tile, part, row_prof, row_inv, col_prof, col_inv, acc, left = refs[2 + n_row + n_col :]
    per = row_in[0].shape[1] // BLK
    col_blocks, row_blocks = n_row * per, n_col * per
    total = counts[0, 0]
    me_row, me_col = places()
    chip, core = me_col // 2, lax.rem(me_col, 2)
    for k, ref in enumerate(row_in):
        piece = shifted(chip, k // 2, n_col // 2) * 2
        piece = piece + (core if k % 2 == 0 else 1 - core)
        for j in range(per):
            block = ref[:, j * BLK : (j + 1) * BLK]
            row_prof[piece * per + j] = block
            width = block.astype(F32)[pcs + 6 : pcs + 7, :]
            row_inv[piece * per + j] = jnp.broadcast_to(1.0 / width, (8, BLK))
    rows = lax.broadcasted_iota(jnp.int32, (FEAT, BLK), 0)
    for k, ref in enumerate(col_in):
        piece = shifted(me_row, k, n_row)
        for j in range(per):
            block = ref[0:FEAT, j * BLK : (j + 1) * BLK].astype(F32)
            turned = jnp.where(rows < pcs, -2.0 * block, 0.0)
            turned = jnp.where((rows >= pcs) & (rows < pcs + 3), 1.0, turned)
            turned = jnp.where(
                (rows >= pcs + 3) & (rows < pcs + 6), pltpu.roll(block, 3, 0), turned
            )
            turned = jnp.where(rows == pcs + 7, pltpu.roll(block, 1, 0), turned)
            turned = turned.T
            col_prof[piece * per + j] = turned.astype(BF16)
            col_inv[piece * per + j] = jnp.broadcast_to(
                -LOG2E / turned[:, pcs + 7 : pcs + 8], (BLK, BLK)
            )

    def step(s):
        rb, cb = lists[0, 0, 0, s], lists[0, 0, 1, s]
        distance = jnp.dot(col_prof[cb], row_prof[rb], preferred_element_type=F32)
        block = jnp.exp2(distance * col_inv[cb] * row_inv[rb][0:1, :])
        tile[s] = block.astype(BF16)

    slot_loop(step, total, 1, GROUP)
    ones = (lax.broadcasted_iota(jnp.int32, (PIECES, BLK), 0) == 0).astype(F32).astype(BF16)
    empty = jnp.zeros_like(ones)
    for b in range(row_blocks):
        left[0, b] = jnp.concatenate([ones, empty], axis=1)
        left[1, b] = jnp.concatenate([empty, ones], axis=1)
    acc[...] = jnp.zeros_like(acc)
    col_sums(lists, tile, left, acc, total, col_blocks)
    part[...] = jnp.sum(acc[0:col_blocks], axis=1)


def pass_kernel(over_rows, n, ratio, n_parts, *refs):
    lists, counts, tile = refs[:3]
    parts = refs[3 : 3 + n_parts]
    out, stage, left, acc = refs[-4:]
    total = counts[0, 0]
    blocks = out.shape[0]
    where = arrivals("row" if over_rows else "col", n, ratio)
    fill_pieces(left, SCALE / ordered_sum(stage, parts, where, n))
    acc[...] = jnp.zeros_like(acc)
    (row_sums if over_rows else col_sums)(lists, tile, left, acc, total, blocks)
    out[...] = jnp.sum(acc[0:blocks], axis=1)


def pieces_of(value):
    return [v.astype(BF16) for v in split3(value)]


def last_kernel(n_row, n_col, n_land, n_parts, *refs):
    lists, counts, marks, tile = refs[:4]
    parts = refs[4 : 4 + n_parts]
    packs = refs[4 + n_parts : 4 + n_parts + n_row]
    keep, away, both, scaling_out, stage, scaled, acc = refs[4 + n_parts + n_row :]
    cols = packs[0].shape[0] - FEAT
    per = packs[0].shape[1] // BLK
    blocks = n_col * per
    total = counts[0, 0]
    me_row, me_col = places()
    where = arrivals("row", n_row, n_col // n_row)
    scaling = SCALE / ordered_sum(stage, parts, where, n_row)
    scaling_out[...] = scaling
    for k in range(n_row):
        piece = shifted(me_row, k, n_row)
        for j in range(per):
            block = packs[k][FEAT:, j * BLK : (j + 1) * BLK].astype(F32)
            b = piece * per + j
            scaled[b, 0:cols] = (block * scaling_out[pl.ds(b, 1), :]).astype(BF16)
    high, mid, low = split3(scaling)
    shape = (PIECES, BLK)
    rows = lax.broadcasted_iota(jnp.int32, shape, 0)
    for b in range(scaling.shape[0]):
        value = jnp.where(
            rows == 0,
            jnp.broadcast_to(high[b : b + 1], shape),
            jnp.where(
                rows == 1,
                jnp.broadcast_to(mid[b : b + 1], shape),
                jnp.where(rows == 2, jnp.broadcast_to(low[b : b + 1], shape), 0.0),
            ),
        )
        scaled[b, cols : cols + PIECES] = value.astype(BF16)
    acc[...] = jnp.zeros_like(acc)

    def step(s):
        target = jnp.where(s < total, lists[0, 0, 0, s], blocks)
        sums = jnp.dot(scaled[lists[0, 0, 1, s]], tile[s], preferred_element_type=F32)
        acc[target] += sums[0 : cols + 8]

    slot_loop(step, total, 1, 8)
    core = lax.rem(me_col, 2)
    for q in range(n_col // 2):
        own = (2 * q + core) * per
        other = (2 * q + 1 - core) * per
        for j in range(per):
            keep[q, j] = acc[own + j, 0:cols]
            away[q, j] = acc[other + j, 0:cols].astype(BF16)
    row_part = jnp.sum(acc[0:blocks, cols : cols + 8], axis=1)
    for i, value in enumerate(pieces_of(row_part)):
        both[i * blocks : (i + 1) * blocks] = value
    for i in range(n_land):
        first = 3 * blocks + i * cols
        both[first : first + cols] = acc[marks[me_row * n_land + i] - me_row * blocks, 0:cols].astype(BF16)


def three(ref, blocks):
    value = ref[0 : 3 * blocks].astype(F32)
    return (value[2 * blocks :] + value[blocks : 2 * blocks]) + value[0:blocks]


def pair_kernel(keep, away, both, both_in, both_out, *outs):
    n_chip, per, cols = keep.shape[:3]
    blocks = 2 * n_chip * per
    chip = places()[1] // 2
    parts = pieces_of(three(both, blocks) + three(both_in, blocks))
    for i, value in enumerate(parts):
        both_out[i * blocks : (i + 1) * blocks] = value
    lands = both[3 * blocks :].astype(F32) + both_in[3 * blocks :].astype(F32)
    both_out[3 * blocks :] = lands.astype(BF16)
    for k, out in enumerate(outs):
        to = lax.rem(chip + k, n_chip)
        for j in range(per):
            value = keep[to, j] + away[to, j].astype(F32)
            out[j * cols : (j + 1) * cols] = value.astype(BF16)


def gram_kernel(n_land, cols, per, *refs):
    marks = refs[0]
    gram, scaling_out, own, inverse, stage, land_stage = refs[-6:]
    parts = refs[1:-6]
    n = len(parts)
    me_row, me_col = places()
    blocks = scaling_out.shape[0]
    for k, part in enumerate(parts):
        place = shifted(me_col // 2, k, n)
        stage[place] = three(part, blocks)
        land_stage[place] = part[3 * blocks :]
    inverse[...] = 1.0 / tree_sum([stage[i] for i in range(n)])
    scaling_out[...] = SCALE * inverse[...]
    for j in range(per):
        own[j : j + 1, :] = inverse[pl.ds(me_col * per + j, 1), :]
    total = None
    for i in range(n_land):
        summed = tree_sum(
            [land_stage[k, i * cols : (i + 1) * cols].astype(F32) for k in range(n)]
        )
        block = marks[me_row * n_land + i] - me_row * blocks
        projected = summed * inverse[pl.ds(block, 1), :]
        product = lax.dot_general(
            projected,
            projected,
            (((1,), (1,)), ((), ())),
            precision=lax.Precision.HIGHEST,
            preferred_element_type=F32,
        )
        total = product if total is None else total + product
    gram[...] = total


WIDE = 4


def eliminate(gram):
    cols = gram.shape[0]
    rows = lax.broadcasted_iota(jnp.int32, (cols, 2 * cols), 0)
    lanes = lax.broadcasted_iota(jnp.int32, (cols, 2 * cols), 1)
    unit = (rows[:, :cols] == lanes[:, :cols]).astype(F32)
    work = jnp.concatenate([gram, unit], axis=1)
    for first in range(0, cols, WIDE):
        tops = [work[first + i : first + i + 1, :] for i in range(WIDE)]
        sides = [
            jnp.broadcast_to(work[:, first + i : first + i + 1], work.shape)
            for i in range(WIDE)
        ]
        change = None
        for i in range(WIDE):
            pivot = first + i
            unit_top = tops[i] / sides[i][pivot : pivot + 1, :]
            for m in range(i + 1, WIDE):
                factor = sides[i][first + m : first + m + 1, :]
                tops[m] = tops[m] - factor * unit_top
                inner = factor / sides[i][pivot : pivot + 1, :]
                sides[m] = sides[m] - sides[i] * inner
            term = sides[i] * unit_top
            change = term if change is None else change + term
        reduced = work - change
        kept = work
        for i in range(WIDE):
            kept = jnp.where(rows == first + i, tops[i], kept)
        work = jnp.where(rows >= first + WIDE, reduced, kept)
    pivots = jnp.sum(jnp.where(rows == lanes, work, 0.0), axis=1, keepdims=True)
    return (work * lax.rsqrt(pivots))[:, cols:]


def ritz_kernel(n_row, ratio, cells, n_grams, *refs):
    grams = refs[:n_grams]
    parts = refs[n_grams:-3]
    own, out, stage = refs[-3:]
    cols = grams[0].shape[0]
    per = out.shape[1] // BLK
    where = arrivals("row", n_row, ratio)
    inverse = eliminate(ordered_sum(stage, grams, where, n_row) * (1.0 / cells))
    for j in range(per):
        summed = tree_sum([m[j * cols : (j + 1) * cols].astype(F32) for m in parts])
        projected = summed * own[j : j + 1, :]
        out[:, j * BLK : (j + 1) * BLK] = jnp.dot(
            inverse, projected, precision=lax.Precision.HIGHEST, preferred_element_type=F32
        )


def shift(x, axis, k):
    n = lax.axis_size(axis)
    return lax.ppermute(x, axis, [(i, (i + k) % n) for i in range(n)])


def exchange(x, axis):
    return [x] + [shift(x, axis, k) for k in range(1, lax.axis_size(axis))]


def rounds(n, late):
    early = n - late
    spread = early // late
    first = [
        [(o, (o + k) % early) for o in range(early)] for k in range(1, early)
    ]
    second = [
        [(early + i, early + (i + k) % late) for i in range(late)] for k in range(1, late)
    ]
    for j in range(early):
        pairs = [(early + i, (j + i * spread) % early) for i in range(late)]
        second.append(pairs + [(b, a) for a, b in pairs])
    return first, second


def origin(axis, ratio, row, col):
    return col // ratio + 1 if axis == "row" else row * ratio + ratio


def arrivals(axis, n, ratio):
    row, col = places()
    me = row if axis == "row" else col
    base = origin(axis, ratio, row, col)
    first, second = rounds(n, 1 if axis == "row" else ratio)
    own = lax.rem(me + (2 * n) - base, n)
    found = [me]
    for pairs in first + second:
        source = n
        for a, b in pairs:
            source = jnp.where(own == b, lax.rem(base + a, n), source)
        found.append(source)
    return found


def late_exchange(x, axis):
    n_row, n_col = lax.axis_size("row"), lax.axis_size("col")
    ratio = n_col // n_row
    along_row = axis == "row"
    n = n_row if along_row else n_col

    def send(value, pairs):
        flat = []
        for line in range(n_col if along_row else n_row):
            base = origin(axis, ratio, line, line)
            for a, b in pairs:
                a, b = (base + a) % n, (base + b) % n
                if along_row:
                    flat.append((a * n_col + line, b * n_col + line))
                else:
                    flat.append((line * n_col + a, line * n_col + b))
        return lax.ppermute(value, ("row", "col"), flat)

    first, second = rounds(n, 1 if along_row else ratio)
    early = [send(x, pairs) for pairs in first]
    x, early = lax.optimization_barrier((x, early))
    return [x] + early + [send(x, pairs) for pairs in second]


def chip_shift(x, k):
    n = lax.axis_size("col") // 2
    return lax.ppermute(
        x,
        "col",
        [(2 * q + p, 2 * ((q + k) % n) + p) for q in range(n) for p in range(2)],
    )


def sibling(x):
    return lax.ppermute(x, "col", [(i, i ^ 1) for i in range(lax.axis_size("col"))])


def vec(*arrays):
    return [("vmem", a) for a in arrays]


def body(profiles, cell_width, basis, block_lists, block_counts, landmarks):
    n_row, n_col = lax.axis_size("row"), lax.axis_size("col")
    n_chip = n_col // 2
    pcs, share = profiles.shape
    cols = basis.shape[0]
    per = share // BLK
    row_blocks, col_blocks = n_col * per, n_row * per
    slots = block_lists.shape[-1]
    n_land = landmarks.shape[0] // n_row

    def shape(*dims, dtype=F32):
        return jax.ShapeDtypeStruct(dims, dtype)

    ratio = n_col // n_row
    packed, packed_all = call(
        pack_kernel,
        [shape(FEAT, share, dtype=BF16), shape(FEAT + cols, share, dtype=BF16)],
        vec(profiles, cell_width.reshape(1, share), basis),
        [pltpu.VMEM((FEAT, share), F32)],
    )
    spread = lax.ppermute(
        packed,
        ("row", "col"),
        [((q % n_row) * n_col + q // n_row, q) for q in range(n_row * n_col)],
    )
    col_packs = exchange(packed_all, "row")
    row_packs = []
    for k in range(n_chip):
        pack = chip_shift(spread, k) if k else spread
        row_packs += [pack, sibling(pack)]
    lists = [("smem", block_lists), ("smem", block_counts)]
    marks = [("smem", landmarks)]
    tile, part = call(
        functools.partial(build_kernel, pcs, n_row, n_col),
        [pltpu.VMEM((slots, BLK, BLK), BF16), shape(col_blocks, BLK)],
        lists + vec(*col_packs, *row_packs),
        [
            pltpu.VMEM((row_blocks, FEAT, BLK), BF16),
            pltpu.VMEM((row_blocks, 8, BLK), F32),
            pltpu.VMEM((col_blocks, BLK, FEAT), BF16),
            pltpu.VMEM((col_blocks, BLK, BLK), F32),
            pltpu.VMEM((col_blocks + 1, 8, BLK), F32),
            pltpu.VMEM((2, row_blocks, PIECES, 2 * BLK), BF16),
        ],
    )
    for number in range(SWEEPS - 1):
        parts = late_exchange(part, "row")
        (part,) = call(
            functools.partial(pass_kernel, True, n_row, ratio, len(parts)),
            [shape(row_blocks, BLK)],
            lists + [("keep", tile)] + vec(*parts),
            [
                pltpu.VMEM((n_row + 1, col_blocks, BLK), F32),
                pltpu.VMEM((2, col_blocks, PIECES, 2 * BLK), BF16),
                pltpu.VMEM((row_blocks + 1, 8, BLK), F32),
            ],
        )
        parts = late_exchange(part, "col")
        (part,) = call(
            functools.partial(pass_kernel, False, n_col, ratio, len(parts)),
            [shape(col_blocks, BLK)],
            lists + [("keep", tile)] + vec(*parts),
            [
                pltpu.VMEM((n_col + 1, row_blocks, BLK), F32),
                pltpu.VMEM((2, row_blocks, PIECES, 2 * BLK), BF16),
                pltpu.VMEM((col_blocks + 1, 8, BLK), F32),
            ],
        )
    both_rows = 3 * row_blocks + n_land * cols
    parts = late_exchange(part, "row")
    keep, away, both, col_scaling = call(
        functools.partial(last_kernel, n_row, n_col, n_land, len(parts)),
        [
            shape(n_chip, per, cols, BLK),
            shape(n_chip, per, cols, BLK, dtype=BF16),
            shape(both_rows, BLK, dtype=BF16),
            shape(col_blocks, BLK),
        ],
        lists + marks + [("keep", tile)] + vec(*parts, *col_packs),
        [
            pltpu.VMEM((n_row + 1, col_blocks, BLK), F32),
            pltpu.VMEM((col_blocks, cols + PIECES, BLK), BF16),
            pltpu.VMEM((row_blocks + 1, cols + 8, BLK), F32),
        ],
    )
    pairs = call(
        pair_kernel,
        [shape(both_rows, BLK, dtype=BF16)]
        + [shape(per * cols, BLK, dtype=BF16)] * n_chip,
        vec(keep, sibling(away), both, sibling(both)),
    )
    sums = [pairs[0]] + [chip_shift(pairs[0], k) for k in range(1, n_chip)]
    shares = [pairs[1]] + [chip_shift(pairs[1 + k], k) for k in range(1, n_chip)]
    gram, row_scaling, own = call(
        functools.partial(gram_kernel, n_land, cols, per),
        [shape(cols, cols), shape(row_blocks, BLK), shape(per, BLK)],
        marks + vec(*sums),
        [
            pltpu.VMEM((row_blocks, BLK), F32),
            pltpu.VMEM((n_chip, row_blocks, BLK), F32),
            pltpu.VMEM((n_chip, n_land * cols, BLK), BF16),
        ],
    )
    grams = late_exchange(gram, "row")
    (ritz,) = call(
        functools.partial(ritz_kernel, n_row, ratio, landmarks.shape[0] * BLK, len(grams)),
        [shape(cols, share)],
        vec(*grams, *shares, own),
        [pltpu.VMEM((n_row + 1, cols, cols), F32)],
    )
    return row_scaling.reshape(-1), col_scaling.reshape(-1), ritz


def solution(mesh):
    placed = (
        P(None, ("col", "row")),
        P(("col", "row")),
        P(None, ("col", "row")),
        P("row", "col", None, None),
        P("row", "col"),
        P(),
    )
    return jax.shard_map(
        body,
        mesh=mesh,
        in_specs=placed,
        out_specs=(P("row"), P("col"), P(None, ("row", "col"))),
        check_vma=False,
    )
```

time: 114 us -> 199 us (1.75)
  starting transfers between devices: 39.5 us -> 142 us
  waiting for transfers between devices: 35.5 us -> 23.9 us
  Pallas kernels: 31.4 us -> 27.1 us
    ppermute x0 -> x44, starting transfers between devices: none -> 115 us  [send(): return lax.ppermute(value, ('row', 'col'), flat)]
    ppermute x32 -> x3, starting transfers between devices: 30.9 us -> 4.96 us  [shift(): return lax.ppermute(x, axis, [(i, (i + k) % n) for i in range(n)])]
    ppermute x32 -> x3, waiting for transfers between devices: 26.9 us -> 1.01 us  [shift(): return lax.ppermute(x, axis, [(i, (i + k) % n) for i in range(n)])]
    ppermute x0 -> x44, waiting for transfers between devices: none -> 16.3 us  [send(): return lax.ppermute(value, ('row', 'col'), flat)]
    ppermute x6 -> x9, starting transfers between devices: 6.89 us -> 20.2 us  [chip_shift(): lax.ppermute(x, 'col', [(2 * q + p, 2 * ((q + k) % n) + p) for q in range...]
    pallas_call x10, Pallas kernels: 31.4 us -> 27.1 us  [call(): pl.pallas_call(kernel, out_shape=tuple(outs), in_specs=specs, out_specs=t...]
    ppermute x6 -> x9, waiting for transfers between devices: 7.46 us -> 5.45 us  [chip_shift(): lax.ppermute(x, 'col', [(2 * q + p, 2 * ((q + k) % n) + p) for q in range...]
  transfers between devices with their start and end apart: 45 -> 63, of which waited for: 23 -> 16; matrix products, arithmetic and copies ran while one was open for 3% -> 0% of each run, Pallas kernels for 5% -> 1%
where the time goes in v3:
time: 199 us; the launch traced here: 198 us
  starting transfers between devices  142 us (71%)
  Pallas kernels  27.1 us (14%)
  waiting for transfers between devices  23.9 us (12%)
  local copies, waits for them, and re-layouts  3.02 us (2%)
  between operations  2.04 us (1%)
    ppermute x44, starting transfers between devices, send(): return lax.ppermute(value, ('row', 'col'), flat)  115 us
    pallas_call x10, Pallas kernels, call(): pl.pallas_call(kernel, out_shape=tuple(outs), in_specs=specs, out_specs=t...  27.1 us
    ppermute x9, starting transfers between devices, chip_shift(): lax.ppermute(x, 'col', [(2 * q + p, 2 * ((q + k) % n) + p) for q in range...  20.2 us
    ppermute x44, waiting for transfers between devices, send(): return lax.ppermute(value, ('row', 'col'), flat)  16.3 us
    ppermute x9, waiting for transfers between devices, chip_shift(): lax.ppermute(x, 'col', [(2 * q + p, 2 * ((q + k) % n) + p) for q in range...  5.45 us
    ppermute x3, starting transfers between devices, shift(): return lax.ppermute(x, axis, [(i, (i + k) % n) for i in range(n)])  4.96 us
  transfers between devices with their start and end apart: 63, of which 16 were waited for; matrix products, arithmetic and copies ran while one was open for 0% of the time, Pallas kernels for 1%

profile of v3, /device:TPU:0, one launch (start us, length us, event | category | flops | bytes accessed | tf_op | source)
XLA Modules:
  0.0 197.7 jit_solution(18337054168573626875)
XLA Ops:
  3.7 13.2 %collective-permute-start.9 = (bf16[64,512]{1,0:T(8,128)(2,1)S(1)}, bf16[64,512]{1,0:T(8,128)(2,1)S(1)}, u32[]{:S(2)}, u32[]{:S(2)}) collective-permute-start(bf16[64,512]{1,0:T(8,128)(2,1)S(1)} %collective-permute-done.3.refs_6_), channel_id=1, source_target_pairs={{0,6},{1,7},{2,0},{3,1},{4,2},{5,3},{6,4},{7,5},{8,14},{9,15},{10,... | collective-permute-start | bytes 196616 | tf_op jit(solution)/shard_map/ppermute | solution.py:464
  17.2 4.4 %collective-permute-start.2 = (bf16[128,512]{1,0:T(8,128)(2,1)S(1)}, bf16[128,512]{1,0:T(8,128)(2,1)S(1)}, u32[]{:S(2)}, u32[]{:S(2)}) collective-permute-start(bf16[128,512]{1,0:T(8,128)(2,1)S(1)} %get-tuple-element.43.refs_2_.refs_10_), channel_id=1, source_target_pairs={{0,24},{8,0},{16,8},{24,16},{1,25},{9,1},{17,9},{25,17},{2,26},{10... | collective-permute-start | bytes 393224 | tf_op jit(solution)/shard_map/ppermute | solution.py:397
  22.2 5.1 %collective-permute-done.5.refs_8_ = bf16[64,512]{1,0:T(8,128)(2,1)S(1)} collective-permute-done((bf16[64,512]{1,0:T(8,128)(2,1)S(1)}, bf16[64,512]{1,0:T(8,128)(2,1)S(1)}, u32[]{:S(2)}, u32[]{:S(2)}) %collective-permute-start.5) | collective-permute-done | bytes 65568 | tf_op jit(solution)/shard_map/ppermute | solution.py:464
  30.3 6.0 %shard_map.86 = (bf16[128,128,128]{2,1,0:T(8,128)(2,1)S(1)}, f32[16,128]{1,0:T(8,128)S(1)}) custom-call(s32[1,1,2,128]{3,2,1,0:T(2,128)S(1)} %copy-done.2, s32[1,1]{1,0:T(1,128)S(6)} %copy.9.refs_1_, bf16[128,512]{1,0:T(8,128)(2,1)S(1)} %get-tuple-element.43.refs_2_.refs_10_, bf16[128,512]{1,0:T(8,128)(2,1)S(1)} %collective-permute-done.refs_3_.refs_11_, ...), custom_call_target="tpu_custom_call" | custom-call | flops 16777216 | bytes 1048576 | tf_op jit(solution)/shard_map/pallas_call | solution.py:51
  37.6 7.9 %collective-permute-start.15 = (f32[16,128]{1,0:T(8,128)S(1)}, f32[16,128]{1,0:T(8,128)S(1)}, u32[]{:S(2)}, u32[]{:S(2)}) collective-permute-start(f32[16,128]{1,0:T(8,128)S(1)} %get-tuple-element.47.refs_3_), channel_id=1, source_target_pairs={{0,24},{24,0},{1,25},{25,1},{10,2},{2,10},{11,3},{3,11},{20,12},{1... | collective-permute-start | bytes 24584 | tf_op jit(solution)/shard_map/ppermute | solution.py:454
  45.5 1.9 collective-permute-start.14
  47.5 1.9 collective-permute-start.13
  49.4 2.6 %collective-permute-done.14.refs_7_ = f32[16,128]{1,0:T(8,128)S(1)} collective-permute-done((f32[16,128]{1,0:T(8,128)S(1)}, f32[16,128]{1,0:T(8,128)S(1)}, u32[]{:S(2)}, u32[]{:S(2)}) %collective-permute-start.14) | collective-permute-done | bytes 8224 | tf_op jit(solution)/shard_map/ppermute | solution.py:454
  53.0 2.5 %shard_map.87.refs_3_ = f32[32,128]{1,0:T(8,128)S(1)} custom-call(s32[1,1,2,128]{3,2,1,0:T(2,128)S(1)} %copy-done.2, s32[1,1]{1,0:T(1,128)S(6)} %copy.9.refs_1_, bf16[128,128,128]{2,1,0:T(8,128)(2,1)S(1)} %get-tuple-element.45.refs_2_.refs_3_, f32[16,128]{1,0:T(8,128)S(1)} %get-tuple-element.47.refs_3_, f32[16,128]{1,0:T(8,128)S(1)} %collective-permute-done.11.refs_4_, ...), custom_call_target="tpu_custom_call" | custom-call | flops 16777216 | bytes 1048576 | tf_op jit(solution)/shard_map/pallas_call | solution.py:51
  58.9 11.3 %collective-permute-start.27 = (f32[32,128]{1,0:T(8,128)S(1)}, f32[32,128]{1,0:T(8,128)S(1)}, u32[]{:S(2)}, u32[]{:S(2)}) collective-permute-start(f32[32,128]{1,0:T(8,128)S(1)} %shard_map.87.refs_3_), channel_id=1, source_target_pairs={{0,7},{1,4},{7,0},{4,1},{10,9},{11,14},{9,10},{14,11},{20,19},{21,... | collective-permute-start | bytes 49160 | tf_op jit(solution)/shard_map/ppermute | solution.py:454
  70.2 1.9 collective-permute-start.26
  72.2 1.9 collective-permute-start.25
  76.0 3.1 %collective-permute-start.23 = (f32[32,128]{1,0:T(8,128)S(1)}, f32[32,128]{1,0:T(8,128)S(1)}, u32[]{:S(2)}, u32[]{:S(2)}) collective-permute-start(f32[32,128]{1,0:T(8,128)S(1)} %shard_map.87.refs_3_), channel_id=1, source_target_pairs={{0,3},{1,6},{3,0},{6,1},{10,13},{11,8},{13,10},{8,11},{20,23},{21,... | collective-permute-start | bytes 49160 | tf_op jit(solution)/shard_map/ppermute | solution.py:454
  79.2 2.2 %collective-permute-start.22 = (f32[32,128]{1,0:T(8,128)S(1)}, f32[32,128]{1,0:T(8,128)S(1)}, u32[]{:S(2)}, u32[]{:S(2)}) collective-permute-start(f32[32,128]{1,0:T(8,128)S(1)} %shard_map.87.refs_3_), channel_id=1, source_target_pairs={{0,2},{1,5},{2,0},{5,1},{10,12},{11,15},{12,10},{15,11},{20,22},{2... | collective-permute-start | bytes 49160 | tf_op jit(solution)/shard_map/ppermute | solution.py:454
  81.4 2.8 %collective-permute-start.21 = (f32[32,128]{1,0:T(8,128)S(1)}, f32[32,128]{1,0:T(8,128)S(1)}, u32[]{:S(2)}, u32[]{:S(2)}) collective-permute-start(f32[32,128]{1,0:T(8,128)S(1)} %shard_map.87.refs_3_), channel_id=1, source_target_pairs={{0,1},{1,0},{10,11},{11,10},{20,21},{21,20},{30,31},{31,30}} | collective-permute-start | bytes 49160 | tf_op jit(solution)/shard_map/ppermute | solution.py:454
  85.0 3.1 %shard_map.88.refs_3_ = f32[16,128]{1,0:T(8,128)S(1)} custom-call(s32[1,1,2,128]{3,2,1,0:T(2,128)S(1)} %copy-done.2, s32[1,1]{1,0:T(1,128)S(6)} %copy.9.refs_1_, bf16[128,128,128]{2,1,0:T(8,128)(2,1)S(1)} %get-tuple-element.45.refs_2_.refs_3_, f32[32,128]{1,0:T(8,128)S(1)} %shard_map.87.refs_3_, f32[32,128]{1,0:T(8,128)S(1)} %collective-permute-done.16.refs_4_, ...), custom_call_target="tpu_custom_call" | custom-call | flops 16777216 | bytes 1048576 | tf_op jit(solution)/shard_map/pallas_call | solution.py:51
  89.5 8.3 %collective-permute-start.32 = (f32[16,128]{1,0:T(8,128)S(1)}, f32[16,128]{1,0:T(8,128)S(1)}, u32[]{:S(2)}, u32[]{:S(2)}) collective-permute-start(f32[16,128]{1,0:T(8,128)S(1)} %shard_map.88.refs_3_), channel_id=1, source_target_pairs={{0,24},{24,0},{1,25},{25,1},{10,2},{2,10},{11,3},{3,11},{20,12},{1... | collective-permute-start | bytes 24584 | tf_op jit(solution)/shard_map/ppermute | solution.py:454
  101.7 2.6 %collective-permute-done.31.refs_7_ = f32[16,128]{1,0:T(8,128)S(1)} collective-permute-done((f32[16,128]{1,0:T(8,128)S(1)}, f32[16,128]{1,0:T(8,128)S(1)}, u32[]{:S(2)}, u32[]{:S(2)}) %collective-permute-start.31) | collective-permute-done | bytes 8224 | tf_op jit(solution)/shard_map/ppermute | solution.py:454
  105.3 2.5 %shard_map.89.refs_3_ = f32[32,128]{1,0:T(8,128)S(1)} custom-call(s32[1,1,2,128]{3,2,1,0:T(2,128)S(1)} %copy-done.2, s32[1,1]{1,0:T(1,128)S(6)} %copy.9.refs_1_, bf16[128,128,128]{2,1,0:T(8,128)(2,1)S(1)} %get-tuple-element.45.refs_2_.refs_3_, f32[16,128]{1,0:T(8,128)S(1)} %shard_map.88.refs_3_, f32[16,128]{1,0:T(8,128)S(1)} %collective-permute-done.28.refs_4_, ...), custom_call_target="tpu_custom_call" | custom-call | flops 16777216 | bytes 1048576 | tf_op jit(solution)/shard_map/pallas_call | solution.py:51
  111.2 11.1 %collective-permute-start.44 = (f32[32,128]{1,0:T(8,128)S(1)}, f32[32,128]{1,0:T(8,128)S(1)}, u32[]{:S(2)}, u32[]{:S(2)}) collective-permute-start(f32[32,128]{1,0:T(8,128)S(1)} %shard_map.89.refs_3_), channel_id=1, source_target_pairs={{0,7},{1,4},{7,0},{4,1},{10,9},{11,14},{9,10},{14,11},{20,19},{21,... | collective-permute-start | bytes 49160 | tf_op jit(solution)/shard_map/ppermute | solution.py:454
  128.1 3.1 %collective-permute-start.40 = (f32[32,128]{1,0:T(8,128)S(1)}, f32[32,128]{1,0:T(8,128)S(1)}, u32[]{:S(2)}, u32[]{:S(2)}) collective-permute-start(f32[32,128]{1,0:T(8,128)S(1)} %shard_map.89.refs_3_), channel_id=1, source_target_pairs={{0,3},{1,6},{3,0},{6,1},{10,13},{11,8},{13,10},{8,11},{20,23},{21,... | collective-permute-start | bytes 49160 | tf_op jit(solution)/shard_map/ppermute | solution.py:454
  131.2 2.2 %collective-permute-start.39 = (f32[32,128]{1,0:T(8,128)S(1)}, f32[32,128]{1,0:T(8,128)S(1)}, u32[]{:S(2)}, u32[]{:S(2)}) collective-permute-start(f32[32,128]{1,0:T(8,128)S(1)} %shard_map.89.refs_3_), channel_id=1, source_target_pairs={{0,2},{1,5},{2,0},{5,1},{10,12},{11,15},{12,10},{15,11},{20,22},{2... | collective-permute-start | bytes 49160 | tf_op jit(solution)/shard_map/ppermute | solution.py:454
  133.4 2.8 %collective-permute-start.38 = (f32[32,128]{1,0:T(8,128)S(1)}, f32[32,128]{1,0:T(8,128)S(1)}, u32[]{:S(2)}, u32[]{:S(2)}) collective-permute-start(f32[32,128]{1,0:T(8,128)S(1)} %shard_map.89.refs_3_), channel_id=1, source_target_pairs={{0,1},{1,0},{10,11},{11,10},{20,21},{21,20},{30,31},{31,30}} | collective-permute-start | bytes 49160 | tf_op jit(solution)/shard_map/ppermute | solution.py:454
  137.1 3.1 %shard_map.90.refs_4_ = f32[16,128]{1,0:T(8,128)S(1)} custom-call(s32[1,1,2,128]{3,2,1,0:T(2,128)S(1)} %copy-done.2, s32[1,1]{1,0:T(1,128)S(6)} %copy.9.refs_1_, bf16[128,128,128]{2,1,0:T(8,128)(2,1)S(1)} %get-tuple-element.45.refs_2_.refs_3_, f32[32,128]{1,0:T(8,128)S(1)} %shard_map.89.refs_3_, f32[32,128]{1,0:T(8,128)S(1)} %collective-permute-done.33.refs_4_, ...), custom_call_target="tpu_custom_call" | custom-call | flops 16777216 | bytes 1048576 | tf_op jit(solution)/shard_map/pallas_call | solution.py:51
  141.5 8.1 %collective-permute-start.49 = (f32[16,128]{1,0:T(8,128)S(1)}, f32[16,128]{1,0:T(8,128)S(1)}, u32[]{:S(2)}, u32[]{:S(2)}) collective-permute-start(f32[16,128]{1,0:T(8,128)S(1)} %shard_map.90.refs_4_), channel_id=1, source_target_pairs={{0,24},{24,0},{1,25},{25,1},{10,2},{2,10},{11,3},{3,11},{20,12},{1... | collective-permute-start | bytes 24584 | tf_op jit(solution)/shard_map/ppermute | solution.py:454
  153.5 2.6 %collective-permute-done.48.refs_8_ = f32[16,128]{1,0:T(8,128)S(1)} collective-permute-done((f32[16,128]{1,0:T(8,128)S(1)}, f32[16,128]{1,0:T(8,128)S(1)}, u32[]{:S(2)}, u32[]{:S(2)}) %collective-permute-start.48) | collective-permute-done | bytes 8224 | tf_op jit(solution)/shard_map/ppermute | solution.py:454
  157.1 5.3 %shard_map.91 = (f32[4,4,64,128]{3,2,1,0:T(8,128)S(1)}, bf16[4,4,64,128]{3,2,1,0:T(8,128)(2,1)S(1)}, bf16[224,128]{1,0:T(8,128)(2,1)S(1)}, f32[16,128]{1,0:T(8,128)}) custom-call(s32[1,1,2,128]{3,2,1,0:T(2,128)S(1)} %copy-done.2, s32[1,1]{1,0:T(1,128)S(6)} %copy.9.refs_1_, s32[8]{0:T(128)S(1)} %copy-done.3, ...), custom_call_target="tpu_custom_call" | custom-call | flops 16777216 | bytes 1048576 | tf_op jit(solution)/shard_map/pallas_call | solution.py:51
  164.3 1.9 collective-permute-start.52
  168.6 2.5 %collective-permute-start.62 = (bf16[256,128]{1,0:T(8,128)(2,1)S(1)}, bf16[256,128]{1,0:T(8,128)(2,1)S(1)}, u32[]{:S(2)}, u32[]{:S(2)}) collective-permute-start(bf16[256,128]{1,0:T(8,128)(2,1)S(1)} %get-tuple-element.81), channel_id=1, source_target_pairs={{0,6},{1,7},{2,0},{3,1},{4,2},{5,3},{6,4},{7,5},{8,14},{9,15},{10,... | collective-permute-start | bytes 196616 | tf_op jit(solution)/shard_map/ppermute | solution.py:464
  173.8 12.9 %collective-permute-start.59 = (f32[64,64]{1,0:T(8,128)S(1)}, f32[64,64]{1,0:T(8,128)S(1)}, u32[]{:S(2)}, u32[]{:S(2)}) collective-permute-start(f32[64,64]{1,0:T(8,128)S(1)} %get-tuple-element.75.refs_0_), channel_id=1, source_target_pairs={{0,24},{24,0},{1,25},{25,1},{10,2},{2,10},{11,3},{3,11},{20,12},{1... | collective-permute-start | bytes 49160 | tf_op jit(solution)/shard_map/ppermute | solution.py:454
  190.6 2.8 %collective-permute-done.58.refs_4_ = f32[64,64]{1,0:T(8,128)S(1)} collective-permute-done((f32[64,64]{1,0:T(8,128)S(1)}, f32[64,64]{1,0:T(8,128)S(1)}, u32[]{:S(2)}, u32[]{:S(2)}) %collective-permute-start.58) | collective-permute-done | bytes 16416 | tf_op jit(solution)/shard_map/ppermute | solution.py:454
  194.4 3.2 %shard_map.94 = f32[64,512]{1,0:T(8,128)} custom-call(f32[64,64]{1,0:T(8,128)S(1)} %get-tuple-element.75.refs_0_, f32[64,64]{1,0:T(8,128)S(1)} %collective-permute-done.55.refs_1_, f32[64,64]{1,0:T(8,128)S(1)} %collective-permute-done.56.refs_2_, f32[64,64]{1,0:T(8,128)S(1)} %collective-permute-done.57.refs_3_, ...), custom_call_target="tpu_custom_call" | custom-call | flops 16777216 | bytes 1048576 | tf_op jit(solution)/shard_map/pallas_call | solution.py:51
  (113 shorter events, 48.7 us)
Async XLA Ops:
  3.7 18.5 %collective-permute-start.9 = (bf16[64,512]{1,0:T(8,128)(2,1)S(1)}, bf16[64,512]{1,0:T(8,128)(2,1)S(1)}, u32[]{:S(2)}, u32[]{:S(2)}) collective-permute-start(bf16[64,512]{1,0:T(8,128)(2,1)S(1)} %collective-permute-done.3.refs_6_), channel_id=1, source_target_pairs={{0,6},{1,7},{2,0},{3,1},{4,2},{5,3},{6,4},{7,5},{8,14},{9,15},{10,... | collective-permute-start | bytes 196616 | tf_op jit(solution)/shard_map/ppermute | solution.py:464
  17.2 10.6 %collective-permute-start.2 = (bf16[128,512]{1,0:T(8,128)(2,1)S(1)}, bf16[128,512]{1,0:T(8,128)(2,1)S(1)}, u32[]{:S(2)}, u32[]{:S(2)}) collective-permute-start(bf16[128,512]{1,0:T(8,128)(2,1)S(1)} %get-tuple-element.43.refs_2_.refs_10_), channel_id=1, source_target_pairs={{0,24},{8,0},{16,8},{24,16},{1,25},{9,1},{17,9},{25,17},{2,26},{10... | collective-permute-start | bytes 393224 | tf_op jit(solution)/shard_map/ppermute | solution.py:397
  21.6 8.0 %collective-permute-start.1 = (bf16[128,512]{1,0:T(8,128)(2,1)S(1)}, bf16[128,512]{1,0:T(8,128)(2,1)S(1)}, u32[]{:S(2)}, u32[]{:S(2)}) collective-permute-start(bf16[128,512]{1,0:T(8,128)(2,1)S(1)} %get-tuple-element.43.refs_2_.refs_10_), channel_id=1, source_target_pairs={{0,16},{8,24},{16,0},{24,8},{1,17},{9,25},{17,1},{25,9},{2,18},{10... | collective-permute-start | bytes 393224 | tf_op jit(solution)/shard_map/ppermute | solution.py:397
  21.6 8.0 %collective-permute-start = (bf16[128,512]{1,0:T(8,128)(2,1)S(1)}, bf16[128,512]{1,0:T(8,128)(2,1)S(1)}, u32[]{:S(2)}, u32[]{:S(2)}) collective-permute-start(bf16[128,512]{1,0:T(8,128)(2,1)S(1)} %get-tuple-element.43.refs_2_.refs_10_), channel_id=1, source_target_pairs={{0,8},{8,16},{16,24},{24,0},{1,9},{9,17},{17,25},{25,1},{2,10},{10... | collective-permute-start | bytes 393224 | tf_op jit(solution)/shard_map/ppermute | solution.py:397
  37.6 11.8 %collective-permute-start.15 = (f32[16,128]{1,0:T(8,128)S(1)}, f32[16,128]{1,0:T(8,128)S(1)}, u32[]{:S(2)}, u32[]{:S(2)}) collective-permute-start(f32[16,128]{1,0:T(8,128)S(1)} %get-tuple-element.47.refs_3_), channel_id=1, source_target_pairs={{0,24},{24,0},{1,25},{25,1},{10,2},{2,10},{11,3},{3,11},{20,12},{1... | collective-permute-start | bytes 24584 | tf_op jit(solution)/shard_map/ppermute | solution.py:454
  45.5 6.4 %collective-permute-start.14 = (f32[16,128]{1,0:T(8,128)S(1)}, f32[16,128]{1,0:T(8,128)S(1)}, u32[]{:S(2)}, u32[]{:S(2)}) collective-permute-start(f32[16,128]{1,0:T(8,128)S(1)} %get-tuple-element.47.refs_3_), channel_id=1, source_target_pairs={{0,16},{16,0},{1,17},{17,1},{10,26},{26,10},{11,27},{27,11},{20,4}... | collective-permute-start | bytes 24584 | tf_op jit(solution)/shard_map/ppermute | solution.py:454
  47.5 5.5 %collective-permute-start.13 = (f32[16,128]{1,0:T(8,128)S(1)}, f32[16,128]{1,0:T(8,128)S(1)}, u32[]{:S(2)}, u32[]{:S(2)}) collective-permute-start(f32[16,128]{1,0:T(8,128)S(1)} %get-tuple-element.47.refs_3_), channel_id=1, source_target_pairs={{0,8},{8,0},{1,9},{9,1},{10,18},{18,10},{11,19},{19,11},{20,28},{2... | collective-permute-start | bytes 24584 | tf_op jit(solution)/shard_map/ppermute | solution.py:454
  58.9 20.3 %collective-permute-start.27 = (f32[32,128]{1,0:T(8,128)S(1)}, f32[32,128]{1,0:T(8,128)S(1)}, u32[]{:S(2)}, u32[]{:S(2)}) collective-permute-start(f32[32,128]{1,0:T(8,128)S(1)} %shard_map.87.refs_3_), channel_id=1, source_target_pairs={{0,7},{1,4},{7,0},{4,1},{10,9},{11,14},{9,10},{14,11},{20,19},{21,... | collective-permute-start | bytes 49160 | tf_op jit(solution)/shard_map/ppermute | solution.py:454
  70.2 11.1 %collective-permute-start.26 = (f32[32,128]{1,0:T(8,128)S(1)}, f32[32,128]{1,0:T(8,128)S(1)}, u32[]{:S(2)}, u32[]{:S(2)}) collective-permute-start(f32[32,128]{1,0:T(8,128)S(1)} %shard_map.87.refs_3_), channel_id=1, source_target_pairs={{0,6},{1,3},{6,0},{3,1},{10,8},{11,13},{8,10},{13,11},{20,18},{21,... | collective-permute-start | bytes 49160 | tf_op jit(solution)/shard_map/ppermute | solution.py:454
  72.2 12.1 %collective-permute-start.25 = (f32[32,128]{1,0:T(8,128)S(1)}, f32[32,128]{1,0:T(8,128)S(1)}, u32[]{:S(2)}, u32[]{:S(2)}) collective-permute-start(f32[32,128]{1,0:T(8,128)S(1)} %shard_map.87.refs_3_), channel_id=1, source_target_pairs={{0,5},{1,2},{5,0},{2,1},{10,15},{11,12},{15,10},{12,11},{20,17},{2... | collective-permute-start | bytes 49160 | tf_op jit(solution)/shard_map/ppermute | solution.py:454
  74.1 10.1 %collective-permute-start.24 = (f32[32,128]{1,0:T(8,128)S(1)}, f32[32,128]{1,0:T(8,128)S(1)}, u32[]{:S(2)}, u32[]{:S(2)}) collective-permute-start(f32[32,128]{1,0:T(8,128)S(1)} %shard_map.87.refs_3_), channel_id=1, source_target_pairs={{0,4},{1,7},{4,0},{7,1},{10,14},{11,9},{14,10},{9,11},{20,16},{21,... | collective-permute-start | bytes 49160 | tf_op jit(solution)/shard_map/ppermute | solution.py:454
  76.0 8.2 %collective-permute-start.23 = (f32[32,128]{1,0:T(8,128)S(1)}, f32[32,128]{1,0:T(8,128)S(1)}, u32[]{:S(2)}, u32[]{:S(2)}) collective-permute-start(f32[32,128]{1,0:T(8,128)S(1)} %shard_map.87.refs_3_), channel_id=1, source_target_pairs={{0,3},{1,6},{3,0},{6,1},{10,13},{11,8},{13,10},{8,11},{20,23},{21,... | collective-permute-start | bytes 49160 | tf_op jit(solution)/shard_map/ppermute | solution.py:454
  79.2 5.6 %collective-permute-start.22 = (f32[32,128]{1,0:T(8,128)S(1)}, f32[32,128]{1,0:T(8,128)S(1)}, u32[]{:S(2)}, u32[]{:S(2)}) collective-permute-start(f32[32,128]{1,0:T(8,128)S(1)} %shard_map.87.refs_3_), channel_id=1, source_target_pairs={{0,2},{1,5},{2,0},{5,1},{10,12},{11,15},{12,10},{15,11},{20,22},{2... | collective-permute-start | bytes 49160 | tf_op jit(solution)/shard_map/ppermute | solution.py:454
  89.5 12.2 %collective-permute-start.32 = (f32[16,128]{1,0:T(8,128)S(1)}, f32[16,128]{1,0:T(8,128)S(1)}, u32[]{:S(2)}, u32[]{:S(2)}) collective-permute-start(f32[16,128]{1,0:T(8,128)S(1)} %shard_map.88.refs_3_), channel_id=1, source_target_pairs={{0,24},{24,0},{1,25},{25,1},{10,2},{2,10},{11,3},{3,11},{20,12},{1... | collective-permute-start | bytes 24584 | tf_op jit(solution)/shard_map/ppermute | solution.py:454
  97.8 6.4 %collective-permute-start.31 = (f32[16,128]{1,0:T(8,128)S(1)}, f32[16,128]{1,0:T(8,128)S(1)}, u32[]{:S(2)}, u32[]{:S(2)}) collective-permute-start(f32[16,128]{1,0:T(8,128)S(1)} %shard_map.88.refs_3_), channel_id=1, source_target_pairs={{0,16},{16,0},{1,17},{17,1},{10,26},{26,10},{11,27},{27,11},{20,4}... | collective-permute-start | bytes 24584 | tf_op jit(solution)/shard_map/ppermute | solution.py:454
  99.7 5.5 %collective-permute-start.30 = (f32[16,128]{1,0:T(8,128)S(1)}, f32[16,128]{1,0:T(8,128)S(1)}, u32[]{:S(2)}, u32[]{:S(2)}) collective-permute-start(f32[16,128]{1,0:T(8,128)S(1)} %shard_map.88.refs_3_), channel_id=1, source_target_pairs={{0,8},{8,0},{1,9},{9,1},{10,18},{18,10},{11,19},{19,11},{20,28},{2... | collective-permute-start | bytes 24584 | tf_op jit(solution)/shard_map/ppermute | solution.py:454
  111.2 20.0 %collective-permute-start.44 = (f32[32,128]{1,0:T(8,128)S(1)}, f32[32,128]{1,0:T(8,128)S(1)}, u32[]{:S(2)}, u32[]{:S(2)}) collective-permute-start(f32[32,128]{1,0:T(8,128)S(1)} %shard_map.89.refs_3_), channel_id=1, source_target_pairs={{0,7},{1,4},{7,0},{4,1},{10,9},{11,14},{9,10},{14,11},{20,19},{21,... | collective-permute-start | bytes 49160 | tf_op jit(solution)/shard_map/ppermute | solution.py:454
  122.3 11.1 %collective-permute-start.43 = (f32[32,128]{1,0:T(8,128)S(1)}, f32[32,128]{1,0:T(8,128)S(1)}, u32[]{:S(2)}, u32[]{:S(2)}) collective-permute-start(f32[32,128]{1,0:T(8,128)S(1)} %shard_map.89.refs_3_), channel_id=1, source_target_pairs={{0,6},{1,3},{6,0},{3,1},{10,8},{11,13},{8,10},{13,11},{20,18},{21,... | collective-permute-start | bytes 49160 | tf_op jit(solution)/shard_map/ppermute | solution.py:454
  124.2 12.1 %collective-permute-start.42 = (f32[32,128]{1,0:T(8,128)S(1)}, f32[32,128]{1,0:T(8,128)S(1)}, u32[]{:S(2)}, u32[]{:S(2)}) collective-permute-start(f32[32,128]{1,0:T(8,128)S(1)} %shard_map.89.refs_3_), channel_id=1, source_target_pairs={{0,5},{1,2},{5,0},{2,1},{10,15},{11,12},{15,10},{12,11},{20,17},{2... | collective-permute-start | bytes 49160 | tf_op jit(solution)/shard_map/ppermute | solution.py:454
  126.1 10.1 %collective-permute-start.41 = (f32[32,128]{1,0:T(8,128)S(1)}, f32[32,128]{1,0:T(8,128)S(1)}, u32[]{:S(2)}, u32[]{:S(2)}) collective-permute-start(f32[32,128]{1,0:T(8,128)S(1)} %shard_map.89.refs_3_), channel_id=1, source_target_pairs={{0,4},{1,7},{4,0},{7,1},{10,14},{11,9},{14,10},{9,11},{20,16},{21,... | collective-permute-start | bytes 49160 | tf_op jit(solution)/shard_map/ppermute | solution.py:454
  128.1 8.2 %collective-permute-start.40 = (f32[32,128]{1,0:T(8,128)S(1)}, f32[32,128]{1,0:T(8,128)S(1)}, u32[]{:S(2)}, u32[]{:S(2)}) collective-permute-start(f32[32,128]{1,0:T(8,128)S(1)} %shard_map.89.refs_3_), channel_id=1, source_target_pairs={{0,3},{1,6},{3,0},{6,1},{10,13},{11,8},{13,10},{8,11},{20,23},{21,... | collective-permute-start | bytes 49160 | tf_op jit(solution)/shard_map/ppermute | solution.py:454
  131.2 5.6 %collective-permute-start.39 = (f32[32,128]{1,0:T(8,128)S(1)}, f32[32,128]{1,0:T(8,128)S(1)}, u32[]{:S(2)}, u32[]{:S(2)}) collective-permute-start(f32[32,128]{1,0:T(8,128)S(1)} %shard_map.89.refs_3_), channel_id=1, source_target_pairs={{0,2},{1,5},{2,0},{5,1},{10,12},{11,15},{12,10},{15,11},{20,22},{2... | collective-permute-start | bytes 49160 | tf_op jit(solution)/shard_map/ppermute | solution.py:454
  141.5 12.0 %collective-permute-start.49 = (f32[16,128]{1,0:T(8,128)S(1)}, f32[16,128]{1,0:T(8,128)S(1)}, u32[]{:S(2)}, u32[]{:S(2)}) collective-permute-start(f32[16,128]{1,0:T(8,128)S(1)} %shard_map.90.refs_4_), channel_id=1, source_target_pairs={{0,24},{24,0},{1,25},{25,1},{10,2},{2,10},{11,3},{3,11},{20,12},{1... | collective-permute-start | bytes 24584 | tf_op jit(solution)/shard_map/ppermute | solution.py:454
  149.6 6.4 %collective-permute-start.48 = (f32[16,128]{1,0:T(8,128)S(1)}, f32[16,128]{1,0:T(8,128)S(1)}, u32[]{:S(2)}, u32[]{:S(2)}) collective-permute-start(f32[16,128]{1,0:T(8,128)S(1)} %shard_map.90.refs_4_), channel_id=1, source_target_pairs={{0,16},{16,0},{1,17},{17,1},{10,26},{26,10},{11,27},{27,11},{20,4}... | collective-permute-start | bytes 24584 | tf_op jit(solution)/shard_map/ppermute | solution.py:454
  164.2 7.0 %collective-permute-start.53 = (bf16[224,128]{1,0:T(8,128)(2,1)S(1)}, bf16[224,128]{1,0:T(8,128)(2,1)S(1)}, u32[]{:S(2)}, u32[]{:S(2)}) collective-permute-start(bf16[224,128]{1,0:T(8,128)(2,1)S(1)} %get-tuple-element.71.refs_1_), channel_id=1, source_target_pairs={{0,4},{1,5},{2,6},{3,7},{4,0},{5,1},{6,2},{7,3},{8,12},{9,13},{10,... | collective-permute-start | bytes 172040 | tf_op jit(solution)/shard_map/ppermute | solution.py:464
  164.3 6.9 %collective-permute-start.52 = (bf16[224,128]{1,0:T(8,128)(2,1)S(1)}, bf16[224,128]{1,0:T(8,128)(2,1)S(1)}, u32[]{:S(2)}, u32[]{:S(2)}) collective-permute-start(bf16[224,128]{1,0:T(8,128)(2,1)S(1)} %get-tuple-element.71.refs_1_), channel_id=1, source_target_pairs={{0,2},{1,3},{2,4},{3,5},{4,6},{5,7},{6,0},{7,1},{8,10},{9,11},{10,... | collective-permute-start | bytes 172040 | tf_op jit(solution)/shard_map/ppermute | solution.py:464
  166.2 22.4 %collective-permute-start.60 = (bf16[256,128]{1,0:T(8,128)(2,1)S(1)}, bf16[256,128]{1,0:T(8,128)(2,1)S(1)}, u32[]{:S(2)}, u32[]{:S(2)}) collective-permute-start(bf16[256,128]{1,0:T(8,128)(2,1)S(1)} %get-tuple-element.79), channel_id=1, source_target_pairs={{0,2},{1,3},{2,4},{3,5},{4,6},{5,7},{6,0},{7,1},{8,10},{9,11},{10,... | collective-permute-start | bytes 196616 | tf_op jit(solution)/shard_map/ppermute | solution.py:464
  167.7 22.8 %collective-permute-start.61 = (bf16[256,128]{1,0:T(8,128)(2,1)S(1)}, bf16[256,128]{1,0:T(8,128)(2,1)S(1)}, u32[]{:S(2)}, u32[]{:S(2)}) collective-permute-start(bf16[256,128]{1,0:T(8,128)(2,1)S(1)} %get-tuple-element.80), channel_id=1, source_target_pairs={{0,4},{1,5},{2,6},{3,7},{4,0},{5,1},{6,2},{7,3},{8,12},{9,13},{10,... | collective-permute-start | bytes 196616 | tf_op jit(solution)/shard_map/ppermute | solution.py:464
  168.6 22.0 %collective-permute-start.62 = (bf16[256,128]{1,0:T(8,128)(2,1)S(1)}, bf16[256,128]{1,0:T(8,128)(2,1)S(1)}, u32[]{:S(2)}, u32[]{:S(2)}) collective-permute-start(bf16[256,128]{1,0:T(8,128)(2,1)S(1)} %get-tuple-element.81), channel_id=1, source_target_pairs={{0,6},{1,7},{2,0},{3,1},{4,2},{5,3},{6,4},{7,5},{8,14},{9,15},{10,... | collective-permute-start | bytes 196616 | tf_op jit(solution)/shard_map/ppermute | solution.py:464
  173.8 16.8 %collective-permute-start.59 = (f32[64,64]{1,0:T(8,128)S(1)}, f32[64,64]{1,0:T(8,128)S(1)}, u32[]{:S(2)}, u32[]{:S(2)}) collective-permute-start(f32[64,64]{1,0:T(8,128)S(1)} %get-tuple-element.75.refs_0_), channel_id=1, source_target_pairs={{0,24},{24,0},{1,25},{25,1},{10,2},{2,10},{11,3},{3,11},{20,12},{1... | collective-permute-start | bytes 49160 | tf_op jit(solution)/shard_map/ppermute | solution.py:454
  186.7 6.7 %collective-permute-start.58 = (f32[64,64]{1,0:T(8,128)S(1)}, f32[64,64]{1,0:T(8,128)S(1)}, u32[]{:S(2)}, u32[]{:S(2)}) collective-permute-start(f32[64,64]{1,0:T(8,128)S(1)} %get-tuple-element.75.refs_0_), channel_id=1, source_target_pairs={{0,16},{16,0},{1,17},{17,1},{10,26},{26,10},{11,27},{27,11},{20,4}... | collective-permute-start | bytes 49160 | tf_op jit(solution)/shard_map/ppermute | solution.py:454
  188.6 5.8 %collective-permute-start.57 = (f32[64,64]{1,0:T(8,128)S(1)}, f32[64,64]{1,0:T(8,128)S(1)}, u32[]{:S(2)}, u32[]{:S(2)}) collective-permute-start(f32[64,64]{1,0:T(8,128)S(1)} %get-tuple-element.75.refs_0_), channel_id=1, source_target_pairs={{0,8},{8,0},{1,9},{9,1},{10,18},{18,10},{11,19},{19,11},{20,28},{2... | collective-permute-start | bytes 49160 | tf_op jit(solution)/shard_map/ppermute | solution.py:454
  (35 other events, 142.8 us)
